TPU v7x, 32 devices: a whole 2x2x4 slice. The times are simulated.
32 devices in a mesh: freq: 4 (over y, x), shot: 8 (over z, core).
Axes of the slice: x: 2, y: 2, z: 4, core: 2. Of those that a mesh axis runs over, the one named last changes fastest.
Arguments:
- up_traces: bfloat16 [512, 128, 1024], P(('freq', 'shot')), may hold values from -6 to 6
- down_traces: bfloat16 [512, 128, 1024], P(('freq', 'shot')), may hold values from -6 to 6
Outputs:
- reflectivity: float32 [4, 1024, 2, 1024], P('freq', 'shot')
All inputs are finite; a program needn't handle non-finite values.
Results may differ from a plain program's by a relative error of at most 0.0054.
Values may be sent and summed in bfloat16 or wider, within the bound.
No kernel may reach another device: no remote copies, remote signals or barrier semaphores. Data moves between devices by JAX's collectives and lax.ppermute only.
A program may use at most 128 MiB of HBM per device.

v0:
```python
import math

import jax
import jax.numpy as jnp
from jax import lax
from jax.sharding import PartitionSpec as P

ITERS = 2


def make_table(samples, nfreq, first):
    times = jnp.arange(samples, dtype=jnp.int32)
    bins = first + jnp.arange(nfreq, dtype=jnp.int32)
    phase = times[:, None] * bins[None, :] % samples
    angle = 2.0 * math.pi * phase.astype(jnp.float32) / samples
    return jnp.stack([jnp.cos(angle), -jnp.sin(angle)], -1).astype(jnp.bfloat16)


def contract(left, right):
    return jnp.einsum("kr,kc->rc", left, right, preferred_element_type=jnp.float32)


def column_apply(direc, gram, damping):
    real_part = jnp.einsum(
        "vs,rs->vr", direc[:, 0], gram[:, 0], precision=lax.Precision.HIGHEST
    ) - jnp.einsum("vs,rs->vr", direc[:, 1], gram[:, 1], precision=lax.Precision.HIGHEST)
    imag_part = jnp.einsum(
        "vs,rs->vr", direc[:, 0], gram[:, 1], precision=lax.Precision.HIGHEST
    ) + jnp.einsum("vs,rs->vr", direc[:, 1], gram[:, 0], precision=lax.Precision.HIGHEST)
    return jnp.stack([real_part, imag_part], 1) + damping * direc


def shards(up_traces, down_traces):
    samples = up_traces.shape[1]
    width = up_traces.shape[2]
    nfreq = lax.axis_size("freq")
    table = make_table(samples, nfreq, samples // 16)
    up_spec = jnp.einsum(
        "str,tfc->sfcr", up_traces, table, preferred_element_type=jnp.float32
    ).astype(jnp.bfloat16)
    down_spec = jnp.einsum(
        "str,tfc->sfcr", down_traces, table, preferred_element_type=jnp.float32
    ).astype(jnp.bfloat16)
    up_local, down_local = (
        lax.all_to_all(up_spec, "freq", split_axis=1, concat_axis=0, tiled=True),
        lax.all_to_all(down_spec, "freq", split_axis=1, concat_axis=0, tiled=True),
    )
    up_re, up_im = (up_local[:, 0, 0, :], up_local[:, 0, 1, :])
    down_re, down_im = (down_local[:, 0, 0, :], down_local[:, 0, 1, :])
    down_even = jnp.concatenate([down_re, down_im], 0)
    down_odd = jnp.concatenate([down_im, -down_re], 0)
    up_stack = jnp.concatenate([up_re, up_im], 0)
    gram_local = jnp.stack([contract(down_even, down_even), contract(down_odd, down_even)], 1)
    gram = lax.psum(gram_local, "shot")
    resid = lax.psum_scatter(
        jnp.stack([contract(up_stack, down_even), contract(up_stack, down_odd)], 1),
        "shot",
        scatter_dimension=0,
        tiled=True,
    )
    damping = 0.1 * jnp.trace(gram[:, 0]) / width
    norm_now = jnp.sum(resid * resid, axis=(1, 2))
    solution = jnp.zeros_like(resid)
    direc = resid
    for step in range(ITERS):
        image = column_apply(direc, gram, damping)
        curv = jnp.sum(direc * image, axis=(1, 2))
        alpha = (norm_now / curv)[:, None, None]
        solution = solution + alpha * direc
        resid = resid - alpha * image
        if step + 1 < ITERS:
            norm_next = jnp.sum(resid * resid, axis=(1, 2))
            direc = resid + (norm_next / norm_now)[:, None, None] * direc
            norm_now = norm_next
    moved = lax.all_to_all(solution, "shot", split_axis=2, concat_axis=0, tiled=True)
    solution = jnp.transpose(moved, (2, 1, 0))
    return solution[None]


def solution(mesh):
    in_specs = (P(("freq", "shot"), None, None), P(("freq", "shot"), None, None))
    out_specs = P("freq", "shot", None, None)
    return jax.shard_map(shards, mesh=mesh, in_specs=in_specs, out_specs=out_specs, check_vma=False)
```

profile of v0, /device:TPU:0, one launch (start us, length us, event | category | flops | bytes accessed | tf_op | source)
XLA Modules:
  0.0 384.1 jit_solution(17246109653387385972)
XLA Ops:
  6.5 0.1 cosine_convert_fusion
  6.7 2.8 fusion.26
  9.5 0.8 copy.11
  10.3 5.2 %all-to-all-start.1 = ((bf16[16,4,2,1024]{3,0,2,1:T(8,128)(2,1)}), bf16[16,4,2,1024]{3,0,2,1:T(8,128)(2,1)S(1)}, u32[]{:S(2)}, u32[]{:S(2)}) async-start(bf16[16,4,2,1024]{3,0,2,1:T(8,128)(2,1)} %copy.11), calls=%async_computation.1 | async-start | bytes 524288 | tf_op jit(solution)/shard_map/all_to_all | solution.py:46
  15.5 2.8 fusion.29
  18.3 0.8 copy.9
  19.1 1.8 all-to-all-done.1
  20.8 3.4 all-to-all-start
  24.2 0.0 all-reduce.2.cloned.1.call-start
  24.3 5.2 %all-to-all-done = bf16[16,4,2,1024]{3,0,2,1:T(8,128)(2,1)S(1)} async-done(((bf16[16,4,2,1024]{3,0,2,1:T(8,128)(2,1)}), bf16[16,4,2,1024]{3,0,2,1:T(8,128)(2,1)S(1)}, u32[]{:S(2)}, u32[]{:S(2)}) %all-to-all-start) | async-done | bytes 262176 | tf_op jit(solution)/shard_map/all_to_all | solution.py:45
  29.7 0.7 convolution_bitcast_fusion.1
  30.4 0.7 convolution_bitcast_fusion
  31.1 4.1 %pad_maximum_fusion.1 = f32[1024,2,1024]{2,0,1:T(8,128)} fusion(f32[1024,1,1024]{2,0,1:T(8,128)S(1)} %convolution_bitcast_fusion, f32[1024,1,1024]{2,0,1:T(8,128)S(1)} %convolution_bitcast_fusion.1), kind=kLoop, calls=%fused_computation.1 | loop fusion | flops 2097152 | bytes 16777216 | tf_op jit(solution)/shard_map/stack | solution.py:53
  35.2 0.0 all-reduce.2.cloned.1.call-update
  35.2 0.2 reduce-scatter.2.cloned.1.call-start
  35.4 0.7 convolution_bitcast_fusion.2
  36.1 0.7 convolution_bitcast_fusion.3
  36.9 4.3 %pad_maximum_fusion = f32[1024,2,1024]{2,0,1:T(8,128)} fusion(f32[1024,1,1024]{2,0,1:T(8,128)S(1)} %convolution_bitcast_fusion.2, f32[1024,1,1024]{2,0,1:T(8,128)S(1)} %convolution_bitcast_fusion.3), kind=kLoop, calls=%fused_computation | loop fusion | flops 2097152 | bytes 16777216 | tf_op jit(solution)/shard_map/stack | solution.py:56
  41.2 0.0 reduce-scatter.2.cloned.1.call-update
  41.2 169.7 %all-reduce.2.cloned.1.call-done = f32[1024,2,1024]{2,0,1:T(8,128)} async-done(((f32[1024,2,1024]{2,0,1:T(8,128)}), f32[1024,2,1024]{2,0,1:T(8,128)}) %all-reduce.2.cloned.1.call-update) | async-done | bytes 8388624 | tf_op jit(solution)/shard_map/psum | solution.py:54
  211.0 2.9 select_reduce_fusion
  214.6 88.5 %reduce-scatter.2.cloned.1.call-done = f32[128,2,1024]{2,0,1:T(8,128)} async-done(((f32[1024,2,1024]{2,0,1:T(8,128)}), f32[128,2,1024]{2,0,1:T(8,128)}) %reduce-scatter.2.cloned.1.call-update) | async-done | bytes 1048592 | tf_op jit(solution)/shard_map/reduce_scatter | solution.py:55
  303.0 0.0 copy-start
  303.0 0.0 copy-start.1
  303.0 6.9 %fusion.6 = f32[128,1024]{1,0:T(8,128)S(1)} fusion(f32[1024,2,1024]{2,0,1:T(8,128)} %all-reduce.2.cloned.1.call-done, f32[128,2,1024]{2,0,1:T(8,128)} %reduce-scatter.2.cloned.1.call-done), kind=kOutput, calls=%fused_computation.12 | convolution fusion | flops 1610612736 | bytes 5242880 | tf_op jit(solution)/shard_map/vs,rs->vr/dot_general | solution.py:27
  309.9 6.7 %fusion.7 = f32[128,1024]{1,0:T(8,128)S(1)} fusion(f32[1024,2,1024]{2,0,1:T(8,128)} %all-reduce.2.cloned.1.call-done, f32[128,2,1024]{2,0,1:T(8,128)} %reduce-scatter.2.cloned.1.call-done), kind=kOutput, calls=%fused_computation.13 | convolution fusion | flops 1610612736 | bytes 5242880 | tf_op jit(solution)/shard_map/vs,rs->vr/dot_general | solution.py:26
  316.7 0.0 copy-done
  316.7 0.0 copy-done.1
  316.7 4.7 %fusion.18 = f32[128,1,1024]{2,0,1:T(8,128)S(1)} fusion(f32[128,1024]{1,0:T(8,128)S(1)} %fusion.6, f32[1024,2,1024]{2,0,1:T(8,128)S(1)} %copy-done, f32[128,2,1024]{2,0,1:T(8,128)S(1)} %copy-done.1), kind=kOutput, calls=%fused_computation.28 | convolution fusion | flops 1610743808 | bytes 5767168 | tf_op jit(solution)/shard_map/vs,rs->vr/dot_general | solution.py:29
  321.4 4.5 %fusion.19 = f32[128,1,1024]{2,0,1:T(8,128)S(1)} fusion(f32[128,1024]{1,0:T(8,128)S(1)} %fusion.7, f32[1024,2,1024]{2,0,1:T(8,128)S(1)} %copy-done, f32[128,2,1024]{2,0,1:T(8,128)S(1)} %copy-done.1), kind=kOutput, calls=%fused_computation.29 | convolution fusion | flops 1610743808 | bytes 5767168 | tf_op jit(solution)/shard_map/vs,rs->vr/dot_general | solution.py:24
  325.8 0.3 multiply_reduce_fusion.1
  326.1 0.3 multiply_reduce_fusion
  326.5 0.4 multiply_add_fusion.1
  326.9 4.5 %fusion.4 = f32[128,1024]{1,0:T(8,128)S(1)} fusion(f32[1024,2,1024]{2,0,1:T(8,128)S(1)} %copy-done, f32[128,2,1024]{2,0,1:T(8,128)S(1)} %multiply_add_fusion.1), kind=kOutput, calls=%fused_computation.10 | convolution fusion | flops 1610612736 | bytes 5242880 | tf_op jit(solution)/shard_map/vs,rs->vr/dot_general | solution.py:27
  331.3 4.5 %fusion.5 = f32[128,1024]{1,0:T(8,128)S(1)} fusion(f32[1024,2,1024]{2,0,1:T(8,128)S(1)} %copy-done, f32[128,2,1024]{2,0,1:T(8,128)S(1)} %multiply_add_fusion.1), kind=kOutput, calls=%fused_computation.11 | convolution fusion | flops 1610612736 | bytes 5242880 | tf_op jit(solution)/shard_map/vs,rs->vr/dot_general | solution.py:26
  335.8 4.7 %fusion.16 = f32[128,1,1024]{2,0,1:T(8,128)S(1)} fusion(f32[128,1024]{1,0:T(8,128)S(1)} %fusion.4, f32[1024,2,1024]{2,0,1:T(8,128)S(1)} %copy-done, f32[128,2,1024]{2,0,1:T(8,128)S(1)} %multiply_add_fusion.1), kind=kOutput, calls=%fused_computation.26 | convolution fusion | flops 1610743808 | bytes 5767168 | tf_op jit(solution)/shard_map/vs,rs->vr/dot_general | solution.py:29
  340.5 4.5 %fusion.17 = f32[128,1,1024]{2,0,1:T(8,128)S(1)} fusion(f32[128,1024]{1,0:T(8,128)S(1)} %fusion.5, f32[1024,2,1024]{2,0,1:T(8,128)S(1)} %copy-done, f32[128,2,1024]{2,0,1:T(8,128)S(1)} %multiply_add_fusion.1), kind=kOutput, calls=%fused_computation.27 | convolution fusion | flops 1610743808 | bytes 5767168 | tf_op jit(solution)/shard_map/vs,rs->vr/dot_general | solution.py:24
  345.0 0.5 fusion.33
  345.5 0.4 multiply_add_fusion
  345.9 0.6 copy.13
  346.5 29.0 %all_to_all.54 = f32[128,2,1024]{0,1,2:T(2,128)S(1)} all-to-all(f32[128,2,1024]{0,1,2:T(2,128)S(1)} %copy.13), channel_id=1, replica_groups=mesh['freq'=4,'shot'=8] {'shot'}, dimensions={2} | all-to-all | bytes 2097152 | tf_op jit(solution)/shard_map/all_to_all | solution.py:75
  375.5 1.3 copy.18
  (8 shorter events, 0.1 us)
Async XLA Ops:
  10.3 10.5 %all-to-all-start.1 = ((bf16[16,4,2,1024]{3,0,2,1:T(8,128)(2,1)}), bf16[16,4,2,1024]{3,0,2,1:T(8,128)(2,1)S(1)}, u32[]{:S(2)}, u32[]{:S(2)}) async-start(bf16[16,4,2,1024]{3,0,2,1:T(8,128)(2,1)} %copy.11), calls=%async_computation.1 | async-start | bytes 524288 | tf_op jit(solution)/shard_map/all_to_all | solution.py:46
  20.8 8.8 %all-to-all-start = ((bf16[16,4,2,1024]{3,0,2,1:T(8,128)(2,1)}), bf16[16,4,2,1024]{3,0,2,1:T(8,128)(2,1)S(1)}, u32[]{:S(2)}, u32[]{:S(2)}) async-start(bf16[16,4,2,1024]{3,0,2,1:T(8,128)(2,1)} %copy.9), calls=%async_computation | async-start | bytes 524288 | tf_op jit(solution)/shard_map/all_to_all | solution.py:45
  24.2 186.7 %all-reduce.2.cloned.1.call-start = ((), (), s32[]{:S(2)}) async-start(), calls=%async_computation.5 | async-start | bytes 16777216 | tf_op jit(solution)/shard_map/psum | solution.py:54
  35.2 267.8 %reduce-scatter.2.cloned.1.call-start = ((), (), s32[]{:S(2)}) async-start(), calls=%async_computation.4 | async-start | bytes 9437184 | tf_op jit(solution)/shard_map/reduce_scatter | solution.py:55
  303.0 13.6 %copy-start = (f32[1024,2,1024]{2,0,1:T(8,128)S(1)}, f32[1024,2,1024]{2,0,1:T(8,128)}, u32[]{:S(2)}) copy-start(f32[1024,2,1024]{2,0,1:T(8,128)} %all-reduce.2.cloned.1.call-done) | copy-start | bytes 25165828
  303.0 13.7 %copy-start.1 = (f32[128,2,1024]{2,0,1:T(8,128)S(1)}, f32[128,2,1024]{2,0,1:T(8,128)}, u32[]{:S(2)}) copy-start(f32[128,2,1024]{2,0,1:T(8,128)} %reduce-scatter.2.cloned.1.call-done) | copy-start | bytes 3145732
Sparse Core Ops, SparseCore 0:
  35.3 175.6 all-reduce.1
  213.3 89.7 reduce-scatter.1
where the time goes:
time: 388 us; the launch traced here: 384 us
  waiting for transfers between devices  265 us (68%)
  matrix products  49.4 us (13%)
  blocking collectives  29 us (7%)
  between operations  14.7 us (4%)
  other arithmetic  13.4 us (3%)
  starting transfers between devices  8.82 us (2%)
    psum x1, waiting for transfers between devices, shards(): gram = lax.psum(gram_local, 'shot')  170 us
    reduce_scatter x1, waiting for transfers between devices, shards(): lax.psum_scatter(jnp.stack([contract(up_stack, down_even), contract(up_st...  88.5 us
    all_to_all x1, blocking collectives, shards(): lax.all_to_all(solution, 'shot', split_axis=2, concat_axis=0, tiled=True)  29 us
    dot_general x2, matrix products, column_apply(): jnp.einsum('vs,rs->vr', direc[:, 0], gram[:, 1], precision=lax.Precision....  11.3 us
    dot_general x2, matrix products, column_apply(): jnp.einsum('vs,rs->vr', direc[:, 1], gram[:, 1], precision=lax.Precision....  11.2 us
    dot_general x2, matrix products, column_apply(): jnp.einsum('vs,rs->vr', direc[:, 1], gram[:, 0], precision=lax.Precision....  9.36 us
    dot_general x2, matrix products, column_apply(): jnp.einsum('vs,rs->vr', direc[:, 0], gram[:, 0], precision=lax.Precision....  8.91 us
  transfers between devices with their start and end apart: 4, of which 4 were waited for; matrix products, arithmetic and copies ran while one was open for 3% of the time, Pallas kernels for 0%

commit v1 on v0

v1 whole, which is shorter than its diff:
```python
import math

import jax
import jax.numpy as jnp
from jax import lax
from jax.sharding import Mesh, PartitionSpec as P


def make_table(samples, nfreq, first):
    times = jnp.arange(samples, dtype=jnp.int32)
    bins = first + jnp.arange(nfreq, dtype=jnp.int32)
    phase = times[:, None] * bins[None, :] % samples
    angle = 2.0 * math.pi * phase.astype(jnp.float32) / samples
    return jnp.stack([jnp.cos(angle), -jnp.sin(angle)], -1).astype(jnp.bfloat16)


def ring_order(chips):
    return [0, 1, 3, 2] if chips == 4 else list(range(chips))


def ring_gather(piece, chips):
    order = ring_order(chips)
    pairs = [(order[i], order[(i + 1) % chips]) for i in range(chips)]
    pieces = [piece]
    for _ in range(chips - 1):
        pieces.append(lax.ppermute(pieces[-1], "chip", pairs))
    return pieces


def swap_core(array):
    return lax.ppermute(array, "core", [(0, 1), (1, 0)])


def split(array):
    high = lax.reduce_precision(array, 8, 7)
    return high.astype(jnp.bfloat16), (array - high).astype(jnp.bfloat16)


def dot(left, right):
    return jnp.dot(left, right, preferred_element_type=jnp.float32)


def dot_t(left, right):
    return lax.dot_general(left, right, (((0,), (0,)), ((), ())), preferred_element_type=jnp.float32)


def spectra(traces, table):
    return jnp.einsum("str,tfc->fcsr", traces, table, preferred_element_type=jnp.float32).astype(jnp.bfloat16)


def to_freq(spec):
    return lax.all_to_all(spec, "freq", split_axis=0, concat_axis=0, tiled=True)


def shards(up_traces, down_traces):
    local_shots, samples, width = up_traces.shape
    nfreq, chips = lax.axis_size("freq"), lax.axis_size("chip")
    core = lax.axis_index("core")
    half = width // 2
    rows = width // (2 * chips)
    table = make_table(samples, nfreq, samples // 16)

    down = to_freq(spectra(down_traces, table))
    own = ring_gather(down, chips)
    down_all = jnp.stack([jnp.stack([piece, swap_core(piece)]) for piece in own])

    up = to_freq(spectra(up_traces, table))
    mine = lax.dynamic_slice_in_dim(up, core * half, half, 3)
    theirs = swap_core(lax.dynamic_slice_in_dim(up, (1 - core) * half, half, 3))
    up_all = jnp.stack(ring_gather(jnp.stack([mine, theirs]), chips))

    even = down_all.reshape(-1, width)
    odd = jnp.stack([-down_all[:, :, :, 1], down_all[:, :, :, 0]], 3).reshape(-1, width)
    start = up_all.reshape(-1, half)

    gram = lax.dot_general(even, even, (((1,), (1,)), ((), ())), preferred_element_type=jnp.float32) + lax.dot_general(
        odd, odd, (((1,), (1,)), ((), ())), preferred_element_type=jnp.float32
    )
    damping = 0.05 * jnp.trace(gram) / width
    gram_high, gram_low = split(gram)

    start_wide = start.astype(jnp.float32)
    image = dot(gram_high, start) + dot(gram_low, start)
    norm_now = jnp.sum(start_wide * image, axis=0)
    alpha = norm_now / (jnp.sum(image * image, axis=0) + damping * norm_now)
    resid = (1.0 - alpha * damping) * start_wide - alpha * image
    resid_image = dot(gram_high, resid.astype(jnp.bfloat16))
    norm_next = jnp.sum(resid * resid_image, axis=0)
    ratio = norm_next / norm_now
    direc = resid + ratio * start_wide
    direc_image = resid_image + ratio * image
    curv = jnp.sum(direc_image * direc_image, axis=0) + damping * jnp.sum(direc * direc_image, axis=0)
    weights = alpha * start_wide + norm_next / curv * direc
    weights_high, weights_low = split(weights)

    chip = lax.axis_index("chip")
    even_rows = lax.dynamic_slice_in_dim(even, chip * 2 * rows, 2 * rows, 1)
    odd_rows = lax.dynamic_slice_in_dim(odd, chip * 2 * rows, 2 * rows, 1)
    real = dot_t(even_rows, weights_high) + dot_t(even_rows, weights_low)
    imag = -(dot_t(odd_rows, weights_high) + dot_t(odd_rows, weights_low))
    block = jnp.stack([real, imag], 1)
    kept = lax.dynamic_slice_in_dim(block, core * rows, rows, 0)
    got = swap_core(lax.dynamic_slice_in_dim(block, (1 - core) * rows, rows, 0))
    first = core == 0
    return jnp.concatenate([jnp.where(first, kept, got), jnp.where(first, got, kept)], 2)[None]


def solution(mesh):
    nfreq, nshot = mesh.devices.shape
    fine = Mesh(mesh.devices.reshape(nfreq, nshot // 2, 2), ("freq", "chip", "core"))
    spec = P(("freq", "chip", "core"), None, None)
    out_specs = P("freq", ("chip", "core"), None, None)
    return jax.shard_map(shards, mesh=fine, in_specs=(spec, spec), out_specs=out_specs, check_vma=False)
```

time: 388 us -> 82.2 us (0.21)
  waiting for transfers between devices: 265 us -> 34.4 us
  matrix products: 49.4 us -> 19.3 us
  blocking collectives: 29 us -> 0 us
  between operations: 14.7 us -> 0.9 us
  other arithmetic: 13.4 us -> 3.2 us
  starting transfers between devices: 8.82 us -> 17.4 us
    psum x1 -> x0, waiting for transfers between devices: 170 us -> none  [shards(): gram = lax.psum(gram_local, 'shot')]
    reduce_scatter x1 -> x0, waiting for transfers between devices: 88.5 us -> none  [shards(): lax.psum_scatter(jnp.stack([contract(up_stack, down_even), contract(up_st...]
    dot_general x14 -> x11, matrix products: 49.4 us -> 19.3 us  [the longest x3 6.42 us: dot(): return jnp.dot(left, right, preferred_element_type=jnp.float32)]
    all_to_all x1 -> x0, blocking collectives: 29 us -> none  [shards(): lax.all_to_all(solution, 'shot', split_axis=2, concat_axis=0, tiled=True)]
    ppermute x0 -> x12, waiting for transfers between devices: none -> 27.5 us  [the longest x6 25.6 us: ring_gather(): pieces.append(lax.ppermute(pieces[-1], 'chip', pairs))]
    ppermute x0 -> x12, starting transfers between devices: none -> 8.82 us  [the longest x6 8.17 us: ring_gather(): pieces.append(lax.ppermute(pieces[-1], 'chip', pairs))]
    another operation x3 -> x10, other arithmetic: 8.51 us -> 1.01 us  [the longest x5 0.47 us: shards(): jnp.stack([jnp.stack([piece, swap_core(piece)]) for piece in own])]
  transfers between devices with their start and end apart: 4 -> 14, of which waited for: 4 -> 9; matrix products, arithmetic and copies ran while one was open for 3% -> 5% of each run, Pallas kernels for 0% -> 0%
where the time goes in v1:
time: 82.2 us; the launch traced here: 81.8 us
  waiting for transfers between devices  34.4 us (42%)
  matrix products  19.3 us (23%)
  starting transfers between devices  17.4 us (21%)
  local copies, waits for them, and re-layouts  6.55 us (8%)
  other arithmetic  3.2 us (4%)
  between operations  0.9 us (1%)
    ppermute x6, waiting for transfers between devices, ring_gather(): pieces.append(lax.ppermute(pieces[-1], 'chip', pairs))  25.6 us
    all_to_all x2, starting transfers between devices, to_freq(): return lax.all_to_all(spec, 'freq', split_axis=0, concat_axis=0, tiled=True)  8.57 us
    ppermute x6, starting transfers between devices, ring_gather(): pieces.append(lax.ppermute(pieces[-1], 'chip', pairs))  8.17 us
    all_to_all x2, waiting for transfers between devices, to_freq(): return lax.all_to_all(spec, 'freq', split_axis=0, concat_axis=0, tiled=True)  6.96 us
    dot_general x3, matrix products, dot(): return jnp.dot(left, right, preferred_element_type=jnp.float32)  6.42 us
    dot_general x2, matrix products, spectra(): jnp.einsum('str,tfc->fcsr', traces, table, preferred_element_type=jnp.flo...  5.69 us
    unnamed x10, local copies, waits for them, and re-layouts  3.16 us
    dot_general x1, matrix products, shards(): lax.dot_general(odd, odd, (((1,), (1,)), ((), ())), preferred_element_typ...  2.97 us
  transfers between devices with their start and end apart: 14, of which 9 were waited for; matrix products, arithmetic and copies ran while one was open for 5% of the time, Pallas kernels for 0%

profile of v1, /device:TPU:0, one launch (start us, length us, event | category | flops | bytes accessed | tf_op | source)
XLA Modules:
  0.0 81.8 jit_solution(376562062414759977)
XLA Ops:
  0.0 0.1 cosine_convert_fusion
  0.1 2.8 %fusion.18 = bf16[4,2,16,1024]{3,0,2,1:T(4,128)(2,1)S(1)} fusion(bf16[16,128,1024]{2,1,0:T(8,128)(2,1)} %param.2, bf16[128,4,1]{0,1,2:T(4,128)(2,1)S(1)} %get-tuple-element.22, bf16[128,4,1]{0,1,2:T(4,128)(2,1)S(1)} %get-tuple-element.21), kind=kOutput, calls=%fused_computation.40 | convolution fusion | flops 33689600 | bytes 4458496 | tf_op jit(solution)/shard_map/str,tfc->fcsr/dot_general | solution.py:48
  3.0 0.8 copy.9
  3.8 5.2 %all-to-all-start.1 = ((bf16[4,2,16,1024]{3,2,1,0:T(8,128)(2,1)}), bf16[4,2,16,1024]{3,2,1,0:T(8,128)(2,1)S(1)}, u32[]{:S(2)}, u32[]{:S(2)}) async-start(bf16[4,2,16,1024]{3,2,1,0:T(8,128)(2,1)} %copy.9), calls=%async_computation.1 | async-start | bytes 524288 | tf_op jit(solution)/shard_map/all_to_all | solution.py:52
  8.9 2.8 %fusion.15 = bf16[4,2,16,1024]{3,0,2,1:T(4,128)(2,1)S(1)} fusion(bf16[16,128,1024]{2,1,0:T(8,128)(2,1)} %param.3, bf16[128,4,1]{0,1,2:T(4,128)(2,1)S(1)} %get-tuple-element.22, bf16[128,4,1]{0,1,2:T(4,128)(2,1)S(1)} %get-tuple-element.21), kind=kOutput, calls=%fused_computation.39 | convolution fusion | flops 33689600 | bytes 4458496 | tf_op jit(solution)/shard_map/str,tfc->fcsr/dot_general | solution.py:48
  11.8 0.8 copy.8
  12.6 1.7 %all-to-all-done.1 = bf16[4,2,16,1024]{3,2,1,0:T(8,128)(2,1)S(1)} async-done(((bf16[4,2,16,1024]{3,2,1,0:T(8,128)(2,1)}), bf16[4,2,16,1024]{3,2,1,0:T(8,128)(2,1)S(1)}, u32[]{:S(2)}, u32[]{:S(2)}) %all-to-all-start.1) | async-done | bytes 262176 | tf_op jit(solution)/shard_map/all_to_all | solution.py:52
  14.3 3.4 %all-to-all-start = ((bf16[4,2,16,1024]{3,2,1,0:T(8,128)(2,1)}), bf16[4,2,16,1024]{3,2,1,0:T(8,128)(2,1)S(1)}, u32[]{:S(2)}, u32[]{:S(2)}) async-start(bf16[4,2,16,1024]{3,2,1,0:T(8,128)(2,1)} %copy.8), calls=%async_computation | async-start | bytes 524288 | tf_op jit(solution)/shard_map/all_to_all | solution.py:52
  17.7 0.1 collective-permute-start.7
  17.8 5.2 %all-to-all-done = bf16[4,2,16,1024]{3,2,1,0:T(8,128)(2,1)S(1)} async-done(((bf16[4,2,16,1024]{3,2,1,0:T(8,128)(2,1)}), bf16[4,2,16,1024]{3,2,1,0:T(8,128)(2,1)S(1)}, u32[]{:S(2)}, u32[]{:S(2)}) %all-to-all-start) | async-done | bytes 262176 | tf_op jit(solution)/shard_map/all_to_all | solution.py:52
  23.1 1.6 %collective-permute-start.1 = (bf16[4,2,16,1024]{3,2,1,0:T(8,128)(2,1)S(1)}, bf16[4,2,16,1024]{3,2,1,0:T(8,128)(2,1)S(1)}, u32[]{:S(2)}, u32[]{:S(2)}) collective-permute-start(bf16[4,2,16,1024]{3,2,1,0:T(8,128)(2,1)S(1)} %all-to-all-done), channel_id=1, source_target_pairs={{0,2},{2,6},{6,4},{4,0},{1,3},{3,7},{7,5},{5,1},{8,10},{10,14},{14... | collective-permute-start | bytes 786440 | tf_op jit(solution)/shard_map/ppermute | solution.py:26
  24.6 0.0 collective-permute-done.7
  24.7 2.6 %collective-permute-start.8 = (bf16[2,4,2,16,512]{4,3,2,1,0:T(8,128)(2,1)S(1)}, bf16[2,4,2,16,512]{4,3,2,1,0:T(8,128)(2,1)S(1)}, u32[]{:S(2)}, u32[]{:S(2)}) collective-permute-start(bf16[2,4,2,16,512]{4,3,2,1,0:T(8,128)(2,1)S(1)} %get-tuple-element.18), channel_id=1, source_target_pairs={{0,2},{2,6},{6,4},{4,0},{1,3},{3,7},{7,5},{5,1},{8,10},{10,14},{14... | collective-permute-start | bytes 786440 | tf_op jit(solution)/shard_map/ppermute | solution.py:26
  27.3 5.9 %collective-permute-done.1 = bf16[4,2,16,1024]{3,2,1,0:T(8,128)(2,1)S(1)} collective-permute-done((bf16[4,2,16,1024]{3,2,1,0:T(8,128)(2,1)S(1)}, bf16[4,2,16,1024]{3,2,1,0:T(8,128)(2,1)S(1)}, u32[]{:S(2)}, u32[]{:S(2)}) %collective-permute-start.1) | collective-permute-done | bytes 262176 | tf_op jit(solution)/shard_map/ppermute | solution.py:26
  33.2 0.8 collective-permute-start.3
  34.0 4.8 %collective-permute-done.8 = bf16[2,4,2,16,512]{4,3,2,1,0:T(8,128)(2,1)S(1)} collective-permute-done((bf16[2,4,2,16,512]{4,3,2,1,0:T(8,128)(2,1)S(1)}, bf16[2,4,2,16,512]{4,3,2,1,0:T(8,128)(2,1)S(1)}, u32[]{:S(2)}, u32[]{:S(2)}) %collective-permute-start.8) | collective-permute-done | bytes 262176 | tf_op jit(solution)/shard_map/ppermute | solution.py:26
  38.8 0.8 collective-permute-start.9
  39.6 0.0 collective-permute-start
  39.6 0.5 collective-permute-start.2
  40.1 3.4 %collective-permute-done.3 = bf16[4,2,16,1024]{3,2,1,0:T(8,128)(2,1)S(1)} collective-permute-done((bf16[4,2,16,1024]{3,2,1,0:T(8,128)(2,1)S(1)}, bf16[4,2,16,1024]{3,2,1,0:T(8,128)(2,1)S(1)}, u32[]{:S(2)}, u32[]{:S(2)}) %collective-permute-start.3) | collective-permute-done | bytes 262176 | tf_op jit(solution)/shard_map/ppermute | solution.py:26
  43.5 1.1 %collective-permute-start.5 = (bf16[4,2,16,1024]{3,2,1,0:T(8,128)(2,1)S(1)}, bf16[4,2,16,1024]{3,2,1,0:T(8,128)(2,1)S(1)}, u32[]{:S(2)}, u32[]{:S(2)}) collective-permute-start(bf16[4,2,16,1024]{3,2,1,0:T(8,128)(2,1)S(1)} %collective-permute-done.3), channel_id=1, source_target_pairs={{0,2},{2,6},{6,4},{4,0},{1,3},{3,7},{7,5},{5,1},{8,10},{10,14},{14... | collective-permute-start | bytes 786440 | tf_op jit(solution)/shard_map/ppermute | solution.py:26
  44.6 0.0 collective-permute-start.4
  44.6 4.3 %collective-permute-done.9 = bf16[2,4,2,16,512]{4,3,2,1,0:T(8,128)(2,1)S(1)} collective-permute-done((bf16[2,4,2,16,512]{4,3,2,1,0:T(8,128)(2,1)S(1)}, bf16[2,4,2,16,512]{4,3,2,1,0:T(8,128)(2,1)S(1)}, u32[]{:S(2)}, u32[]{:S(2)}) %collective-permute-start.9) | collective-permute-done | bytes 262176 | tf_op jit(solution)/shard_map/ppermute | solution.py:26
  48.9 1.3 %collective-permute-start.10 = (bf16[2,4,2,16,512]{4,3,2,1,0:T(8,128)(2,1)S(1)}, bf16[2,4,2,16,512]{4,3,2,1,0:T(8,128)(2,1)S(1)}, u32[]{:S(2)}, u32[]{:S(2)}) collective-permute-start(bf16[2,4,2,16,512]{4,3,2,1,0:T(8,128)(2,1)S(1)} %collective-permute-done.9), channel_id=1, source_target_pairs={{0,2},{2,6},{6,4},{4,0},{1,3},{3,7},{7,5},{5,1},{8,10},{10,14},{14... | collective-permute-start | bytes 786440 | tf_op jit(solution)/shard_map/ppermute | solution.py:26
  50.2 0.0 collective-permute-done
  50.2 0.1 maximum_bitcast_fusion.1
  50.2 0.0 collective-permute-done.2
  50.3 0.1 maximum_bitcast_fusion.2
  50.3 4.2 %collective-permute-done.5 = bf16[4,2,16,1024]{3,2,1,0:T(8,128)(2,1)S(1)} collective-permute-done((bf16[4,2,16,1024]{3,2,1,0:T(8,128)(2,1)S(1)}, bf16[4,2,16,1024]{3,2,1,0:T(8,128)(2,1)S(1)}, u32[]{:S(2)}, u32[]{:S(2)}) %collective-permute-start.5) | collective-permute-done | bytes 262176 | tf_op jit(solution)/shard_map/ppermute | solution.py:26
  54.5 0.0 collective-permute-start.6
  54.5 0.0 collective-permute-done.4
  54.5 0.1 maximum_bitcast_fusion.3
  54.6 3.0 %collective-permute-done.10 = bf16[2,4,2,16,512]{4,3,2,1,0:T(8,128)(2,1)S(1)} collective-permute-done((bf16[2,4,2,16,512]{4,3,2,1,0:T(8,128)(2,1)S(1)}, bf16[2,4,2,16,512]{4,3,2,1,0:T(8,128)(2,1)S(1)}, u32[]{:S(2)}, u32[]{:S(2)}) %collective-permute-start.10) | collective-permute-done | bytes 262176 | tf_op jit(solution)/shard_map/ppermute | solution.py:26
  57.5 0.1 pad_maximum_fusion.2
  57.7 0.0 collective-permute-done.6
  57.7 0.1 maximum_bitcast_fusion.4
  57.7 0.3 pad_maximum_fusion
  58.0 0.0 copy-start.1
  58.0 0.1 slice_negate_fusion
  58.2 1.2 %copy-done.1 = bf16[4,2,4,2,16,1024]{5,4,3,2,1,0:T(8,128)(2,1)} copy-done((bf16[4,2,4,2,16,1024]{5,4,3,2,1,0:T(8,128)(2,1)}, bf16[4,2,4,2,16,1024]{5,4,3,2,1,0:T(8,128)(2,1)S(1)}, u32[]{:S(2)}) %copy-start.1) | copy-done | bytes 2097176
  59.3 2.4 %fusion.42 = f32[1024,1024]{1,0:T(8,128)S(1)} fusion(bf16[1024,1024]{1,0:T(8,128)(2,1)S(1)} %bitcast.67), kind=kOutput, calls=%fused_computation.83 | convolution fusion | flops 2147483648 | bytes 6291456 | tf_op jit(solution)/shard_map/dot_general | solution.py:76
  61.7 0.2 pad_maximum_fusion.1
  61.9 0.0 copy-start.3
  61.9 3.0 %select_reduce_fusion = (f32[]{:T(128)}, f32[1024,1024]{1,0:T(8,128)S(1)}) fusion(f32[1024,1024]{1,0:T(8,128)S(1)} %fusion.42, bf16[1024,1024]{1,0:T(8,128)(2,1)S(1)} %bitcast.70), kind=kOutput, calls=%fused_computation.7 | convolution fusion | flops 2151677952 | bytes 10485764 | tf_op jit(solution)/shard_map/dot_general | solution.py:76
  64.9 0.0 copy-done.3
  64.9 1.2 %fusion.10 = f32[1024,512]{1,0:T(8,128)S(1)} fusion(bf16[1024,512]{1,0:T(8,128)(2,1)S(1)} %bitcast.64, f32[1024,1024]{1,0:T(8,128)S(1)} %get-tuple-element.24), kind=kOutput, calls=%fused_computation.20 | convolution fusion | flops 1076887552 | bytes 7340032 | tf_op jit(solution)/shard_map/dot_general | solution.py:40
  66.2 0.7 copy-done
  66.9 1.5 %multiply_reduce_fusion.3 = (f32[512]{0:T(512)S(1)}, f32[512]{0:T(512)S(1)}, f32[1024,512]{1,0:T(8,128)S(1)}) fusion(bf16[4,2,4,2,16,512]{5,4,3,2,1,0:T(8,128)(2,1)S(1)} %pad_maximum_fusion.2, f32[1024,512]{1,0:T(8,128)S(1)} %fusion.10, bf16[1024,512]{1,0:T(8,128)(2,1)S(1)} %bitcast.65, f32[1024,1024]{1,0:T(8,128)S(1)} %get-tuple-element.24), kind=kOutput, calls=%fused_computation.27 | convolution fusion | flops 1078983680 | bytes 10489856 | tf_op jit(solution)/shard_map/dot_general | solution.py:40
  69.0 3.7 %multiply_reduce_fusion.2 = (f32[512]{0:T(512)S(1)}, f32[1024,512]{1,0:T(8,128)S(1)}) fusion(f32[1024,512]{1,0:T(8,128)S(1)} %get-tuple-element.25, f32[512]{0:T(512)S(1)} %get-tuple-element.10, f32[512]{0:T(512)S(1)} %get-tuple-element.9, bf16[4,2,4,2,16,512]{5,4,3,2,1,0:T(8,128)(2,1)S(1)} %pad_maximum_fusion.2, bf16[1024,512]{1,0:T(8,128)(2,1)S(1)} %bitcast.66, ...), kind=kOutput, calls=%fused_computation.26 | convolution fusion | flops 1081605632 | bytes 10491904 | tf_op jit(solution)/shard_map/dot_general | solution.py:40
  72.7 0.9 %multiply_reduce_fusion = (f32[512]{0:T(512)S(1)}, f32[512]{0:T(512)S(1)}) fusion(f32[512]{0:T(512)S(1)} %div.39, f32[1024,512]{1,0:T(8,128)S(1)} %get-tuple-element.27, f32[1024,512]{1,0:T(8,128)S(1)} %get-tuple-element.25, f32[512]{0:T(512)S(1)} %get-tuple-element.10, f32[512]{0:T(512)S(1)} %get-tuple-element.9, ...), kind=kLoop, calls=%fused_computation.23 | loop fusion | flops 6290432 | bytes 5253120 | tf_op jit(solution)/shard_map/reduce_sum | solution.py:92
  73.6 0.0 copy-start.4
  73.6 0.9 %fusion.5 = (bf16[1024,512]{1,0:T(8,128)(2,1)S(1)}, bf16[1024,512]{1,0:T(8,128)(2,1)S(1)}) fusion(f32[512]{0:T(512)S(1)} %div.39, f32[512]{0:T(512)S(1)} %add_divide_fusion, f32[512]{0:T(512)S(1)} %get-tuple-element.10, f32[1024,512]{1,0:T(8,128)S(1)} %get-tuple-element.25, f32[512]{0:T(512)S(1)} %get-tuple-element.9, ...), kind=kLoop, calls=%fused_computation.15 | loop fusion | flops 6815744 | bytes 5251072 | tf_op jit(solution)/shard_map/convert_element_type | solution.py:36
  74.5 0.0 copy-start.2
  74.6 0.7 copy-done.4
  75.2 0.5 fusion.26
  75.7 0.6 copy-done.2
  76.3 0.5 fusion.29
  76.8 0.5 fusion.13
  77.3 0.5 fusion.14
  77.8 0.1 collective-permute-start.11
  77.9 1.9 %collective-permute-done.11 = f32[128,2,512]{2,0,1:T(8,128)S(1)} collective-permute-done((f32[128,2,512]{2,0,1:T(8,128)S(1)}, f32[128,2,512]{2,0,1:T(8,128)S(1)}, u32[]{:S(2)}, u32[]{:S(2)}) %collective-permute-start.11) | collective-permute-done | bytes 524320 | tf_op jit(solution)/shard_map/ppermute | solution.py:31
  79.8 0.1 broadcast_select_fusion.1
  79.9 0.1 maximum_bitcast_fusion
  80.0 1.8 %copy.10 = f32[1,128,2,1024]{3,2,1,0:T(2,128)} copy(f32[1,128,2,1024]{3,1,2,0:T(8,128)S(1)} %maximum_bitcast_fusion) | data formatting | bytes 2097152 | tf_op jit(solution)/shard_map/broadcast_in_dim | solution.py:105
  (8 shorter events, 0.1 us)
Async XLA Ops:
  3.8 10.5 %all-to-all-start.1 = ((bf16[4,2,16,1024]{3,2,1,0:T(8,128)(2,1)}), bf16[4,2,16,1024]{3,2,1,0:T(8,128)(2,1)S(1)}, u32[]{:S(2)}, u32[]{:S(2)}) async-start(bf16[4,2,16,1024]{3,2,1,0:T(8,128)(2,1)} %copy.9), calls=%async_computation.1 | async-start | bytes 524288 | tf_op jit(solution)/shard_map/all_to_all | solution.py:52
  14.3 8.8 %all-to-all-start = ((bf16[4,2,16,1024]{3,2,1,0:T(8,128)(2,1)}), bf16[4,2,16,1024]{3,2,1,0:T(8,128)(2,1)S(1)}, u32[]{:S(2)}, u32[]{:S(2)}) async-start(bf16[4,2,16,1024]{3,2,1,0:T(8,128)(2,1)} %copy.8), calls=%async_computation | async-start | bytes 524288 | tf_op jit(solution)/shard_map/all_to_all | solution.py:52
  17.7 6.9 %collective-permute-start.7 = (bf16[4,2,16,512]{3,2,1,0:T(8,128)(2,1)S(1)}, bf16[4,2,16,512]{3,2,1,0:T(8,128)(2,1)S(1)}, u32[]{:S(2)}, u32[]{:S(2)}) collective-permute-start(bf16[4,2,16,512]{3,2,1,0:T(8,128)(2,1)S(1)} %get-tuple-element.20), channel_id=1, source_target_pairs={{0,1},{1,0},{2,3},{3,2},{4,5},{5,4},{6,7},{7,6},{8,9},{9,8},{10,11... | collective-permute-start | bytes 393224 | tf_op jit(solution)/shard_map/ppermute | solution.py:31
  23.1 10.1 %collective-permute-start.1 = (bf16[4,2,16,1024]{3,2,1,0:T(8,128)(2,1)S(1)}, bf16[4,2,16,1024]{3,2,1,0:T(8,128)(2,1)S(1)}, u32[]{:S(2)}, u32[]{:S(2)}) collective-permute-start(bf16[4,2,16,1024]{3,2,1,0:T(8,128)(2,1)S(1)} %all-to-all-done), channel_id=1, source_target_pairs={{0,2},{2,6},{6,4},{4,0},{1,3},{3,7},{7,5},{5,1},{8,10},{10,14},{14... | collective-permute-start | bytes 786440 | tf_op jit(solution)/shard_map/ppermute | solution.py:26
  24.7 14.1 %collective-permute-start.8 = (bf16[2,4,2,16,512]{4,3,2,1,0:T(8,128)(2,1)S(1)}, bf16[2,4,2,16,512]{4,3,2,1,0:T(8,128)(2,1)S(1)}, u32[]{:S(2)}, u32[]{:S(2)}) collective-permute-start(bf16[2,4,2,16,512]{4,3,2,1,0:T(8,128)(2,1)S(1)} %get-tuple-element.18), channel_id=1, source_target_pairs={{0,2},{2,6},{6,4},{4,0},{1,3},{3,7},{7,5},{5,1},{8,10},{10,14},{14... | collective-permute-start | bytes 786440 | tf_op jit(solution)/shard_map/ppermute | solution.py:26
  33.2 10.3 %collective-permute-start.3 = (bf16[4,2,16,1024]{3,2,1,0:T(8,128)(2,1)S(1)}, bf16[4,2,16,1024]{3,2,1,0:T(8,128)(2,1)S(1)}, u32[]{:S(2)}, u32[]{:S(2)}) collective-permute-start(bf16[4,2,16,1024]{3,2,1,0:T(8,128)(2,1)S(1)} %collective-permute-done.1), channel_id=1, source_target_pairs={{0,2},{2,6},{6,4},{4,0},{1,3},{3,7},{7,5},{5,1},{8,10},{10,14},{14... | collective-permute-start | bytes 786440 | tf_op jit(solution)/shard_map/ppermute | solution.py:26
  38.8 10.1 %collective-permute-start.9 = (bf16[2,4,2,16,512]{4,3,2,1,0:T(8,128)(2,1)S(1)}, bf16[2,4,2,16,512]{4,3,2,1,0:T(8,128)(2,1)S(1)}, u32[]{:S(2)}, u32[]{:S(2)}) collective-permute-start(bf16[2,4,2,16,512]{4,3,2,1,0:T(8,128)(2,1)S(1)} %collective-permute-done.8), channel_id=1, source_target_pairs={{0,2},{2,6},{6,4},{4,0},{1,3},{3,7},{7,5},{5,1},{8,10},{10,14},{14... | collective-permute-start | bytes 786440 | tf_op jit(solution)/shard_map/ppermute | solution.py:26
  39.6 10.6 %collective-permute-start = (bf16[4,2,16,1024]{3,2,1,0:T(8,128)(2,1)S(1)}, bf16[4,2,16,1024]{3,2,1,0:T(8,128)(2,1)S(1)}, u32[]{:S(2)}, u32[]{:S(2)}) collective-permute-start(bf16[4,2,16,1024]{3,2,1,0:T(8,128)(2,1)S(1)} %all-to-all-done), channel_id=1, source_target_pairs={{0,1},{1,0},{2,3},{3,2},{4,5},{5,4},{6,7},{7,6},{8,9},{9,8},{10,11... | collective-permute-start | bytes 786440 | tf_op jit(solution)/shard_map/ppermute | solution.py:31
  39.6 10.6 %collective-permute-start.2 = (bf16[4,2,16,1024]{3,2,1,0:T(8,128)(2,1)S(1)}, bf16[4,2,16,1024]{3,2,1,0:T(8,128)(2,1)S(1)}, u32[]{:S(2)}, u32[]{:S(2)}) collective-permute-start(bf16[4,2,16,1024]{3,2,1,0:T(8,128)(2,1)S(1)} %collective-permute-done.1), channel_id=1, source_target_pairs={{0,1},{1,0},{2,3},{3,2},{4,5},{5,4},{6,7},{7,6},{8,9},{9,8},{10,11... | collective-permute-start | bytes 786440 | tf_op jit(solution)/shard_map/ppermute | solution.py:31
  43.5 11.0 %collective-permute-start.5 = (bf16[4,2,16,1024]{3,2,1,0:T(8,128)(2,1)S(1)}, bf16[4,2,16,1024]{3,2,1,0:T(8,128)(2,1)S(1)}, u32[]{:S(2)}, u32[]{:S(2)}) collective-permute-start(bf16[4,2,16,1024]{3,2,1,0:T(8,128)(2,1)S(1)} %collective-permute-done.3), channel_id=1, source_target_pairs={{0,2},{2,6},{6,4},{4,0},{1,3},{3,7},{7,5},{5,1},{8,10},{10,14},{14... | collective-permute-start | bytes 786440 | tf_op jit(solution)/shard_map/ppermute | solution.py:26
  44.6 10.0 %collective-permute-start.4 = (bf16[4,2,16,1024]{3,2,1,0:T(8,128)(2,1)S(1)}, bf16[4,2,16,1024]{3,2,1,0:T(8,128)(2,1)S(1)}, u32[]{:S(2)}, u32[]{:S(2)}) collective-permute-start(bf16[4,2,16,1024]{3,2,1,0:T(8,128)(2,1)S(1)} %collective-permute-done.3), channel_id=1, source_target_pairs={{0,1},{1,0},{2,3},{3,2},{4,5},{5,4},{6,7},{7,6},{8,9},{9,8},{10,11... | collective-permute-start | bytes 786440 | tf_op jit(solution)/shard_map/ppermute | solution.py:31
  48.9 8.6 %collective-permute-start.10 = (bf16[2,4,2,16,512]{4,3,2,1,0:T(8,128)(2,1)S(1)}, bf16[2,4,2,16,512]{4,3,2,1,0:T(8,128)(2,1)S(1)}, u32[]{:S(2)}, u32[]{:S(2)}) collective-permute-start(bf16[2,4,2,16,512]{4,3,2,1,0:T(8,128)(2,1)S(1)} %collective-permute-done.9), channel_id=1, source_target_pairs={{0,2},{2,6},{6,4},{4,0},{1,3},{3,7},{7,5},{5,1},{8,10},{10,14},{14... | collective-permute-start | bytes 786440 | tf_op jit(solution)/shard_map/ppermute | solution.py:26
  54.5 3.1 %collective-permute-start.6 = (bf16[4,2,16,1024]{3,2,1,0:T(8,128)(2,1)S(1)}, bf16[4,2,16,1024]{3,2,1,0:T(8,128)(2,1)S(1)}, u32[]{:S(2)}, u32[]{:S(2)}) collective-permute-start(bf16[4,2,16,1024]{3,2,1,0:T(8,128)(2,1)S(1)} %collective-permute-done.5), channel_id=1, source_target_pairs={{0,1},{1,0},{2,3},{3,2},{4,5},{5,4},{6,7},{7,6},{8,9},{9,8},{10,11... | collective-permute-start | bytes 786440 | tf_op jit(solution)/shard_map/ppermute | solution.py:31
  58.0 1.3 %copy-start.1 = (bf16[4,2,4,2,16,1024]{5,4,3,2,1,0:T(8,128)(2,1)}, bf16[4,2,4,2,16,1024]{5,4,3,2,1,0:T(8,128)(2,1)S(1)}, u32[]{:S(2)}) copy-start(bf16[4,2,4,2,16,1024]{5,4,3,2,1,0:T(8,128)(2,1)S(1)} %pad_maximum_fusion) | copy-start | bytes 6291460
  61.9 3.0 %copy-start.3 = (bf16[4,2,4,2,16,1024]{5,4,3,2,1,0:T(8,128)(2,1)}, bf16[4,2,4,2,16,1024]{5,4,3,2,1,0:T(8,128)(2,1)S(1)}, u32[]{:S(2)}) copy-start(bf16[4,2,4,2,16,1024]{5,4,3,2,1,0:T(8,128)(2,1)S(1)} %pad_maximum_fusion.1) | copy-start | bytes 6291460
  64.9 1.9 %copy-start = (f32[1024,1024]{1,0:T(8,128)}, f32[1024,1024]{1,0:T(8,128)S(1)}, u32[]{:S(2)}) copy-start(f32[1024,1024]{1,0:T(8,128)S(1)} %get-tuple-element.24) | copy-start | bytes 12582916
  73.6 1.6 %copy-start.4 = (bf16[4,2,4,2,16,1024]{5,4,3,2,1,0:T(8,128)(2,1)S(1)}, bf16[4,2,4,2,16,1024]{5,4,3,2,1,0:T(8,128)(2,1)}, u32[]{:S(2)}) copy-start(bf16[4,2,4,2,16,1024]{5,4,3,2,1,0:T(8,128)(2,1)} %copy-done.3) | copy-start | bytes 6291460
  74.5 1.7 %copy-start.2 = (bf16[4,2,4,2,16,1024]{5,4,3,2,1,0:T(8,128)(2,1)S(1)}, bf16[4,2,4,2,16,1024]{5,4,3,2,1,0:T(8,128)(2,1)}, u32[]{:S(2)}) copy-start(bf16[4,2,4,2,16,1024]{5,4,3,2,1,0:T(8,128)(2,1)} %copy-done.1) | copy-start | bytes 6291460
  77.8 2.0 %collective-permute-start.11 = (f32[128,2,512]{2,0,1:T(8,128)S(1)}, f32[128,2,512]{2,0,1:T(8,128)S(1)}, u32[]{:S(2)}, u32[]{:S(2)}) collective-permute-start(f32[128,2,512]{2,0,1:T(8,128)S(1)} %fusion.23), channel_id=1, source_target_pairs={{0,1},{1,0},{2,3},{3,2},{4,5},{5,4},{6,7},{7,6},{8,9},{9,8},{10,11... | collective-permute-start | bytes 1572872 | tf_op jit(solution)/shard_map/ppermute | solution.py:31

commit v2 on v1

v2 whole, which is shorter than its diff:
```python
import functools
import math

import jax
import jax.numpy as jnp
import numpy as np
from jax import lax
from jax.experimental import pallas as pl
from jax.experimental.pallas import tpu as pltpu
from jax.sharding import Mesh, PartitionSpec as P

CHUNK = 256
LIMIT = 48 * 1024 * 1024


def make_table(samples, nfreq, first):
    times = np.arange(samples)
    phase = times[:, None] * (first + np.arange(nfreq))[None, :] % samples
    angle = np.float32(2.0 * math.pi) * phase.astype(np.float32) / np.float32(samples)
    return np.stack([np.cos(angle), -np.sin(angle)], -1).astype(jnp.bfloat16)


def spread_table(samples, nfreq, shots):
    table = make_table(samples, nfreq, samples // 16).astype(np.float32)
    whole = np.einsum("tfc,sz->fcszt", table, np.eye(shots, dtype=np.float32))
    return whole.reshape(nfreq * 2 * shots, shots * samples).astype(jnp.bfloat16)


def ring_order(chips):
    return [0, 1, 3, 2] if chips == 4 else list(range(chips))


def ring_gather(piece, chips):
    order = ring_order(chips)
    pairs = [(order[i], order[(i + 1) % chips]) for i in range(chips)]
    pieces = [piece]
    for _ in range(chips - 1):
        pieces.append(lax.ppermute(pieces[-1], "chip", pairs))
    return pieces


def swap_core(array):
    return lax.ppermute(array, "core", [(0, 1), (1, 0)])


def split(array):
    high = lax.reduce_precision(array, 8, 7)
    return high.astype(jnp.bfloat16), (array - high).astype(jnp.bfloat16)


def dot(left, right):
    return jnp.dot(left, right, preferred_element_type=jnp.float32)


def dot_nt(left, right):
    return lax.dot_general(left, right, (((1,), (1,)), ((), ())), preferred_element_type=jnp.float32)


def spectra(traces, matrix):
    return dot(matrix, traces.reshape(-1, traces.shape[2])).astype(jnp.bfloat16)


def to_freq(spec, nfreq):
    parts = spec.reshape(nfreq, -1, spec.shape[1])
    me = lax.axis_index("freq")
    out = []
    for step in range(nfreq):
        there = me ^ step
        part = lax.dynamic_index_in_dim(parts, there, 0, keepdims=False)
        out.append(part if step == 0 else lax.ppermute(part, "freq", [(f, f ^ step) for f in range(nfreq)]))
    return jnp.concatenate(out, 0)


def gram_kernel(shots, place, *refs):
    pieces, (high, low, damping, rows_t), (both,) = refs[:-5], refs[-5:-1], refs[-1:]
    width = pieces[0].shape[1]
    count = pieces[0].shape[0]
    total = jnp.zeros((1, width), jnp.float32)
    for number, piece in enumerate(pieces):
        block = piece[...]
        wide = block.astype(jnp.float32)
        total = total + jnp.sum(wide * wide, axis=0, keepdims=True)
        at = number * count
        both[pl.ds(at, count), pl.ds(0, width)] = block
        for part in range(0, count, 2 * shots):
            both[pl.ds(at + part, shots), pl.ds(width, width)] = -block[part + shots : part + 2 * shots]
            both[pl.ds(at + part + shots, shots), pl.ds(width, width)] = block[part : part + shots]
    damping[...] = 0.1 * jnp.sum(total, axis=1, keepdims=True) / width
    size = both.shape[0]
    for at in range(0, size, 256):
        gram = dot_nt(both[pl.ds(at, 256), :], both[...])
        rounded = gram.astype(jnp.bfloat16)
        high[pl.ds(at, 256), :] = rounded
        low[pl.ds(at, 256), :] = (gram - rounded.astype(jnp.float32)).astype(jnp.bfloat16)
    wide = rows_t.shape[0] // 4
    for number in range(2):
        start = pl.multiple_of(place[number] * wide, wide)
        rows_t[pl.ds(2 * number * wide, wide), :] = both[:, pl.ds(start, wide)].T
        rows_t[pl.ds((2 * number + 1) * wide, wide), :] = -both[:, pl.ds(width + start, wide)].T


def gram_call(place, pieces, shots, rows):
    count, width = pieces[0].shape
    size = count * len(pieces)
    square = jax.ShapeDtypeStruct((size, size), jnp.bfloat16)
    return pl.pallas_call(
        functools.partial(gram_kernel, shots),
        out_shape=(
            square,
            square,
            jax.ShapeDtypeStruct((1, 1), jnp.float32),
            jax.ShapeDtypeStruct((4 * rows, size), jnp.bfloat16),
        ),
        in_specs=[pl.BlockSpec(memory_space=pltpu.SMEM)] + [pl.BlockSpec(memory_space=pltpu.VMEM)] * len(pieces),
        out_specs=(pl.BlockSpec(memory_space=pltpu.VMEM),) * 4,
        scratch_shapes=[pltpu.VMEM((size, 2 * width), jnp.bfloat16)],
        compiler_params=pltpu.CompilerParams(vmem_limit_bytes=LIMIT),
        cost_estimate=pl.CostEstimate(flops=4 * size * size * width, bytes_accessed=4 * size * size, transcendentals=0),
        name="gram",
    )(place, *pieces)


def solve_kernel(high, low, damping, rows_t, *refs):
    pieces, (kept, sent), (start, image, step_high, step_low, step_image) = refs[:-7], refs[-7:-5], refs[-5:]
    size, columns = start.shape
    tiles = [pl.ds(at, 256) for at in range(0, size, 256)]
    count = pieces[0].shape[0]
    for number, piece in enumerate(pieces):
        start[pl.ds(number * count, count), :] = piece[...]
    damp = damping[...]
    norm_now = jnp.zeros((1, columns), jnp.float32)
    image_norm = jnp.zeros((1, columns), jnp.float32)
    for tile in tiles:
        value = dot(high[tile, :], start[...]) + dot(low[tile, :], start[...])
        image[tile, :] = value
        norm_now += jnp.sum(start[tile, :].astype(jnp.float32) * value, axis=0, keepdims=True)
        image_norm += jnp.sum(value * value, axis=0, keepdims=True)
    alpha = norm_now / (image_norm + damp * norm_now)
    keep = 1.0 - alpha * damp
    for tile in tiles:
        resid = keep * start[tile, :].astype(jnp.float32) - alpha * image[tile, :]
        rounded = resid.astype(jnp.bfloat16)
        step_high[tile, :] = rounded
        step_low[tile, :] = (resid - rounded.astype(jnp.float32)).astype(jnp.bfloat16)
    norm_next = jnp.zeros((1, columns), jnp.float32)
    for tile in tiles:
        value = dot(high[tile, :], step_high[...]) + (
            dot(low[tile, :], step_high[...]) + dot(high[tile, :], step_low[...])
        )
        step_image[tile, :] = value
        resid = keep * start[tile, :].astype(jnp.float32) - alpha * image[tile, :]
        norm_next += jnp.sum(resid * value, axis=0, keepdims=True)
    ratio = norm_next / norm_now
    curv = jnp.zeros((1, columns), jnp.float32)
    for tile in tiles:
        direc = (keep + ratio) * start[tile, :].astype(jnp.float32) - alpha * image[tile, :]
        value = step_image[tile, :] + ratio * image[tile, :]
        curv += jnp.sum(value * (value + damp * direc), axis=0, keepdims=True)
    beta = norm_next / curv
    from_start = alpha + beta * (keep + ratio)
    from_image = alpha * beta
    for tile in tiles:
        weight = from_start * start[tile, :].astype(jnp.float32) - from_image * image[tile, :]
        rounded = weight.astype(jnp.bfloat16)
        step_high[tile, :] = rounded
        step_low[tile, :] = (weight - rounded.astype(jnp.float32)).astype(jnp.bfloat16)
    rows = rows_t.shape[0] // 4
    for number, out in enumerate((kept, sent)):
        for part in range(2):
            left = rows_t[pl.ds((2 * number + part) * rows, rows), :]
            out[part] = dot(left, step_high[...]) + dot(left, step_low[...])


def solve_call(high, low, damping, rows_t, pieces):
    size = high.shape[0]
    columns = pieces[0].shape[1]
    rows = rows_t.shape[0] // 4
    block = jax.ShapeDtypeStruct((2, rows, columns), jnp.float32)
    return pl.pallas_call(
        solve_kernel,
        out_shape=(block, block),
        in_specs=[pl.BlockSpec(memory_space=pltpu.VMEM)] * (4 + len(pieces)),
        out_specs=(pl.BlockSpec(memory_space=pltpu.VMEM),) * 2,
        scratch_shapes=[
            pltpu.VMEM((size, columns), jnp.bfloat16),
            pltpu.VMEM((size, columns), jnp.float32),
            pltpu.VMEM((size, columns), jnp.bfloat16),
            pltpu.VMEM((size, columns), jnp.bfloat16),
            pltpu.VMEM((size, columns), jnp.float32),
        ],
        compiler_params=pltpu.CompilerParams(vmem_limit_bytes=LIMIT),
        cost_estimate=pl.CostEstimate(flops=12 * size * size * columns, bytes_accessed=4 * size * size, transcendentals=0),
        name="solve",
    )(high, low, damping, rows_t, *pieces)


def plain_gram(place, pieces, shots, rows):
    width = pieces[0].shape[1]
    even = jnp.concatenate(pieces, 0)
    turned = even.reshape(-1, 2, shots, width)
    odd = jnp.stack([-turned[:, 1], turned[:, 0]], 1).reshape(even.shape)
    blocks = []
    for number in range(2):
        blocks.append(lax.dynamic_slice_in_dim(even, place[number] * rows, rows, 1).T)
        blocks.append(-lax.dynamic_slice_in_dim(odd, place[number] * rows, rows, 1).T)
    return even, odd, 0.1 * jnp.sum(jnp.square(even.astype(jnp.float32))) / width, jnp.concatenate(blocks, 0)


def dot_tn(left, right):
    return lax.dot_general(left, right, (((0,), (0,)), ((), ())), preferred_element_type=jnp.float32)


def plain_apply(even, odd, parts):
    out = []
    for side in (even, odd):
        high, low = split(sum(dot_tn(side, part) for part in parts))
        out.append(dot(side, high) + dot(side, low))
    return out[0] + out[1]


def plain_solve(even, odd, damping, rows_t, pieces):
    start = jnp.concatenate(pieces, 0)
    wide = start.astype(jnp.float32)
    image = plain_apply(even, odd, (start,))
    norm_now = jnp.sum(wide * image, axis=0)
    alpha = norm_now / (jnp.sum(image * image, axis=0) + damping * norm_now)
    resid = (1.0 - alpha * damping) * wide - alpha * image
    resid_image = plain_apply(even, odd, split(resid))
    norm_next = jnp.sum(resid * resid_image, axis=0)
    ratio = norm_next / norm_now
    direc = resid + ratio * wide
    direc_image = resid_image + ratio * image
    curv = jnp.sum(direc_image * (direc_image + damping * direc), axis=0)
    weights_high, weights_low = split(alpha * wide + norm_next / curv * direc)
    block = (dot(rows_t, weights_high) + dot(rows_t, weights_low)).reshape(2, 2, -1, start.shape[1])
    return block[0], block[1]


def shards(up_traces, down_traces):
    local_shots, samples, width = up_traces.shape
    nfreq, chips = lax.axis_size("freq"), lax.axis_size("chip")
    core = lax.axis_index("core")
    half = width // 2
    rows = width // (2 * chips)
    size = 2 * local_shots * nfreq * 2 * chips
    matrix = jnp.asarray(spread_table(samples, nfreq, local_shots))

    down = to_freq(spectra(down_traces, matrix), nfreq)
    own = ring_gather(down, chips)
    pieces = []
    for piece in own:
        pieces += [piece, swap_core(piece)]

    up = to_freq(spectra(up_traces, matrix), nfreq)
    mine = lax.dynamic_slice_in_dim(up, core * half, half, 1)
    theirs = swap_core(lax.dynamic_slice_in_dim(up, (1 - core) * half, half, 1))
    up = jnp.concatenate([mine, theirs], 0)

    place = 2 * lax.axis_index("chip") + jnp.stack([core, 1 - core]).astype(jnp.int32)
    small = size <= 1024 and rows % 128 == 0 and half % CHUNK == 0 and local_shots % 16 == 0
    gram, solve = (gram_call, solve_call) if small else (plain_gram, plain_solve)
    operator = gram(place, pieces, local_shots, rows)
    chunk = CHUNK if half % CHUNK == 0 else half
    kept, got = [], []
    for at in range(0, half, chunk):
        stay, send = solve(*operator, ring_gather(up[:, at : at + chunk], chips))
        kept.append(stay)
        got.append(swap_core(send))
    kept, got = jnp.concatenate(kept, 2), jnp.concatenate(got, 2)
    first = core == 0
    block = jnp.concatenate([jnp.where(first, kept, got), jnp.where(first, got, kept)], 2)
    return jnp.transpose(block, (1, 0, 2))[None]


def solution(mesh):
    nfreq, nshot = mesh.devices.shape
    fine = Mesh(mesh.devices.reshape(nfreq, nshot // 2, 2), ("freq", "chip", "core"))
    spec = P(("freq", "chip", "core"), None, None)
    out_specs = P("freq", ("chip", "core"), None, None)
    return jax.shard_map(shards, mesh=fine, in_specs=(spec, spec), out_specs=out_specs, check_vma=False)
```

time: 82.2 us -> 74.6 us (0.908)
  Pallas kernels: 0 us -> 20.2 us
  matrix products: 19.3 us -> 3.95 us
  waiting for transfers between devices: 34.4 us -> 26.7 us
  local copies, waits for them, and re-layouts: 6.55 us -> 1.94 us
  starting transfers between devices: 17.4 us -> 21 us
  other arithmetic: 3.2 us -> 0.35 us
    pallas_call x0 -> x3, Pallas kernels: none -> 20.2 us  [the longest x2 13.6 us: solve_call(): pl.pallas_call(solve_kernel, out_shape=(block, block), in_specs=[pl.Block...]
    dot_general x8 -> x0, matrix products: 12.9 us -> none  [the longest x2 5.69 us: spectra(): jnp.einsum('str,tfc->fcsr', traces, table, preferred_element_type=jnp.flo...]
    ppermute x6 -> x9, waiting for transfers between devices: 25.6 us -> 16 us  [ring_gather(): pieces.append(lax.ppermute(pieces[-1], 'chip', pairs))]
    all_to_all x2 -> x0, starting transfers between devices: 8.57 us -> none  [to_freq(): return lax.all_to_all(spec, 'freq', split_axis=0, concat_axis=0, tiled=True)]
    ppermute x0 -> x6, waiting for transfers between devices: none -> 8.33 us  [to_freq(): lax.ppermute(part, 'freq', [(f, f ^ step) for f in range(nfreq)])]
    ppermute x0 -> x6, starting transfers between devices: none -> 8.1 us  [to_freq(): lax.ppermute(part, 'freq', [(f, f ^ step) for f in range(nfreq)])]
    all_to_all x2 -> x0, waiting for transfers between devices: 6.96 us -> none  [to_freq(): return lax.all_to_all(spec, 'freq', split_axis=0, concat_axis=0, tiled=True)]
    ppermute x6 -> x9, starting transfers between devices: 8.17 us -> 11.7 us  [ring_gather(): pieces.append(lax.ppermute(pieces[-1], 'chip', pairs))]
  transfers between devices with their start and end apart: 14 -> 22, of which waited for: 9 -> 14; matrix products, arithmetic and copies ran while one was open for 5% -> 1% of each run, Pallas kernels for 0% -> 27%
where the time goes in v2:
time: 74.6 us; the launch traced here: 74.4 us
  waiting for transfers between devices  26.7 us (36%)
  starting transfers between devices  21 us (28%)
  Pallas kernels  20.2 us (27%)
  matrix products  3.95 us (5%)
  local copies, waits for them, and re-layouts  1.94 us (3%)
    ppermute x9, waiting for transfers between devices, ring_gather(): pieces.append(lax.ppermute(pieces[-1], 'chip', pairs))  16 us
    pallas_call x2, Pallas kernels, solve_call(): pl.pallas_call(solve_kernel, out_shape=(block, block), in_specs=[pl.Block...  13.6 us
    ppermute x9, starting transfers between devices, ring_gather(): pieces.append(lax.ppermute(pieces[-1], 'chip', pairs))  11.7 us
    ppermute x6, waiting for transfers between devices, to_freq(): lax.ppermute(part, 'freq', [(f, f ^ step) for f in range(nfreq)])  8.33 us
    ppermute x6, starting transfers between devices, to_freq(): lax.ppermute(part, 'freq', [(f, f ^ step) for f in range(nfreq)])  8.1 us
    pallas_call x1, Pallas kernels, gram_call(): pl.pallas_call(functools.partial(gram_kernel, shots), out_shape=(square,...  6.6 us
    dot_general x2, matrix products, dot(): return jnp.dot(left, right, preferred_element_type=jnp.float32)  3.95 us
    ppermute x7, waiting for transfers between devices, swap_core(): return lax.ppermute(array, 'core', [(0, 1), (1, 0)])  2.4 us
  transfers between devices with their start and end apart: 22, of which 14 were waited for; matrix products, arithmetic and copies ran while one was open for 1% of the time, Pallas kernels for 27%

profile of v2, /device:TPU:0, one launch (start us, length us, event | category | flops | bytes accessed | tf_op | source)
XLA Modules:
  0.0 74.4 jit_solution(18069371342842183297)
XLA Ops:
  0.0 0.0 copy-start.1
  0.0 0.0 copy-start
  0.0 3.2 %convolution_convert_fusion.1 = bf16[128,1024]{1,0:T(8,128)(2,1)S(1)} fusion(bf16[128,2048]{1,0:T(8,128)(2,1)} %constant.44.clone, bf16[2048,1024]{1,0:T(8,128)(2,1)} %bitcast.30), kind=kOutput, calls=%fused_computation.1 | convolution fusion | flops 537001984 | bytes 4980736 | tf_op jit(solution)/shard_map/dot_general | solution.py:52
  3.3 3.0 %collective-permute-start = (bf16[32,1024]{1,0:T(8,128)(2,1)S(1)}, bf16[32,1024]{1,0:T(8,128)(2,1)S(1)}, u32[]{:S(2)}, u32[]{:S(2)}) collective-permute-start(bf16[32,1024]{1,0:T(8,128)(2,1)S(1)} %get-tuple-element.34), channel_id=1, source_target_pairs={{0,8},{8,0},{16,24},{24,16},{1,9},{9,1},{17,25},{25,17},{2,10},{10... | collective-permute-start | bytes 196616 | tf_op jit(solution)/shard_map/ppermute | solution.py:70
  6.3 1.5 %collective-permute-start.1 = (bf16[32,1024]{1,0:T(8,128)(2,1)S(1)}, bf16[32,1024]{1,0:T(8,128)(2,1)S(1)}, u32[]{:S(2)}, u32[]{:S(2)}) collective-permute-start(bf16[32,1024]{1,0:T(8,128)(2,1)S(1)} %get-tuple-element.33), channel_id=1, source_target_pairs={{0,16},{8,24},{16,0},{24,8},{1,17},{9,25},{17,1},{25,9},{2,18},{10... | collective-permute-start | bytes 196616 | tf_op jit(solution)/shard_map/ppermute | solution.py:70
  7.8 0.0 collective-permute-start.2
  7.8 0.8 %collective-permute-done = bf16[32,1024]{1,0:T(8,128)(2,1)S(1)} collective-permute-done((bf16[32,1024]{1,0:T(8,128)(2,1)S(1)}, bf16[32,1024]{1,0:T(8,128)(2,1)S(1)}, u32[]{:S(2)}, u32[]{:S(2)}) %collective-permute-start) | collective-permute-done | bytes 65568 | tf_op jit(solution)/shard_map/ppermute | solution.py:70
  8.6 1.9 %collective-permute-done.1 = bf16[32,1024]{1,0:T(8,128)(2,1)S(1)} collective-permute-done((bf16[32,1024]{1,0:T(8,128)(2,1)S(1)}, bf16[32,1024]{1,0:T(8,128)(2,1)S(1)}, u32[]{:S(2)}, u32[]{:S(2)}) %collective-permute-start.1) | collective-permute-done | bytes 65568 | tf_op jit(solution)/shard_map/ppermute | solution.py:70
  10.5 2.4 %collective-permute-done.2 = bf16[32,1024]{1,0:T(8,128)(2,1)S(1)} collective-permute-done((bf16[32,1024]{1,0:T(8,128)(2,1)S(1)}, bf16[32,1024]{1,0:T(8,128)(2,1)S(1)}, u32[]{:S(2)}, u32[]{:S(2)}) %collective-permute-start.2) | collective-permute-done | bytes 65568 | tf_op jit(solution)/shard_map/ppermute | solution.py:70
  13.0 1.6 %collective-permute-start.4 = (bf16[128,1024]{1,0:T(8,128)(2,1)S(1)}, bf16[128,1024]{1,0:T(8,128)(2,1)S(1)}, u32[]{:S(2)}, u32[]{:S(2)}) collective-permute-start(bf16[128,1024]{1,0:T(8,128)(2,1)S(1)} %pad_maximum_fusion.refs_0_), channel_id=1, source_target_pairs={{0,2},{2,6},{6,4},{4,0},{1,3},{3,7},{7,5},{5,1},{8,10},{10,14},{14... | collective-permute-start | bytes 786440 | tf_op jit(solution)/shard_map/ppermute | solution.py:38
  14.6 0.0 copy-done.1
  14.6 0.0 copy-done
  14.6 0.7 convolution_convert_fusion
  15.4 4.9 %collective-permute-done.4.refs_2_ = bf16[128,1024]{1,0:T(8,128)(2,1)S(1)} collective-permute-done((bf16[128,1024]{1,0:T(8,128)(2,1)S(1)}, bf16[128,1024]{1,0:T(8,128)(2,1)S(1)}, u32[]{:S(2)}, u32[]{:S(2)}) %collective-permute-start.4) | collective-permute-done | bytes 262176 | tf_op jit(solution)/shard_map/ppermute | solution.py:38
  20.3 0.8 %collective-permute-start.6 = (bf16[128,1024]{1,0:T(8,128)(2,1)S(1)}, bf16[128,1024]{1,0:T(8,128)(2,1)S(1)}, u32[]{:S(2)}, u32[]{:S(2)}) collective-permute-start(bf16[128,1024]{1,0:T(8,128)(2,1)S(1)} %collective-permute-done.4.refs_2_), channel_id=1, source_target_pairs={{0,2},{2,6},{6,4},{4,0},{1,3},{3,7},{7,5},{5,1},{8,10},{10,14},{14... | collective-permute-start | bytes 786440 | tf_op jit(solution)/shard_map/ppermute | solution.py:38
  21.1 1.0 %collective-permute-start.10 = (bf16[32,1024]{1,0:T(8,128)(2,1)S(1)}, bf16[32,1024]{1,0:T(8,128)(2,1)S(1)}, u32[]{:S(2)}, u32[]{:S(2)}) collective-permute-start(bf16[32,1024]{1,0:T(8,128)(2,1)S(1)} %get-tuple-element.30), channel_id=1, source_target_pairs={{0,8},{8,0},{16,24},{24,16},{1,9},{9,1},{17,25},{25,17},{2,10},{10... | collective-permute-start | bytes 196616 | tf_op jit(solution)/shard_map/ppermute | solution.py:70
  22.1 0.6 collective-permute-start.11
  22.7 2.0 %collective-permute-start.12 = (bf16[32,1024]{1,0:T(8,128)(2,1)S(1)}, bf16[32,1024]{1,0:T(8,128)(2,1)S(1)}, u32[]{:S(2)}, u32[]{:S(2)}) collective-permute-start(bf16[32,1024]{1,0:T(8,128)(2,1)S(1)} %get-tuple-element.28), channel_id=1, source_target_pairs={{0,24},{8,16},{16,8},{24,0},{1,25},{9,17},{17,9},{25,1},{2,26},{10... | collective-permute-start | bytes 196616 | tf_op jit(solution)/shard_map/ppermute | solution.py:70
  24.7 0.0 collective-permute-start.3
  24.7 0.8 %collective-permute-done.10 = bf16[32,1024]{1,0:T(8,128)(2,1)S(1)} collective-permute-done((bf16[32,1024]{1,0:T(8,128)(2,1)S(1)}, bf16[32,1024]{1,0:T(8,128)(2,1)S(1)}, u32[]{:S(2)}, u32[]{:S(2)}) %collective-permute-start.10) | collective-permute-done | bytes 65568 | tf_op jit(solution)/shard_map/ppermute | solution.py:70
  25.4 0.9 %collective-permute-done.11 = bf16[32,1024]{1,0:T(8,128)(2,1)S(1)} collective-permute-done((bf16[32,1024]{1,0:T(8,128)(2,1)S(1)}, bf16[32,1024]{1,0:T(8,128)(2,1)S(1)}, u32[]{:S(2)}, u32[]{:S(2)}) %collective-permute-start.11) | collective-permute-done | bytes 65568 | tf_op jit(solution)/shard_map/ppermute | solution.py:70
  26.3 1.5 %collective-permute-done.12 = bf16[32,1024]{1,0:T(8,128)(2,1)S(1)} collective-permute-done((bf16[32,1024]{1,0:T(8,128)(2,1)S(1)}, bf16[32,1024]{1,0:T(8,128)(2,1)S(1)}, u32[]{:S(2)}, u32[]{:S(2)}) %collective-permute-start.12) | collective-permute-done | bytes 65568 | tf_op jit(solution)/shard_map/ppermute | solution.py:70
  27.9 0.0 collective-permute-done.6.refs_4_
  27.9 3.4 %collective-permute-start.8 = (bf16[128,1024]{1,0:T(8,128)(2,1)S(1)}, bf16[128,1024]{1,0:T(8,128)(2,1)S(1)}, u32[]{:S(2)}, u32[]{:S(2)}) collective-permute-start(bf16[128,1024]{1,0:T(8,128)(2,1)S(1)} %collective-permute-done.6.refs_4_), channel_id=1, source_target_pairs={{0,2},{2,6},{6,4},{4,0},{1,3},{3,7},{7,5},{5,1},{8,10},{10,14},{14... | collective-permute-start | bytes 786440 | tf_op jit(solution)/shard_map/ppermute | solution.py:38
  31.3 0.1 collective-permute-start.13
  31.4 1.3 %collective-permute-done.13 = bf16[128,512]{1,0:T(8,128)(2,1)S(1)} collective-permute-done((bf16[128,512]{1,0:T(8,128)(2,1)S(1)}, bf16[128,512]{1,0:T(8,128)(2,1)S(1)}, u32[]{:S(2)}, u32[]{:S(2)}) %collective-permute-start.13) | collective-permute-done | bytes 131104 | tf_op jit(solution)/shard_map/ppermute | solution.py:43
  32.8 0.5 collective-permute-start.17
  33.2 0.4 collective-permute-start.14
  33.6 0.0 collective-permute-start.5
  33.6 0.0 collective-permute-done.3.refs_1_
  33.6 0.5 collective-permute-start.7
  34.1 2.8 %collective-permute-done.8.refs_6_ = bf16[128,1024]{1,0:T(8,128)(2,1)S(1)} collective-permute-done((bf16[128,1024]{1,0:T(8,128)(2,1)S(1)}, bf16[128,1024]{1,0:T(8,128)(2,1)S(1)}, u32[]{:S(2)}, u32[]{:S(2)}) %collective-permute-start.8) | collective-permute-done | bytes 262176 | tf_op jit(solution)/shard_map/ppermute | solution.py:38
  36.9 0.0 collective-permute-start.9
  36.9 3.2 %collective-permute-done.17.refs_1_ = bf16[256,256]{1,0:T(8,128)(2,1)S(1)} collective-permute-done((bf16[256,256]{1,0:T(8,128)(2,1)S(1)}, bf16[256,256]{1,0:T(8,128)(2,1)S(1)}, u32[]{:S(2)}, u32[]{:S(2)}) %collective-permute-start.17) | collective-permute-done | bytes 131104 | tf_op jit(solution)/shard_map/ppermute | solution.py:38
  40.1 1.8 %collective-permute-start.18 = (bf16[256,256]{1,0:T(8,128)(2,1)S(1)}, bf16[256,256]{1,0:T(8,128)(2,1)S(1)}, u32[]{:S(2)}, u32[]{:S(2)}) collective-permute-start(bf16[256,256]{1,0:T(8,128)(2,1)S(1)} %collective-permute-done.17.refs_1_), channel_id=1, source_target_pairs={{0,2},{2,6},{6,4},{4,0},{1,3},{3,7},{7,5},{5,1},{8,10},{10,14},{14... | collective-permute-start | bytes 393224 | tf_op jit(solution)/shard_map/ppermute | solution.py:38
  41.9 0.2 collective-permute-done.14.refs_1_
  42.1 2.0 %collective-permute-start.15 = (bf16[256,256]{1,0:T(8,128)(2,1)S(1)}, bf16[256,256]{1,0:T(8,128)(2,1)S(1)}, u32[]{:S(2)}, u32[]{:S(2)}) collective-permute-start(bf16[256,256]{1,0:T(8,128)(2,1)S(1)} %collective-permute-done.14.refs_1_), channel_id=1, source_target_pairs={{0,2},{2,6},{6,4},{4,0},{1,3},{3,7},{7,5},{5,1},{8,10},{10,14},{14... | collective-permute-start | bytes 393224 | tf_op jit(solution)/shard_map/ppermute | solution.py:38
  44.1 0.1 add_add_fusion.place
  44.1 2.9 %collective-permute-done.18.refs_2_ = bf16[256,256]{1,0:T(8,128)(2,1)S(1)} collective-permute-done((bf16[256,256]{1,0:T(8,128)(2,1)S(1)}, bf16[256,256]{1,0:T(8,128)(2,1)S(1)}, u32[]{:S(2)}, u32[]{:S(2)}) %collective-permute-start.18) | collective-permute-done | bytes 131104 | tf_op jit(solution)/shard_map/ppermute | solution.py:38
  47.1 0.8 %collective-permute-start.19 = (bf16[256,256]{1,0:T(8,128)(2,1)S(1)}, bf16[256,256]{1,0:T(8,128)(2,1)S(1)}, u32[]{:S(2)}, u32[]{:S(2)}) collective-permute-start(bf16[256,256]{1,0:T(8,128)(2,1)S(1)} %collective-permute-done.18.refs_2_), channel_id=1, source_target_pairs={{0,2},{2,6},{6,4},{4,0},{1,3},{3,7},{7,5},{5,1},{8,10},{10,14},{14... | collective-permute-start | bytes 393224 | tf_op jit(solution)/shard_map/ppermute | solution.py:38
  47.8 2.0 %collective-permute-done.15.refs_2_ = bf16[256,256]{1,0:T(8,128)(2,1)S(1)} collective-permute-done((bf16[256,256]{1,0:T(8,128)(2,1)S(1)}, bf16[256,256]{1,0:T(8,128)(2,1)S(1)}, u32[]{:S(2)}, u32[]{:S(2)}) %collective-permute-start.15) | collective-permute-done | bytes 131104 | tf_op jit(solution)/shard_map/ppermute | solution.py:38
  49.9 0.5 collective-permute-start.16
  50.3 0.0 collective-permute-done.5.refs_3_
  50.3 0.0 collective-permute-done.7.refs_5_
  50.3 0.0 collective-permute-done.9.refs_7_
  50.3 6.6 %gram.1 = (bf16[1024,1024]{1,0:T(8,128)(2,1)S(1)}, bf16[1024,1024]{1,0:T(8,128)(2,1)}, f32[1,1]{1,0:T(1,128)}, bf16[512,1024]{1,0:T(8,128)(2,1)S(1)}) custom-call(s32[2]{0:T(128)S(1)} %add_add_fusion.place, bf16[128,1024]{1,0:T(8,128)(2,1)S(1)} %pad_maximum_fusion.refs_0_, bf16[128,1024]{1,0:T(8,128)(2,1)S(1)} %collective-permute-done.3.refs_1_, ...), custom_call_target="tpu_custom_call" | custom-call | flops 4294967296 | bytes 4194304 | tf_op jit(solution)/shard_map/gram/pallas_call | solution.py:106
  56.9 0.0 collective-permute-done.16.refs_3_
  56.9 6.8 %solve.2 = (f32[2,128,256]{2,1,0:T(8,128)S(1)}, f32[2,128,256]{2,1,0:T(8,128)S(1)}) custom-call(bf16[1024,1024]{1,0:T(8,128)(2,1)S(1)} %get-tuple-element.13.high, bf16[1024,1024]{1,0:T(8,128)(2,1)} %get-tuple-element.14.low, f32[1,1]{1,0:T(1,128)} %get-tuple-element.15.damping, bf16[512,1024]{1,0:T(8,128)(2,1)S(1)} %get-tuple-element.16.rows_t, ...), custom_call_target="tpu_custom_call" | custom-call | flops 3221225472 | bytes 4194304 | tf_op jit(solution)/shard_map/solve/pallas_call | solution.py:179
  63.7 0.1 collective-permute-start.20
  63.8 0.0 collective-permute-done.19.refs_3_
  63.8 6.8 %solve.3 = (f32[2,128,256]{2,1,0:T(8,128)S(1)}, f32[2,128,256]{2,1,0:T(8,128)S(1)}) custom-call(bf16[1024,1024]{1,0:T(8,128)(2,1)S(1)} %get-tuple-element.13.high, bf16[1024,1024]{1,0:T(8,128)(2,1)} %get-tuple-element.14.low, f32[1,1]{1,0:T(1,128)} %get-tuple-element.15.damping, bf16[512,1024]{1,0:T(8,128)(2,1)S(1)} %get-tuple-element.16.rows_t, ...), custom_call_target="tpu_custom_call" | custom-call | flops 3221225472 | bytes 4194304 | tf_op jit(solution)/shard_map/solve/pallas_call | solution.py:179
  70.6 0.6 collective-permute-start.21
  71.2 0.0 collective-permute-done.20
  71.3 1.1 %collective-permute-done.21 = f32[2,128,256]{2,1,0:T(8,128)S(1)} collective-permute-done((f32[2,128,256]{2,1,0:T(8,128)S(1)}, f32[2,128,256]{2,1,0:T(8,128)S(1)}, u32[]{:S(2)}, u32[]{:S(2)}) %collective-permute-start.21) | collective-permute-done | bytes 262176 | tf_op jit(solution)/shard_map/ppermute | solution.py:43
  72.3 0.1 broadcast_select_fusion.1
  72.5 0.1 maximum_bitcast_fusion
  72.6 1.8 %copy.4 = f32[1,128,2,1024]{3,2,1,0:T(2,128)} copy(f32[1,128,2,1024]{3,1,2,0:T(8,128)S(1)} %maximum_bitcast_fusion) | data formatting | bytes 2097152 | tf_op jit(solution)/shard_map/broadcast_in_dim | solution.py:272
  (10 shorter events, 0.2 us)
Async XLA Ops:
  0.0 14.6 %copy-start.1 = (bf16[128,2048]{1,0:T(8,128)(2,1)S(1)}, bf16[128,2048]{1,0:T(8,128)(2,1)}, u32[]{:S(2)}) copy-start(bf16[128,2048]{1,0:T(8,128)(2,1)} %constant.44.clone) | copy-start | bytes 1572868
  0.0 14.6 %copy-start = (bf16[16,128,1024]{2,1,0:T(8,128)(2,1)S(1)}, bf16[16,128,1024]{2,1,0:T(8,128)(2,1)}, u32[]{:S(2)}) copy-start(bf16[16,128,1024]{2,1,0:T(8,128)(2,1)} %param.3) | copy-start | bytes 12582916
  3.3 5.4 %collective-permute-start = (bf16[32,1024]{1,0:T(8,128)(2,1)S(1)}, bf16[32,1024]{1,0:T(8,128)(2,1)S(1)}, u32[]{:S(2)}, u32[]{:S(2)}) collective-permute-start(bf16[32,1024]{1,0:T(8,128)(2,1)S(1)} %get-tuple-element.34), channel_id=1, source_target_pairs={{0,8},{8,0},{16,24},{24,16},{1,9},{9,1},{17,25},{25,17},{2,10},{10... | collective-permute-start | bytes 196616 | tf_op jit(solution)/shard_map/ppermute | solution.py:70
  6.3 4.3 %collective-permute-start.1 = (bf16[32,1024]{1,0:T(8,128)(2,1)S(1)}, bf16[32,1024]{1,0:T(8,128)(2,1)S(1)}, u32[]{:S(2)}, u32[]{:S(2)}) collective-permute-start(bf16[32,1024]{1,0:T(8,128)(2,1)S(1)} %get-tuple-element.33), channel_id=1, source_target_pairs={{0,16},{8,24},{16,0},{24,8},{1,17},{9,25},{17,1},{25,9},{2,18},{10... | collective-permute-start | bytes 196616 | tf_op jit(solution)/shard_map/ppermute | solution.py:70
  7.8 5.2 %collective-permute-start.2 = (bf16[32,1024]{1,0:T(8,128)(2,1)S(1)}, bf16[32,1024]{1,0:T(8,128)(2,1)S(1)}, u32[]{:S(2)}, u32[]{:S(2)}) collective-permute-start(bf16[32,1024]{1,0:T(8,128)(2,1)S(1)} %get-tuple-element.32), channel_id=1, source_target_pairs={{0,24},{8,16},{16,8},{24,0},{1,25},{9,17},{17,9},{25,1},{2,26},{10... | collective-permute-start | bytes 196616 | tf_op jit(solution)/shard_map/ppermute | solution.py:70
  13.0 7.3 %collective-permute-start.4 = (bf16[128,1024]{1,0:T(8,128)(2,1)S(1)}, bf16[128,1024]{1,0:T(8,128)(2,1)S(1)}, u32[]{:S(2)}, u32[]{:S(2)}) collective-permute-start(bf16[128,1024]{1,0:T(8,128)(2,1)S(1)} %pad_maximum_fusion.refs_0_), channel_id=1, source_target_pairs={{0,2},{2,6},{6,4},{4,0},{1,3},{3,7},{7,5},{5,1},{8,10},{10,14},{14... | collective-permute-start | bytes 786440 | tf_op jit(solution)/shard_map/ppermute | solution.py:38
  20.3 7.6 %collective-permute-start.6 = (bf16[128,1024]{1,0:T(8,128)(2,1)S(1)}, bf16[128,1024]{1,0:T(8,128)(2,1)S(1)}, u32[]{:S(2)}, u32[]{:S(2)}) collective-permute-start(bf16[128,1024]{1,0:T(8,128)(2,1)S(1)} %collective-permute-done.4.refs_2_), channel_id=1, source_target_pairs={{0,2},{2,6},{6,4},{4,0},{1,3},{3,7},{7,5},{5,1},{8,10},{10,14},{14... | collective-permute-start | bytes 786440 | tf_op jit(solution)/shard_map/ppermute | solution.py:38
  21.1 4.3 %collective-permute-start.10 = (bf16[32,1024]{1,0:T(8,128)(2,1)S(1)}, bf16[32,1024]{1,0:T(8,128)(2,1)S(1)}, u32[]{:S(2)}, u32[]{:S(2)}) collective-permute-start(bf16[32,1024]{1,0:T(8,128)(2,1)S(1)} %get-tuple-element.30), channel_id=1, source_target_pairs={{0,8},{8,0},{16,24},{24,16},{1,9},{9,1},{17,25},{25,17},{2,10},{10... | collective-permute-start | bytes 196616 | tf_op jit(solution)/shard_map/ppermute | solution.py:70
  22.1 4.3 %collective-permute-start.11 = (bf16[32,1024]{1,0:T(8,128)(2,1)S(1)}, bf16[32,1024]{1,0:T(8,128)(2,1)S(1)}, u32[]{:S(2)}, u32[]{:S(2)}) collective-permute-start(bf16[32,1024]{1,0:T(8,128)(2,1)S(1)} %get-tuple-element.29), channel_id=1, source_target_pairs={{0,16},{8,24},{16,0},{24,8},{1,17},{9,25},{17,1},{25,9},{2,18},{10... | collective-permute-start | bytes 196616 | tf_op jit(solution)/shard_map/ppermute | solution.py:70
  22.7 5.2 %collective-permute-start.12 = (bf16[32,1024]{1,0:T(8,128)(2,1)S(1)}, bf16[32,1024]{1,0:T(8,128)(2,1)S(1)}, u32[]{:S(2)}, u32[]{:S(2)}) collective-permute-start(bf16[32,1024]{1,0:T(8,128)(2,1)S(1)} %get-tuple-element.28), channel_id=1, source_target_pairs={{0,24},{8,16},{16,8},{24,0},{1,25},{9,17},{17,9},{25,1},{2,26},{10... | collective-permute-start | bytes 196616 | tf_op jit(solution)/shard_map/ppermute | solution.py:70
  24.7 9.0 %collective-permute-start.3 = (bf16[128,1024]{1,0:T(8,128)(2,1)S(1)}, bf16[128,1024]{1,0:T(8,128)(2,1)S(1)}, u32[]{:S(2)}, u32[]{:S(2)}) collective-permute-start(bf16[128,1024]{1,0:T(8,128)(2,1)S(1)} %pad_maximum_fusion.refs_0_), channel_id=1, source_target_pairs={{0,1},{1,0},{2,3},{3,2},{4,5},{5,4},{6,7},{7,6},{8,9},{9,8},{10,11... | collective-permute-start | bytes 786440 | tf_op jit(solution)/shard_map/ppermute | solution.py:43
  27.9 9.0 %collective-permute-start.8 = (bf16[128,1024]{1,0:T(8,128)(2,1)S(1)}, bf16[128,1024]{1,0:T(8,128)(2,1)S(1)}, u32[]{:S(2)}, u32[]{:S(2)}) collective-permute-start(bf16[128,1024]{1,0:T(8,128)(2,1)S(1)} %collective-permute-done.6.refs_4_), channel_id=1, source_target_pairs={{0,2},{2,6},{6,4},{4,0},{1,3},{3,7},{7,5},{5,1},{8,10},{10,14},{14... | collective-permute-start | bytes 786440 | tf_op jit(solution)/shard_map/ppermute | solution.py:38
  31.3 1.4 %collective-permute-start.13 = (bf16[128,512]{1,0:T(8,128)(2,1)S(1)}, bf16[128,512]{1,0:T(8,128)(2,1)S(1)}, u32[]{:S(2)}, u32[]{:S(2)}) collective-permute-start(bf16[128,512]{1,0:T(8,128)(2,1)S(1)} %get-tuple-element.25), channel_id=1, source_target_pairs={{0,1},{1,0},{2,3},{3,2},{4,5},{5,4},{6,7},{7,6},{8,9},{9,8},{10,11... | collective-permute-start | bytes 393224 | tf_op jit(solution)/shard_map/ppermute | solution.py:43
  32.8 7.3 %collective-permute-start.17 = (bf16[256,256]{1,0:T(8,128)(2,1)S(1)}, bf16[256,256]{1,0:T(8,128)(2,1)S(1)}, u32[]{:S(2)}, u32[]{:S(2)}) collective-permute-start(bf16[256,256]{1,0:T(8,128)(2,1)S(1)} %get-tuple-element.23.refs_0_), channel_id=1, source_target_pairs={{0,2},{2,6},{6,4},{4,0},{1,3},{3,7},{7,5},{5,1},{8,10},{10,14},{14... | collective-permute-start | bytes 393224 | tf_op jit(solution)/shard_map/ppermute | solution.py:38
  33.2 8.8 %collective-permute-start.14 = (bf16[256,256]{1,0:T(8,128)(2,1)S(1)}, bf16[256,256]{1,0:T(8,128)(2,1)S(1)}, u32[]{:S(2)}, u32[]{:S(2)}) collective-permute-start(bf16[256,256]{1,0:T(8,128)(2,1)S(1)} %get-tuple-element.24.refs_0_), channel_id=1, source_target_pairs={{0,2},{2,6},{6,4},{4,0},{1,3},{3,7},{7,5},{5,1},{8,10},{10,14},{14... | collective-permute-start | bytes 393224 | tf_op jit(solution)/shard_map/ppermute | solution.py:38
  33.6 16.7 %collective-permute-start.5 = (bf16[128,1024]{1,0:T(8,128)(2,1)S(1)}, bf16[128,1024]{1,0:T(8,128)(2,1)S(1)}, u32[]{:S(2)}, u32[]{:S(2)}) collective-permute-start(bf16[128,1024]{1,0:T(8,128)(2,1)S(1)} %collective-permute-done.4.refs_2_), channel_id=1, source_target_pairs={{0,1},{1,0},{2,3},{3,2},{4,5},{5,4},{6,7},{7,6},{8,9},{9,8},{10,11... | collective-permute-start | bytes 786440 | tf_op jit(solution)/shard_map/ppermute | solution.py:43
  33.6 16.7 %collective-permute-start.7 = (bf16[128,1024]{1,0:T(8,128)(2,1)S(1)}, bf16[128,1024]{1,0:T(8,128)(2,1)S(1)}, u32[]{:S(2)}, u32[]{:S(2)}) collective-permute-start(bf16[128,1024]{1,0:T(8,128)(2,1)S(1)} %collective-permute-done.6.refs_4_), channel_id=1, source_target_pairs={{0,1},{1,0},{2,3},{3,2},{4,5},{5,4},{6,7},{7,6},{8,9},{9,8},{10,11... | collective-permute-start | bytes 786440 | tf_op jit(solution)/shard_map/ppermute | solution.py:43
  36.9 13.4 %collective-permute-start.9 = (bf16[128,1024]{1,0:T(8,128)(2,1)S(1)}, bf16[128,1024]{1,0:T(8,128)(2,1)S(1)}, u32[]{:S(2)}, u32[]{:S(2)}) collective-permute-start(bf16[128,1024]{1,0:T(8,128)(2,1)S(1)} %collective-permute-done.8.refs_6_), channel_id=1, source_target_pairs={{0,1},{1,0},{2,3},{3,2},{4,5},{5,4},{6,7},{7,6},{8,9},{9,8},{10,11... | collective-permute-start | bytes 786440 | tf_op jit(solution)/shard_map/ppermute | solution.py:43
  40.1 7.0 %collective-permute-start.18 = (bf16[256,256]{1,0:T(8,128)(2,1)S(1)}, bf16[256,256]{1,0:T(8,128)(2,1)S(1)}, u32[]{:S(2)}, u32[]{:S(2)}) collective-permute-start(bf16[256,256]{1,0:T(8,128)(2,1)S(1)} %collective-permute-done.17.refs_1_), channel_id=1, source_target_pairs={{0,2},{2,6},{6,4},{4,0},{1,3},{3,7},{7,5},{5,1},{8,10},{10,14},{14... | collective-permute-start | bytes 393224 | tf_op jit(solution)/shard_map/ppermute | solution.py:38
  42.1 7.8 %collective-permute-start.15 = (bf16[256,256]{1,0:T(8,128)(2,1)S(1)}, bf16[256,256]{1,0:T(8,128)(2,1)S(1)}, u32[]{:S(2)}, u32[]{:S(2)}) collective-permute-start(bf16[256,256]{1,0:T(8,128)(2,1)S(1)} %collective-permute-done.14.refs_1_), channel_id=1, source_target_pairs={{0,2},{2,6},{6,4},{4,0},{1,3},{3,7},{7,5},{5,1},{8,10},{10,14},{14... | collective-permute-start | bytes 393224 | tf_op jit(solution)/shard_map/ppermute | solution.py:38
  47.1 16.8 %collective-permute-start.19 = (bf16[256,256]{1,0:T(8,128)(2,1)S(1)}, bf16[256,256]{1,0:T(8,128)(2,1)S(1)}, u32[]{:S(2)}, u32[]{:S(2)}) collective-permute-start(bf16[256,256]{1,0:T(8,128)(2,1)S(1)} %collective-permute-done.18.refs_2_), channel_id=1, source_target_pairs={{0,2},{2,6},{6,4},{4,0},{1,3},{3,7},{7,5},{5,1},{8,10},{10,14},{14... | collective-permute-start | bytes 393224 | tf_op jit(solution)/shard_map/ppermute | solution.py:38
  49.9 7.1 %collective-permute-start.16 = (bf16[256,256]{1,0:T(8,128)(2,1)S(1)}, bf16[256,256]{1,0:T(8,128)(2,1)S(1)}, u32[]{:S(2)}, u32[]{:S(2)}) collective-permute-start(bf16[256,256]{1,0:T(8,128)(2,1)S(1)} %collective-permute-done.15.refs_2_), channel_id=1, source_target_pairs={{0,2},{2,6},{6,4},{4,0},{1,3},{3,7},{7,5},{5,1},{8,10},{10,14},{14... | collective-permute-start | bytes 393224 | tf_op jit(solution)/shard_map/ppermute | solution.py:38
  63.7 7.5 %collective-permute-start.20 = (f32[2,128,256]{2,1,0:T(8,128)S(1)}, f32[2,128,256]{2,1,0:T(8,128)S(1)}, u32[]{:S(2)}, u32[]{:S(2)}) collective-permute-start(f32[2,128,256]{2,1,0:T(8,128)S(1)} %get-tuple-element.19), channel_id=1, source_target_pairs={{0,1},{1,0},{2,3},{3,2},{4,5},{5,4},{6,7},{7,6},{8,9},{9,8},{10,11... | collective-permute-start | bytes 786440 | tf_op jit(solution)/shard_map/ppermute | solution.py:43
  70.6 1.7 %collective-permute-start.21 = (f32[2,128,256]{2,1,0:T(8,128)S(1)}, f32[2,128,256]{2,1,0:T(8,128)S(1)}, u32[]{:S(2)}, u32[]{:S(2)}) collective-permute-start(f32[2,128,256]{2,1,0:T(8,128)S(1)} %get-tuple-element.20), channel_id=1, source_target_pairs={{0,1},{1,0},{2,3},{3,2},{4,5},{5,4},{6,7},{7,6},{8,9},{9,8},{10,11... | collective-permute-start | bytes 786440 | tf_op jit(solution)/shard_map/ppermute | solution.py:43

commit v3 on v2

--- a/solution.py
+++ b/solution.py
@@ -37,6 +37,10 @@
     for _ in range(chips - 1):
         pieces.append(lax.ppermute(pieces[-1], "chip", pairs))
     return pieces
+
+
+def after(array, *others):
+    return lax.optimization_barrier((array, *others))[0]
 
 
 def swap_core(array):
@@ -92,8 +96,8 @@
         rounded = gram.astype(jnp.bfloat16)
         high[pl.ds(at, 256), :] = rounded
         low[pl.ds(at, 256), :] = (gram - rounded.astype(jnp.float32)).astype(jnp.bfloat16)
-    wide = rows_t.shape[0] // 4
-    for number in range(2):
+    wide = rows_t.shape[0] // 8
+    for number in range(4):
         start = pl.multiple_of(place[number] * wide, wide)
         rows_t[pl.ds(2 * number * wide, wide), :] = both[:, pl.ds(start, wide)].T
         rows_t[pl.ds((2 * number + 1) * wide, wide), :] = -both[:, pl.ds(width + start, wide)].T
@@ -109,7 +113,7 @@
             square,
             square,
             jax.ShapeDtypeStruct((1, 1), jnp.float32),
-            jax.ShapeDtypeStruct((4 * rows, size), jnp.bfloat16),
+            jax.ShapeDtypeStruct((8 * rows, size), jnp.bfloat16),
         ),
         in_specs=[pl.BlockSpec(memory_space=pltpu.SMEM)] + [pl.BlockSpec(memory_space=pltpu.VMEM)] * len(pieces),
         out_specs=(pl.BlockSpec(memory_space=pltpu.VMEM),) * 4,
@@ -121,7 +125,7 @@
 
 
 def solve_kernel(high, low, damping, rows_t, *refs):
-    pieces, (kept, sent), (start, image, step_high, step_low, step_image) = refs[:-7], refs[-7:-5], refs[-5:]
+    pieces, outs, (start, image, step_high, step_low, step_image) = refs[:-9], refs[-9:-5], refs[-5:]
     size, columns = start.shape
     tiles = [pl.ds(at, 256) for at in range(0, size, 256)]
     count = pieces[0].shape[0]
@@ -164,23 +168,24 @@
         rounded = weight.astype(jnp.bfloat16)
         step_high[tile, :] = rounded
         step_low[tile, :] = (weight - rounded.astype(jnp.float32)).astype(jnp.bfloat16)
-    rows = rows_t.shape[0] // 4
-    for number, out in enumerate((kept, sent)):
+    rows = rows_t.shape[0] // 8
+    for number, out in enumerate(outs):
         for part in range(2):
             left = rows_t[pl.ds((2 * number + part) * rows, rows), :]
-            out[part] = dot(left, step_high[...]) + dot(left, step_low[...])
+            out[part] = (dot(left, step_high[...]) + dot(left, step_low[...])).astype(out.dtype)
 
 
 def solve_call(high, low, damping, rows_t, pieces):
     size = high.shape[0]
     columns = pieces[0].shape[1]
-    rows = rows_t.shape[0] // 4
+    rows = rows_t.shape[0] // 8
     block = jax.ShapeDtypeStruct((2, rows, columns), jnp.float32)
+    rounded = jax.ShapeDtypeStruct((2, rows, columns), jnp.bfloat16)
     return pl.pallas_call(
         solve_kernel,
-        out_shape=(block, block),
+        out_shape=(block, block, rounded, rounded),
         in_specs=[pl.BlockSpec(memory_space=pltpu.VMEM)] * (4 + len(pieces)),
-        out_specs=(pl.BlockSpec(memory_space=pltpu.VMEM),) * 2,
+        out_specs=(pl.BlockSpec(memory_space=pltpu.VMEM),) * 4,
         scratch_shapes=[
             pltpu.VMEM((size, columns), jnp.bfloat16),
             pltpu.VMEM((size, columns), jnp.float32),
@@ -236,13 +241,12 @@
     return block[0], block[1]
 
 
-def shards(up_traces, down_traces):
+def ring_shards(up_traces, down_traces):
     local_shots, samples, width = up_traces.shape
     nfreq, chips = lax.axis_size("freq"), lax.axis_size("chip")
     core = lax.axis_index("core")
     half = width // 2
     rows = width // (2 * chips)
-    size = 2 * local_shots * nfreq * 2 * chips
     matrix = jnp.asarray(spread_table(samples, nfreq, local_shots))
 
     down = to_freq(spectra(down_traces, matrix), nfreq)
@@ -257,13 +261,11 @@
     up = jnp.concatenate([mine, theirs], 0)
 
     place = 2 * lax.axis_index("chip") + jnp.stack([core, 1 - core]).astype(jnp.int32)
-    small = size <= 1024 and rows % 128 == 0 and half % CHUNK == 0 and local_shots % 16 == 0
-    gram, solve = (gram_call, solve_call) if small else (plain_gram, plain_solve)
-    operator = gram(place, pieces, local_shots, rows)
+    operator = plain_gram(place, pieces, local_shots, rows)
     chunk = CHUNK if half % CHUNK == 0 else half
     kept, got = [], []
     for at in range(0, half, chunk):
-        stay, send = solve(*operator, ring_gather(up[:, at : at + chunk], chips))
+        stay, send = plain_solve(*operator, ring_gather(up[:, at : at + chunk], chips))
         kept.append(stay)
         got.append(swap_core(send))
     kept, got = jnp.concatenate(kept, 2), jnp.concatenate(got, 2)
@@ -272,9 +274,123 @@
     return jnp.transpose(block, (1, 0, 2))[None]
 
 
+def spectra_kernel(steps, down_traces, up_traces, matrix, *refs):
+    outs, (traces, turned, arrived) = refs[:steps], refs[steps:]
+    me = lax.axis_index("freq")
+    depth = traces.shape[2]
+    copies = []
+    for side, source in enumerate((down_traces, up_traces)):
+        for part in range(traces.shape[1]):
+            copy = pltpu.make_async_copy(
+                source.at[pl.ds(part * depth, depth)], traces.at[side, part], arrived.at[side, part]
+            )
+            copy.start()
+            copies.append(copy)
+    for step in range(steps):
+        turned[step] = matrix[me ^ step]
+    rows = turned.shape[1]
+    for side in range(2):
+        total = None
+        for part in range(traces.shape[1]):
+            copies[side * traces.shape[1] + part].wait()
+            left = turned[:, :, pl.ds(part * depth, depth)].reshape(steps * rows, depth)
+            value = dot(left, traces[side, part])
+            total = value if total is None else total + value
+        total = total.astype(jnp.bfloat16)
+        for step, out in enumerate(outs):
+            out[pl.ds(side * rows, rows), :] = total[step * rows : (step + 1) * rows]
+
+
+def spectra_call(down_traces, up_traces, matrix):
+    steps, rows, depth = matrix.shape
+    width = down_traces.shape[2]
+    parts = 4
+    return pl.pallas_call(
+        functools.partial(spectra_kernel, steps),
+        out_shape=(jax.ShapeDtypeStruct((2 * rows, width), jnp.bfloat16),) * steps,
+        in_specs=[pl.BlockSpec(memory_space=pl.ANY)] * 2 + [pl.BlockSpec(memory_space=pltpu.VMEM)],
+        out_specs=(pl.BlockSpec(memory_space=pltpu.VMEM),) * steps,
+        scratch_shapes=[
+            pltpu.VMEM((2, parts, depth // parts, width), jnp.bfloat16),
+            pltpu.VMEM((steps, rows, depth), jnp.bfloat16),
+            pltpu.SemaphoreType.DMA((2, parts)),
+        ],
+        compiler_params=pltpu.CompilerParams(vmem_limit_bytes=LIMIT),
+        cost_estimate=pl.CostEstimate(
+            flops=4 * steps * rows * depth * width, bytes_accessed=4 * depth * width, transcendentals=0
+        ),
+        name="spectra",
+    )(down_traces.reshape(-1, width), up_traces.reshape(-1, width), matrix)
+
+
+def line_shards(up_traces, down_traces):
+    local_shots, samples, width = up_traces.shape
+    nfreq = lax.axis_size("freq")
+    core, chip = lax.axis_index("core"), lax.axis_index("chip")
+    half = width // 2
+    rows = width // 8
+    group = 2 * local_shots
+    matrix = jnp.asarray(spread_table(samples, nfreq, local_shots)).reshape(nfreq, group, -1)
+
+    parts = spectra_call(down_traces, up_traces, matrix)
+    parts = [parts[0]] + [
+        lax.ppermute(parts[step], "freq", [(f, f ^ step) for f in range(nfreq)]) for step in range(1, nfreq)
+    ]
+    down = jnp.concatenate([part[:group] for part in parts], 0)
+    up = jnp.concatenate([part[group:] for part in parts], 0)
+
+    def inwards(array):
+        return lax.ppermute(array, "chip", [(0, 1), (3, 2)])
+
+    def across(array):
+        return lax.ppermute(array, "chip", [(1, 2), (2, 1)])
+
+    def outwards(array, turn):
+        pairs = [(2 * hub + c, 2 * end + (c ^ turn)) for hub, end in ((1, 0), (2, 3)) for c in range(2)]
+        return lax.ppermute(array, ("chip", "core"), pairs)
+
+    mine = lax.dynamic_slice_in_dim(up, core * half, half, 1)
+    theirs = swap_core(lax.dynamic_slice_in_dim(up, (1 - core) * half, half, 1))
+    up = jnp.concatenate([mine, theirs], 0)
+    chunks = [up[:, at : at + CHUNK] for at in range(0, half, CHUNK)]
+
+    outer = inwards(down)
+    inner = across(down)
+    first_outer = inwards(chunks[0])
+    first_inner = across(chunks[0])
+    far = across(outer)
+    gathered = [[chunks[0], first_outer, first_inner, across(after(first_outer, far))]]
+    for chunk in chunks[1:]:
+        chunk = after(chunk, outer)
+        chunk_outer = inwards(chunk)
+        gathered.append([chunk, chunk_outer, across(chunk), across(after(chunk_outer, gathered[-1][-1]))])
+
+    pieces = []
+    for piece in (down, outer, inner, far):
+        pieces += [piece, swap_core(piece)]
+    end = jnp.where(chip < 2, 0, 3)
+    place = jnp.stack([2 * chip + core, 2 * chip + 1 - core, 2 * end + core, 2 * end + 1 - core]).astype(jnp.int32)
+    operator = gram_call(place, pieces, local_shots, rows)
+    is_end = (chip == 0) | (chip == 3)
+    own, other = [], []
+    for chunk in gathered:
+        kept, sent, outside, crossed = solve_call(*operator, chunk)
+        own.append(jnp.where(is_end, outwards(outside, 0).astype(jnp.float32), kept))
+        other.append(jnp.where(is_end, outwards(crossed, 1).astype(jnp.float32), swap_core(sent)))
+    own, other = jnp.concatenate(own, 2), jnp.concatenate(other, 2)
+    block = jnp.where(core == 0, jnp.concatenate([own, other], 2), jnp.concatenate([other, own], 2))
+    return jnp.transpose(block, (1, 0, 2))[None]
+
+
 def solution(mesh):
     nfreq, nshot = mesh.devices.shape
     fine = Mesh(mesh.devices.reshape(nfreq, nshot // 2, 2), ("freq", "chip", "core"))
     spec = P(("freq", "chip", "core"), None, None)
     out_specs = P("freq", ("chip", "core"), None, None)
+
+    def shards(up_traces, down_traces):
+        shots, _, width = up_traces.shape
+        line = nshot == 8 and nfreq == 4 and shots == 16 and width % (2 * CHUNK) == 0
+        return (line_shards if line else ring_shards)(up_traces, down_traces)
+
     return jax.shard_map(shards, mesh=fine, in_specs=(spec, spec), out_specs=out_specs, check_vma=False)

time: 74.6 us -> 93.1 us (1.25)
  starting transfers between devices: 21 us -> 27.7 us
  waiting for transfers between devices: 26.7 us -> 32.9 us
  local copies, waits for them, and re-layouts: 1.94 us -> 6.66 us
  Pallas kernels: 20.2 us -> 24.5 us
  matrix products: 3.95 us -> 0 us
    ppermute x15 -> x16, waiting for transfers between devices: 24.3 us -> 32.9 us  [the longest x4 20 us: outwards(): return lax.ppermute(array, ('chip', 'core'), pairs)]
    ppermute x15 -> x16, starting transfers between devices: 19.8 us -> 25.9 us  [the longest x3 12 us: inwards(): return lax.ppermute(array, 'chip', [(0, 1), (3, 2)])]
    unnamed x6, local copies, waits for them, and re-layouts: 0.05 us -> 4.82 us
    dot_general x2 -> x0, matrix products: 3.95 us -> none  [dot(): return jnp.dot(left, right, preferred_element_type=jnp.float32)]
    pallas_call x2 -> x3, Pallas kernels: 13.6 us -> 17.2 us  [the longest x2 14.4 us: solve_call(): pl.pallas_call(solve_kernel, out_shape=(block, block, rounded, rounded),...]
    ppermute x7, waiting for transfers between devices: 2.4 us -> 0.02 us  [swap_core(): return lax.ppermute(array, 'core', [(0, 1), (1, 0)])]
  transfers between devices with their start and end apart: 22 -> 23, of which waited for: 14 -> 8; matrix products, arithmetic and copies ran while one was open for 1% -> 0% of each run, Pallas kernels for 27% -> 23%
where the time goes in v3:
time: 93.1 us; the launch traced here: 92.6 us
  waiting for transfers between devices  32.9 us (35%)
  starting transfers between devices  27.7 us (30%)
  Pallas kernels  24.5 us (26%)
  local copies, waits for them, and re-layouts  6.66 us (7%)
    ppermute x4, waiting for transfers between devices, outwards(): return lax.ppermute(array, ('chip', 'core'), pairs)  20 us
    pallas_call x2, Pallas kernels, solve_call(): pl.pallas_call(solve_kernel, out_shape=(block, block, rounded, rounded),...  14.4 us
    ppermute x3, starting transfers between devices, inwards(): return lax.ppermute(array, 'chip', [(0, 1), (3, 2)])  12 us
    pallas_call x1, Pallas kernels, gram_call(): pl.pallas_call(functools.partial(gram_kernel, shots), out_shape=(square,...  7.34 us
    ppermute x3, waiting for transfers between devices, inwards(): return lax.ppermute(array, 'chip', [(0, 1), (3, 2)])  7.01 us
    ppermute x3, waiting for transfers between devices, line_shards(): lax.ppermute(parts[step], 'freq', [(f, f ^ step) for f in range(nfreq)])  5.87 us
    ppermute x4, starting transfers between devices, outwards(): return lax.ppermute(array, ('chip', 'core'), pairs)  5.33 us
    unnamed x6, local copies, waits for them, and re-layouts  4.82 us
  transfers between devices with their start and end apart: 23, of which 8 were waited for; matrix products, arithmetic and copies ran while one was open for 0% of the time, Pallas kernels for 23%

profile of v3, /device:TPU:0, one launch (start us, length us, event | category | flops | bytes accessed | tf_op | source)
XLA Modules:
  0.0 92.6 jit_solution(6235731103950277180)
XLA Ops:
  0.0 0.0 copy-start
  0.0 2.2 %copy-done = bf16[16,128,1024]{2,1,0:T(8,128)(2,1)S(1)} copy-done((bf16[16,128,1024]{2,1,0:T(8,128)(2,1)S(1)}, bf16[16,128,1024]{2,1,0:T(8,128)(2,1)}, u32[]{:S(2)}) %copy-start) | copy-done | bytes 4194328
  2.2 0.0 copy-start.1
  2.2 1.0 %copy-done.1 = bf16[4,32,2048]{2,1,0:T(8,128)(2,1)S(1)} copy-done((bf16[4,32,2048]{2,1,0:T(8,128)(2,1)S(1)}, bf16[4,32,2048]{2,1,0:T(8,128)(2,1)}, u32[]{:S(2)}) %copy-start.1) | copy-done | bytes 524312
  3.2 2.8 %spectra.1 = (bf16[64,1024]{1,0:T(8,128)(2,1)S(1)}, bf16[64,1024]{1,0:T(8,128)(2,1)S(1)}, bf16[64,1024]{1,0:T(8,128)(2,1)S(1)}, bf16[64,1024]{1,0:T(8,128)(2,1)S(1)}) custom-call(bf16[2048,1024]{1,0:T(8,128)(2,1)S(1)} %bitcast.10, bf16[2048,1024]{1,0:T(8,128)(2,1)} %bitcast.11, bf16[4,32,2048]{2,1,0:T(8,128)(2,1)S(1)} %copy-done.1), custom_call_target="tpu_custom_call" | custom-call | flops 1073741824 | bytes 8388608 | tf_op jit(solution)/shard_map/spectra/pallas_call | solution.py:308
  6.1 4.0 %collective-permute-start.2 = (bf16[64,1024]{1,0:T(8,128)(2,1)S(1)}, bf16[64,1024]{1,0:T(8,128)(2,1)S(1)}, u32[]{:S(2)}, u32[]{:S(2)}) collective-permute-start(bf16[64,1024]{1,0:T(8,128)(2,1)S(1)} %get-tuple-element.27), channel_id=1, source_target_pairs={{0,24},{8,16},{16,8},{24,0},{1,25},{9,17},{17,9},{25,1},{2,26},{10... | collective-permute-start | bytes 393224 | tf_op jit(solution)/shard_map/ppermute | solution.py:337
  10.0 0.5 collective-permute-start.1
  10.5 0.1 collective-permute-start
  10.7 3.2 %collective-permute-done.2 = bf16[64,1024]{1,0:T(8,128)(2,1)S(1)} collective-permute-done((bf16[64,1024]{1,0:T(8,128)(2,1)S(1)}, bf16[64,1024]{1,0:T(8,128)(2,1)S(1)}, u32[]{:S(2)}, u32[]{:S(2)}) %collective-permute-start.2) | collective-permute-done | bytes 131104 | tf_op jit(solution)/shard_map/ppermute | solution.py:337
  13.9 2.4 %collective-permute-done.1 = bf16[64,1024]{1,0:T(8,128)(2,1)S(1)} collective-permute-done((bf16[64,1024]{1,0:T(8,128)(2,1)S(1)}, bf16[64,1024]{1,0:T(8,128)(2,1)S(1)}, u32[]{:S(2)}, u32[]{:S(2)}) %collective-permute-start.1) | collective-permute-done | bytes 131104 | tf_op jit(solution)/shard_map/ppermute | solution.py:337
  16.4 0.2 collective-permute-done
  16.6 3.5 %collective-permute-start.4 = (bf16[128,1024]{1,0:T(8,128)(2,1)S(1)}, bf16[128,1024]{1,0:T(8,128)(2,1)S(1)}, u32[]{:S(2)}, u32[]{:S(2)}) collective-permute-start(bf16[128,1024]{1,0:T(8,128)(2,1)S(1)} %pad_maximum_fusion.refs_0_), channel_id=1, source_target_pairs={{0,2},{6,4},{1,3},{7,5},{8,10},{14,12},{9,11},{15,13},{16,18},{22,... | collective-permute-start | bytes 786440 | tf_op jit(solution)/shard_map/ppermute | solution.py:343
  20.2 0.1 collective-permute-start.10
  20.3 0.7 collective-permute-start.6
  21.0 4.9 %collective-permute-done.4.refs_2_ = bf16[128,1024]{1,0:T(8,128)(2,1)S(1)} collective-permute-done((bf16[128,1024]{1,0:T(8,128)(2,1)S(1)}, bf16[128,1024]{1,0:T(8,128)(2,1)S(1)}, u32[]{:S(2)}, u32[]{:S(2)}) %collective-permute-start.4) | collective-permute-done | bytes 262176 | tf_op jit(solution)/shard_map/ppermute | solution.py:343
  25.8 0.7 collective-permute-start.8
  26.5 0.0 collective-permute-done.10
  26.5 7.2 %collective-permute-start.11 = (bf16[256,256]{1,0:T(8,128)(2,1)S(1)}, bf16[256,256]{1,0:T(8,128)(2,1)S(1)}, u32[]{:S(2)}, u32[]{:S(2)}) collective-permute-start(bf16[256,256]{1,0:T(8,128)(2,1)S(1)} %get-tuple-element.43.refs_0_), channel_id=1, source_target_pairs={{0,2},{6,4},{1,3},{7,5},{8,10},{14,12},{9,11},{15,13},{16,18},{22,... | collective-permute-start | bytes 393224 | tf_op jit(solution)/shard_map/ppermute | solution.py:343
  33.7 1.3 %collective-permute-start.15 = (bf16[256,256]{1,0:T(8,128)(2,1)S(1)}, bf16[256,256]{1,0:T(8,128)(2,1)S(1)}, u32[]{:S(2)}, u32[]{:S(2)}) collective-permute-start(bf16[256,256]{1,0:T(8,128)(2,1)S(1)} %get-tuple-element.35.refs_0_), channel_id=1, source_target_pairs={{0,2},{6,4},{1,3},{7,5},{8,10},{14,12},{9,11},{15,13},{16,18},{22,... | collective-permute-start | bytes 393224 | tf_op jit(solution)/shard_map/ppermute | solution.py:343
  35.0 0.1 collective-permute-start.3
  35.1 0.0 collective-permute-done.6.refs_4_
  35.1 0.5 collective-permute-start.5
  35.6 1.3 %collective-permute-done.11.refs_1_ = bf16[256,256]{1,0:T(8,128)(2,1)S(1)} collective-permute-done((bf16[256,256]{1,0:T(8,128)(2,1)S(1)}, bf16[256,256]{1,0:T(8,128)(2,1)S(1)}, u32[]{:S(2)}, u32[]{:S(2)}) %collective-permute-start.11) | collective-permute-done | bytes 131104 | tf_op jit(solution)/shard_map/ppermute | solution.py:343
  36.9 0.0 collective-permute-start.7
  36.9 0.0 collective-permute-done.8.refs_6_
  36.9 0.5 collective-permute-start.9
  37.4 0.9 collective-permute-done.15.refs_1_
  38.3 0.7 collective-permute-start.13
  39.0 0.1 pad_add_fusion.place
  39.1 0.0 collective-permute-done.13.refs_3_
  39.1 0.7 collective-permute-start.12
  39.7 0.0 collective-permute-done.3.refs_1_
  39.7 0.7 collective-permute-start.16
  40.4 0.0 collective-permute-done.5.refs_3_
  40.4 0.7 collective-permute-start.17
  41.1 0.0 collective-permute-done.7.refs_5_
  41.1 0.0 collective-permute-done.9.refs_7_
  41.1 7.3 %gram.1 = (bf16[1024,1024]{1,0:T(8,128)(2,1)S(1)}, bf16[1024,1024]{1,0:T(8,128)(2,1)}, f32[1,1]{1,0:T(1,128)}, bf16[1024,1024]{1,0:T(8,128)(2,1)}) custom-call(s32[4]{0:T(128)S(1)} %pad_add_fusion.place, bf16[128,1024]{1,0:T(8,128)(2,1)S(1)} %pad_maximum_fusion.refs_0_, bf16[128,1024]{1,0:T(8,128)(2,1)S(1)} %collective-permute-done.3.refs_1_, ...), custom_call_target="tpu_custom_call" | custom-call | flops 4294967296 | bytes 4194304 | tf_op jit(solution)/shard_map/gram/pallas_call | solution.py:110
  48.5 0.0 collective-permute-done.16.refs_2_
  48.5 0.0 collective-permute-done.17.refs_3_
  48.5 0.0 copy-start.2
  48.5 1.6 %copy-done.2 = bf16[1024,1024]{1,0:T(8,128)(2,1)S(1)} copy-done((bf16[1024,1024]{1,0:T(8,128)(2,1)S(1)}, bf16[1024,1024]{1,0:T(8,128)(2,1)}, u32[]{:S(2)}) %copy-start.2) | copy-done | bytes 2097176
  50.1 7.2 %solve.3 = (f32[2,128,256]{2,1,0:T(8,128)S(1)}, f32[2,128,256]{2,1,0:T(8,128)S(1)}, bf16[2,128,256]{2,1,0:T(8,128)(2,1)S(1)}, bf16[2,128,256]{2,1,0:T(8,128)(2,1)S(1)}) custom-call(bf16[1024,1024]{1,0:T(8,128)(2,1)S(1)} %get-tuple-element.28.high, bf16[1024,1024]{1,0:T(8,128)(2,1)S(1)} %copy-done.2, f32[1,1]{1,0:T(1,128)} %get-tuple-element.30.damping, ...), custom_call_target="tpu_custom_call" | custom-call | flops 3221225472 | bytes 4194304 | tf_op jit(solution)/shard_map/solve/pallas_call | solution.py:184
  57.3 0.1 collective-permute-start.22
  57.3 1.3 %collective-permute-start.21 = (bf16[2,128,256]{2,1,0:T(8,128)(2,1)S(1)}, bf16[2,128,256]{2,1,0:T(8,128)(2,1)S(1)}, u32[]{:S(2)}, u32[]{:S(2)}) collective-permute-start(bf16[2,128,256]{2,1,0:T(8,128)(2,1)S(1)} %get-tuple-element.41), channel_id=1, source_target_pairs={{2,1},{3,0},{4,7},{5,6},{10,9},{11,8},{12,15},{13,14},{18,17},{19,... | collective-permute-start | bytes 393224 | tf_op jit(solution)/shard_map/ppermute | solution.py:350
  58.6 1.5 %collective-permute-start.18 = (bf16[2,128,256]{2,1,0:T(8,128)(2,1)S(1)}, bf16[2,128,256]{2,1,0:T(8,128)(2,1)S(1)}, u32[]{:S(2)}, u32[]{:S(2)}) collective-permute-start(bf16[2,128,256]{2,1,0:T(8,128)(2,1)S(1)} %get-tuple-element.37), channel_id=1, source_target_pairs={{2,0},{3,1},{4,6},{5,7},{10,8},{11,9},{12,14},{13,15},{18,16},{19,... | collective-permute-start | bytes 393224 | tf_op jit(solution)/shard_map/ppermute | solution.py:350
  60.1 0.0 collective-permute-done.12.refs_2_
  60.1 7.2 %solve.2 = (f32[2,128,256]{2,1,0:T(8,128)S(1)}, f32[2,128,256]{2,1,0:T(8,128)S(1)}, bf16[2,128,256]{2,1,0:T(8,128)(2,1)S(1)}, bf16[2,128,256]{2,1,0:T(8,128)(2,1)S(1)}) custom-call(bf16[1024,1024]{1,0:T(8,128)(2,1)S(1)} %get-tuple-element.28.high, bf16[1024,1024]{1,0:T(8,128)(2,1)S(1)} %copy-done.2, f32[1,1]{1,0:T(1,128)} %get-tuple-element.30.damping, ...), custom_call_target="tpu_custom_call" | custom-call | flops 3221225472 | bytes 4194304 | tf_op jit(solution)/shard_map/solve/pallas_call | solution.py:184
  67.3 0.6 collective-permute-start.20
  67.9 1.3 %collective-permute-start.19 = (bf16[2,128,256]{2,1,0:T(8,128)(2,1)S(1)}, bf16[2,128,256]{2,1,0:T(8,128)(2,1)S(1)}, u32[]{:S(2)}, u32[]{:S(2)}) collective-permute-start(bf16[2,128,256]{2,1,0:T(8,128)(2,1)S(1)} %get-tuple-element.39), channel_id=1, source_target_pairs={{2,1},{3,0},{4,7},{5,6},{10,9},{11,8},{12,15},{13,14},{18,17},{19,... | collective-permute-start | bytes 393224 | tf_op jit(solution)/shard_map/ppermute | solution.py:350
  69.2 11.2 %collective-permute-done.18 = bf16[2,128,256]{2,1,0:T(8,128)(2,1)S(1)} collective-permute-done((bf16[2,128,256]{2,1,0:T(8,128)(2,1)S(1)}, bf16[2,128,256]{2,1,0:T(8,128)(2,1)S(1)}, u32[]{:S(2)}, u32[]{:S(2)}) %collective-permute-start.18) | collective-permute-done | bytes 131104 | tf_op jit(solution)/shard_map/ppermute | solution.py:350
  80.4 1.3 %collective-permute-start.14 = (bf16[2,128,256]{2,1,0:T(8,128)(2,1)S(1)}, bf16[2,128,256]{2,1,0:T(8,128)(2,1)S(1)}, u32[]{:S(2)}, u32[]{:S(2)}) collective-permute-start(bf16[2,128,256]{2,1,0:T(8,128)(2,1)S(1)} %get-tuple-element.33), channel_id=1, source_target_pairs={{2,0},{3,1},{4,6},{5,7},{10,8},{11,9},{12,14},{13,15},{18,16},{19,... | collective-permute-start | bytes 393224 | tf_op jit(solution)/shard_map/ppermute | solution.py:350
  81.7 8.8 %collective-permute-done.14 = bf16[2,128,256]{2,1,0:T(8,128)(2,1)S(1)} collective-permute-done((bf16[2,128,256]{2,1,0:T(8,128)(2,1)S(1)}, bf16[2,128,256]{2,1,0:T(8,128)(2,1)S(1)}, u32[]{:S(2)}, u32[]{:S(2)}) %collective-permute-start.14) | collective-permute-done | bytes 131104 | tf_op jit(solution)/shard_map/ppermute | solution.py:350
  90.5 0.0 collective-permute-done.21
  90.5 0.0 collective-permute-done.22
  90.6 0.0 collective-permute-done.19
  90.6 0.0 collective-permute-done.20
  90.6 0.2 fusion
  90.8 1.8 %copy.4 = f32[1,128,2,1024]{3,2,1,0:T(2,128)} copy(f32[1,128,2,1024]{3,1,2,0:T(8,128)S(1)} %fusion) | data formatting | bytes 2097152 | tf_op jit(solution)/shard_map/broadcast_in_dim | solution.py:382
  (12 shorter events, 0.2 us)
Async XLA Ops:
  0.0 2.2 %copy-start = (bf16[16,128,1024]{2,1,0:T(8,128)(2,1)S(1)}, bf16[16,128,1024]{2,1,0:T(8,128)(2,1)}, u32[]{:S(2)}) copy-start(bf16[16,128,1024]{2,1,0:T(8,128)(2,1)} %param.4) | copy-start | bytes 12582916
  2.2 1.0 %copy-start.1 = (bf16[4,32,2048]{2,1,0:T(8,128)(2,1)S(1)}, bf16[4,32,2048]{2,1,0:T(8,128)(2,1)}, u32[]{:S(2)}) copy-start(bf16[4,32,2048]{2,1,0:T(8,128)(2,1)} %constant.25.matrix) | copy-start | bytes 1572868
  6.1 7.9 %collective-permute-start.2 = (bf16[64,1024]{1,0:T(8,128)(2,1)S(1)}, bf16[64,1024]{1,0:T(8,128)(2,1)S(1)}, u32[]{:S(2)}, u32[]{:S(2)}) collective-permute-start(bf16[64,1024]{1,0:T(8,128)(2,1)S(1)} %get-tuple-element.27), channel_id=1, source_target_pairs={{0,24},{8,16},{16,8},{24,0},{1,25},{9,17},{17,9},{25,1},{2,26},{10... | collective-permute-start | bytes 393224 | tf_op jit(solution)/shard_map/ppermute | solution.py:337
  10.0 6.3 %collective-permute-start.1 = (bf16[64,1024]{1,0:T(8,128)(2,1)S(1)}, bf16[64,1024]{1,0:T(8,128)(2,1)S(1)}, u32[]{:S(2)}, u32[]{:S(2)}) collective-permute-start(bf16[64,1024]{1,0:T(8,128)(2,1)S(1)} %get-tuple-element.26), channel_id=1, source_target_pairs={{0,16},{8,24},{16,0},{24,8},{1,17},{9,25},{17,1},{25,9},{2,18},{10... | collective-permute-start | bytes 393224 | tf_op jit(solution)/shard_map/ppermute | solution.py:337
  10.5 6.0 %collective-permute-start = (bf16[64,1024]{1,0:T(8,128)(2,1)S(1)}, bf16[64,1024]{1,0:T(8,128)(2,1)S(1)}, u32[]{:S(2)}, u32[]{:S(2)}) collective-permute-start(bf16[64,1024]{1,0:T(8,128)(2,1)S(1)} %get-tuple-element.25), channel_id=1, source_target_pairs={{0,8},{8,0},{16,24},{24,16},{1,9},{9,1},{17,25},{25,17},{2,10},{10... | collective-permute-start | bytes 393224 | tf_op jit(solution)/shard_map/ppermute | solution.py:337
  16.6 9.2 %collective-permute-start.4 = (bf16[128,1024]{1,0:T(8,128)(2,1)S(1)}, bf16[128,1024]{1,0:T(8,128)(2,1)S(1)}, u32[]{:S(2)}, u32[]{:S(2)}) collective-permute-start(bf16[128,1024]{1,0:T(8,128)(2,1)S(1)} %pad_maximum_fusion.refs_0_), channel_id=1, source_target_pairs={{0,2},{6,4},{1,3},{7,5},{8,10},{14,12},{9,11},{15,13},{16,18},{22,... | collective-permute-start | bytes 786440 | tf_op jit(solution)/shard_map/ppermute | solution.py:343
  20.2 6.3 %collective-permute-start.10 = (bf16[128,512]{1,0:T(8,128)(2,1)S(1)}, bf16[128,512]{1,0:T(8,128)(2,1)S(1)}, u32[]{:S(2)}, u32[]{:S(2)}) collective-permute-start(bf16[128,512]{1,0:T(8,128)(2,1)S(1)} %get-tuple-element.46), channel_id=1, source_target_pairs={{0,1},{1,0},{2,3},{3,2},{4,5},{5,4},{6,7},{7,6},{8,9},{9,8},{10,11... | collective-permute-start | bytes 393224 | tf_op jit(solution)/shard_map/ppermute | solution.py:47
  20.3 14.8 %collective-permute-start.6 = (bf16[128,1024]{1,0:T(8,128)(2,1)S(1)}, bf16[128,1024]{1,0:T(8,128)(2,1)S(1)}, u32[]{:S(2)}, u32[]{:S(2)}) collective-permute-start(bf16[128,1024]{1,0:T(8,128)(2,1)S(1)} %pad_maximum_fusion.refs_0_), channel_id=1, source_target_pairs={{2,4},{4,2},{3,5},{5,3},{10,12},{12,10},{11,13},{13,11},{18,20},{2... | collective-permute-start | bytes 786440 | tf_op jit(solution)/shard_map/ppermute | solution.py:346
  25.8 11.1 %collective-permute-start.8 = (bf16[128,1024]{1,0:T(8,128)(2,1)S(1)}, bf16[128,1024]{1,0:T(8,128)(2,1)S(1)}, u32[]{:S(2)}, u32[]{:S(2)}) collective-permute-start(bf16[128,1024]{1,0:T(8,128)(2,1)S(1)} %collective-permute-done.4.refs_2_), channel_id=1, source_target_pairs={{2,4},{4,2},{3,5},{5,3},{10,12},{12,10},{11,13},{13,11},{18,20},{2... | collective-permute-start | bytes 786440 | tf_op jit(solution)/shard_map/ppermute | solution.py:346
  26.5 10.4 %collective-permute-start.11 = (bf16[256,256]{1,0:T(8,128)(2,1)S(1)}, bf16[256,256]{1,0:T(8,128)(2,1)S(1)}, u32[]{:S(2)}, u32[]{:S(2)}) collective-permute-start(bf16[256,256]{1,0:T(8,128)(2,1)S(1)} %get-tuple-element.43.refs_0_), channel_id=1, source_target_pairs={{0,2},{6,4},{1,3},{7,5},{8,10},{14,12},{9,11},{15,13},{16,18},{22,... | collective-permute-start | bytes 393224 | tf_op jit(solution)/shard_map/ppermute | solution.py:343
  33.7 4.6 %collective-permute-start.15 = (bf16[256,256]{1,0:T(8,128)(2,1)S(1)}, bf16[256,256]{1,0:T(8,128)(2,1)S(1)}, u32[]{:S(2)}, u32[]{:S(2)}) collective-permute-start(bf16[256,256]{1,0:T(8,128)(2,1)S(1)} %get-tuple-element.35.refs_0_), channel_id=1, source_target_pairs={{0,2},{6,4},{1,3},{7,5},{8,10},{14,12},{9,11},{15,13},{16,18},{22,... | collective-permute-start | bytes 393224 | tf_op jit(solution)/shard_map/ppermute | solution.py:343
  35.0 4.7 %collective-permute-start.3 = (bf16[128,1024]{1,0:T(8,128)(2,1)S(1)}, bf16[128,1024]{1,0:T(8,128)(2,1)S(1)}, u32[]{:S(2)}, u32[]{:S(2)}) collective-permute-start(bf16[128,1024]{1,0:T(8,128)(2,1)S(1)} %pad_maximum_fusion.refs_0_), channel_id=1, source_target_pairs={{0,1},{1,0},{2,3},{3,2},{4,5},{5,4},{6,7},{7,6},{8,9},{9,8},{10,11... | collective-permute-start | bytes 786440 | tf_op jit(solution)/shard_map/ppermute | solution.py:47
  35.1 5.3 %collective-permute-start.5 = (bf16[128,1024]{1,0:T(8,128)(2,1)S(1)}, bf16[128,1024]{1,0:T(8,128)(2,1)S(1)}, u32[]{:S(2)}, u32[]{:S(2)}) collective-permute-start(bf16[128,1024]{1,0:T(8,128)(2,1)S(1)} %collective-permute-done.4.refs_2_), channel_id=1, source_target_pairs={{0,1},{1,0},{2,3},{3,2},{4,5},{5,4},{6,7},{7,6},{8,9},{9,8},{10,11... | collective-permute-start | bytes 786440 | tf_op jit(solution)/shard_map/ppermute | solution.py:47
  36.9 4.2 %collective-permute-start.7 = (bf16[128,1024]{1,0:T(8,128)(2,1)S(1)}, bf16[128,1024]{1,0:T(8,128)(2,1)S(1)}, u32[]{:S(2)}, u32[]{:S(2)}) collective-permute-start(bf16[128,1024]{1,0:T(8,128)(2,1)S(1)} %collective-permute-done.6.refs_4_), channel_id=1, source_target_pairs={{0,1},{1,0},{2,3},{3,2},{4,5},{5,4},{6,7},{7,6},{8,9},{9,8},{10,11... | collective-permute-start | bytes 786440 | tf_op jit(solution)/shard_map/ppermute | solution.py:47
  36.9 4.2 %collective-permute-start.9 = (bf16[128,1024]{1,0:T(8,128)(2,1)S(1)}, bf16[128,1024]{1,0:T(8,128)(2,1)S(1)}, u32[]{:S(2)}, u32[]{:S(2)}) collective-permute-start(bf16[128,1024]{1,0:T(8,128)(2,1)S(1)} %collective-permute-done.8.refs_6_), channel_id=1, source_target_pairs={{0,1},{1,0},{2,3},{3,2},{4,5},{5,4},{6,7},{7,6},{8,9},{9,8},{10,11... | collective-permute-start | bytes 786440 | tf_op jit(solution)/shard_map/ppermute | solution.py:47
  38.3 0.8 collective-permute-start.13
  39.1 21.1 %collective-permute-start.12 = (bf16[256,256]{1,0:T(8,128)(2,1)S(1)}, bf16[256,256]{1,0:T(8,128)(2,1)S(1)}, u32[]{:S(2)}, u32[]{:S(2)}) collective-permute-start(bf16[256,256]{1,0:T(8,128)(2,1)S(1)} %get-tuple-element.43.refs_0_), channel_id=1, source_target_pairs={{2,4},{4,2},{3,5},{5,3},{10,12},{12,10},{11,13},{13,11},{18,20},{2... | collective-permute-start | bytes 393224 | tf_op jit(solution)/shard_map/ppermute | solution.py:346
  39.7 8.7 %collective-permute-start.16 = (bf16[256,256]{1,0:T(8,128)(2,1)S(1)}, bf16[256,256]{1,0:T(8,128)(2,1)S(1)}, u32[]{:S(2)}, u32[]{:S(2)}) collective-permute-start(bf16[256,256]{1,0:T(8,128)(2,1)S(1)} %get-tuple-element.35.refs_0_), channel_id=1, source_target_pairs={{2,4},{4,2},{3,5},{5,3},{10,12},{12,10},{11,13},{13,11},{18,20},{2... | collective-permute-start | bytes 393224 | tf_op jit(solution)/shard_map/ppermute | solution.py:346
  40.4 8.0 %collective-permute-start.17 = (bf16[256,256]{1,0:T(8,128)(2,1)S(1)}, bf16[256,256]{1,0:T(8,128)(2,1)S(1)}, u32[]{:S(2)}, u32[]{:S(2)}) collective-permute-start(bf16[256,256]{1,0:T(8,128)(2,1)S(1)} %collective-permute-done.15.refs_1_), channel_id=1, source_target_pairs={{2,4},{4,2},{3,5},{5,3},{10,12},{12,10},{11,13},{13,11},{18,20},{2... | collective-permute-start | bytes 393224 | tf_op jit(solution)/shard_map/ppermute | solution.py:346
  48.5 1.6 %copy-start.2 = (bf16[1024,1024]{1,0:T(8,128)(2,1)S(1)}, bf16[1024,1024]{1,0:T(8,128)(2,1)}, u32[]{:S(2)}) copy-start(bf16[1024,1024]{1,0:T(8,128)(2,1)} %get-tuple-element.29.low) | copy-start | bytes 6291460
  57.3 33.3 %collective-permute-start.22 = (f32[2,128,256]{2,1,0:T(8,128)S(1)}, f32[2,128,256]{2,1,0:T(8,128)S(1)}, u32[]{:S(2)}, u32[]{:S(2)}) collective-permute-start(f32[2,128,256]{2,1,0:T(8,128)S(1)} %get-tuple-element.42), channel_id=1, source_target_pairs={{0,1},{1,0},{2,3},{3,2},{4,5},{5,4},{6,7},{7,6},{8,9},{9,8},{10,11... | collective-permute-start | bytes 786440 | tf_op jit(solution)/shard_map/ppermute | solution.py:47
  57.3 33.2 %collective-permute-start.21 = (bf16[2,128,256]{2,1,0:T(8,128)(2,1)S(1)}, bf16[2,128,256]{2,1,0:T(8,128)(2,1)S(1)}, u32[]{:S(2)}, u32[]{:S(2)}) collective-permute-start(bf16[2,128,256]{2,1,0:T(8,128)(2,1)S(1)} %get-tuple-element.41), channel_id=1, source_target_pairs={{2,1},{3,0},{4,7},{5,6},{10,9},{11,8},{12,15},{13,14},{18,17},{19,... | collective-permute-start | bytes 393224 | tf_op jit(solution)/shard_map/ppermute | solution.py:350
  58.6 21.8 %collective-permute-start.18 = (bf16[2,128,256]{2,1,0:T(8,128)(2,1)S(1)}, bf16[2,128,256]{2,1,0:T(8,128)(2,1)S(1)}, u32[]{:S(2)}, u32[]{:S(2)}) collective-permute-start(bf16[2,128,256]{2,1,0:T(8,128)(2,1)S(1)} %get-tuple-element.37), channel_id=1, source_target_pairs={{2,0},{3,1},{4,6},{5,7},{10,8},{11,9},{12,14},{13,15},{18,16},{19,... | collective-permute-start | bytes 393224 | tf_op jit(solution)/shard_map/ppermute | solution.py:350
  67.3 23.3 %collective-permute-start.20 = (f32[2,128,256]{2,1,0:T(8,128)S(1)}, f32[2,128,256]{2,1,0:T(8,128)S(1)}, u32[]{:S(2)}, u32[]{:S(2)}) collective-permute-start(f32[2,128,256]{2,1,0:T(8,128)S(1)} %get-tuple-element.40), channel_id=1, source_target_pairs={{0,1},{1,0},{2,3},{3,2},{4,5},{5,4},{6,7},{7,6},{8,9},{9,8},{10,11... | collective-permute-start | bytes 786440 | tf_op jit(solution)/shard_map/ppermute | solution.py:47
  67.9 22.7 %collective-permute-start.19 = (bf16[2,128,256]{2,1,0:T(8,128)(2,1)S(1)}, bf16[2,128,256]{2,1,0:T(8,128)(2,1)S(1)}, u32[]{:S(2)}, u32[]{:S(2)}) collective-permute-start(bf16[2,128,256]{2,1,0:T(8,128)(2,1)S(1)} %get-tuple-element.39), channel_id=1, source_target_pairs={{2,1},{3,0},{4,7},{5,6},{10,9},{11,8},{12,15},{13,14},{18,17},{19,... | collective-permute-start | bytes 393224 | tf_op jit(solution)/shard_map/ppermute | solution.py:350
  80.4 10.1 %collective-permute-start.14 = (bf16[2,128,256]{2,1,0:T(8,128)(2,1)S(1)}, bf16[2,128,256]{2,1,0:T(8,128)(2,1)S(1)}, u32[]{:S(2)}, u32[]{:S(2)}) collective-permute-start(bf16[2,128,256]{2,1,0:T(8,128)(2,1)S(1)} %get-tuple-element.33), channel_id=1, source_target_pairs={{2,0},{3,1},{4,6},{5,7},{10,8},{11,9},{12,14},{13,15},{18,16},{19,... | collective-permute-start | bytes 393224 | tf_op jit(solution)/shard_map/ppermute | solution.py:350

commit v4 on v2

v4 whole, which is shorter than its diff:
```python
import functools
import math

import jax
import jax.numpy as jnp
import numpy as np
from jax import lax
from jax.experimental import pallas as pl
from jax.experimental.pallas import tpu as pltpu
from jax.sharding import Mesh, PartitionSpec as P

CHUNK = 256
LIMIT = 32 * 1024 * 1024
GRAM_COST = 1024
SOLVE_COST = 1024


def make_table(samples, nfreq, first):
    times = np.arange(samples)
    phase = times[:, None] * (first + np.arange(nfreq))[None, :] % samples
    angle = np.float32(2.0 * math.pi) * phase.astype(np.float32) / np.float32(samples)
    return np.stack([np.cos(angle), -np.sin(angle)], -1).astype(jnp.bfloat16)


def spread_table(samples, nfreq, shots):
    table = make_table(samples, nfreq, samples // 16).astype(np.float32)
    whole = np.einsum("tfc,sz->fcszt", table, np.eye(shots, dtype=np.float32))
    return whole.reshape(nfreq * 2 * shots, shots * samples).astype(jnp.bfloat16)


def ring_order(chips):
    return [0, 1, 3, 2] if chips == 4 else list(range(chips))


def ring_gather(piece, chips):
    order = ring_order(chips)
    pairs = [(order[i], order[(i + 1) % chips]) for i in range(chips)]
    pieces = [piece]
    for _ in range(chips - 1):
        pieces.append(lax.ppermute(pieces[-1], "chip", pairs))
    return pieces


def after(array, *others):
    return lax.optimization_barrier((array, *others))[0]


def swap_core(array):
    return lax.ppermute(array, "core", [(0, 1), (1, 0)])


def split(array):
    high = lax.reduce_precision(array, 8, 7)
    return high.astype(jnp.bfloat16), (array - high).astype(jnp.bfloat16)


def dot(left, right):
    return jnp.dot(left, right, preferred_element_type=jnp.float32)


def dot_nt(left, right):
    return lax.dot_general(left, right, (((1,), (1,)), ((), ())), preferred_element_type=jnp.float32)


def spectra(traces, matrix):
    return dot(matrix, traces.reshape(-1, traces.shape[2])).astype(jnp.bfloat16)


def to_freq(spec, nfreq):
    parts = spec.reshape(nfreq, -1, spec.shape[1])
    me = lax.axis_index("freq")
    out = []
    for step in range(nfreq):
        there = me ^ step
        part = lax.dynamic_index_in_dim(parts, there, 0, keepdims=False)
        out.append(part if step == 0 else lax.ppermute(part, "freq", [(f, f ^ step) for f in range(nfreq)]))
    return jnp.concatenate(out, 0)


def gram_kernel(shots, place, *refs):
    sources, (high, low, damping, rows_t), (both, pieces, arrived) = refs[:-7], refs[-7:-3], refs[-3:]
    count, width = sources[0].shape
    half = both.shape[0] // 2
    copies = [pltpu.make_async_copy(source, pieces.at[n], arrived.at[n]) for n, source in enumerate(sources)]
    for copy in copies:
        copy.start()
    total = jnp.zeros((1, width), jnp.float32)
    at = 0
    for number, copy in enumerate(copies):
        copy.wait()
        piece = pieces.at[number]
        for part in range(0, count, 2 * shots):
            real, imag = piece[pl.ds(part, shots), :], piece[pl.ds(part + shots, shots), :]
            both[pl.ds(at, shots), pl.ds(0, width)] = real
            both[pl.ds(at, shots), pl.ds(width, width)] = -imag
            both[pl.ds(half + at, shots), pl.ds(0, width)] = imag
            both[pl.ds(half + at, shots), pl.ds(width, width)] = real
            real, imag = real.astype(jnp.float32), imag.astype(jnp.float32)
            total += jnp.sum(real * real + imag * imag, axis=0, keepdims=True)
            at += shots
    damping[...] = 0.1 * jnp.sum(total, axis=1, keepdims=True) / width
    for at in range(0, half, 256):
        gram = dot_nt(both[pl.ds(at, 256), :], both[...])
        rounded = gram.astype(jnp.bfloat16)
        high[pl.ds(at, 256), :] = rounded
        low[pl.ds(at, 256), :] = (gram - rounded.astype(jnp.float32)).astype(jnp.bfloat16)
    wide = rows_t.shape[0] // 2
    for number in range(2):
        start = pl.multiple_of(place[number] * wide, wide)
        rows_t[pl.ds(number * wide, wide), :] = both[:, pl.ds(start, wide)].T


def gram_call(place, pieces, shots, rows):
    count, width = pieces[0].shape
    size = count * len(pieces)
    block = jax.ShapeDtypeStruct((size // 2, size), jnp.bfloat16)
    return pl.pallas_call(
        functools.partial(gram_kernel, shots),
        out_shape=(
            block,
            block,
            jax.ShapeDtypeStruct((1, 1), jnp.float32),
            jax.ShapeDtypeStruct((2 * rows, size), jnp.bfloat16),
        ),
        in_specs=[pl.BlockSpec(memory_space=pltpu.SMEM)] + [pl.BlockSpec(memory_space=pltpu.HBM)] * len(pieces),
        out_specs=(pl.BlockSpec(memory_space=pltpu.VMEM),) * 4,
        scratch_shapes=[
            pltpu.VMEM((size, 2 * width), jnp.bfloat16),
            pltpu.VMEM((len(pieces), count, width), jnp.bfloat16),
            pltpu.SemaphoreType.DMA((len(pieces),)),
        ],
        compiler_params=pltpu.CompilerParams(vmem_limit_bytes=LIMIT),
        cost_estimate=pl.CostEstimate(flops=GRAM_COST, bytes_accessed=1024, transcendentals=0),
        name="gram",
    )(place, *pieces)


def fill_turned(target, tile, value):
    half, columns = target.shape[0] // 2, target.shape[1] // 2
    target[tile, :] = value
    below = pl.ds(half + tile.start, tile.size)
    target[below, pl.ds(0, columns)] = value[:, columns:]
    target[below, pl.ds(columns, columns)] = -value[:, :columns]


def per_column(total):
    columns = total.shape[1] // 2
    total = total[:, :columns] + total[:, columns:]
    return jnp.concatenate([total, total], 1)


def two_parts(value):
    high = value.astype(jnp.bfloat16)
    return high, (value - high.astype(jnp.float32)).astype(jnp.bfloat16)


def solve_kernel(shots, first, count, damping, *refs):
    sources, refs = refs[: 3 + count], refs[3 + count :]
    block, sent, start, image, step_high, step_low, step_image, high, low, rows_t, pieces, staged, arrived = refs[-13:]
    half, columns = start.shape[0] // 2, start.shape[1] // 2
    targets = [high, low, rows_t] + [pieces.at[number] for number in range(count)]
    copies = [pltpu.make_async_copy(sources[n], target, arrived.at[n]) for n, target in enumerate(targets)]
    for copy in copies[3:] + copies[:3]:
        copy.start()
    tiles = [pl.ds(at, 256) for at in range(0, half, 256)]
    at = 0
    for number in range(count):
        copies[3 + number].wait()
        piece = pieces.at[number]
        for part in range(0, piece.shape[0], 2 * shots):
            real, imag = piece[pl.ds(part, shots), :], piece[pl.ds(part + shots, shots), :]
            fill_turned(start, pl.ds(at, shots), jnp.concatenate([real, imag], 1))
            at += shots
    copies[0].wait()
    copies[1].wait()
    damp = damping[...]
    norm_now = jnp.zeros((1, 2 * columns), jnp.float32)
    image_norm = jnp.zeros((1, 2 * columns), jnp.float32)
    for tile in tiles:
        value = dot(high[tile, :], start[...]) + dot(low[tile, :], start[...])
        image[tile, :] = value
        norm_now += jnp.sum(start[tile, :].astype(jnp.float32) * value, axis=0, keepdims=True)
        image_norm += jnp.sum(value * value, axis=0, keepdims=True)
    norm_now, image_norm = per_column(norm_now), per_column(image_norm)
    alpha = norm_now / (image_norm + damp * norm_now)
    keep = 1.0 - alpha * damp
    for tile in tiles:
        resid_high, resid_low = two_parts(keep * start[tile, :].astype(jnp.float32) - alpha * image[tile, :])
        fill_turned(step_high, tile, resid_high)
        fill_turned(step_low, tile, resid_low)
    norm_next = jnp.zeros((1, 2 * columns), jnp.float32)
    for tile in tiles:
        value = dot(high[tile, :], step_high[...]) + (
            dot(low[tile, :], step_high[...]) + dot(high[tile, :], step_low[...])
        )
        step_image[tile, :] = value
        resid = keep * start[tile, :].astype(jnp.float32) - alpha * image[tile, :]
        norm_next += jnp.sum(resid * value, axis=0, keepdims=True)
    norm_next = per_column(norm_next)
    ratio = norm_next / norm_now
    curv = jnp.zeros((1, 2 * columns), jnp.float32)
    for tile in tiles:
        direc = (keep + ratio) * start[tile, :].astype(jnp.float32) - alpha * image[tile, :]
        value = step_image[tile, :] + ratio * image[tile, :]
        curv += jnp.sum(value * (value + damp * direc), axis=0, keepdims=True)
    beta = norm_next / per_column(curv)
    from_start = alpha + beta * (keep + ratio)
    from_image = alpha * beta
    for tile in tiles:
        weight = from_start * start[tile, :].astype(jnp.float32) - from_image * image[tile, :]
        weight_high, weight_low = two_parts(weight)
        fill_turned(step_high, tile, weight_high)
        fill_turned(step_low, tile, weight_low)
    copies[2].wait()
    rows = rows_t.shape[0] // 2
    value = dot(rows_t[pl.ds(0, rows), :], step_high[...]) + dot(rows_t[pl.ds(0, rows), :], step_low[...])
    staged[:, 0, :] = value[:, :columns]
    staged[:, 1, :] = -value[:, columns:]
    offset = lax.axis_index("core") * (block.shape[2] // 2) + first
    copy = pltpu.make_async_copy(
        staged, block.at[:, :, pl.ds(pl.multiple_of(offset, columns), columns)], arrived.at[len(targets)]
    )
    copy.start()
    value = dot(rows_t[pl.ds(rows, rows), :], step_high[...]) + dot(rows_t[pl.ds(rows, rows), :], step_low[...])
    sent[...] = jnp.concatenate([value[:, :columns], -value[:, columns:]], 1)
    copy.wait()


def solve_call(high, low, damping, rows_t, pieces, shots, first, block, width):
    half, size = high.shape
    count, columns = len(pieces), pieces[0].shape[1]
    rows = rows_t.shape[0] // 2
    earlier = [] if block is None else [block]
    return pl.pallas_call(
        functools.partial(solve_kernel, shots, first, count),
        out_shape=(
            jax.ShapeDtypeStruct((rows, 2, width), jnp.float32),
            jax.ShapeDtypeStruct((rows, 2 * columns), jnp.float32),
        ),
        in_specs=[pl.BlockSpec(memory_space=pltpu.VMEM)] + [pl.BlockSpec(memory_space=pltpu.HBM)] * (3 + count + len(earlier)),
        out_specs=(pl.BlockSpec(memory_space=pltpu.HBM), pl.BlockSpec(memory_space=pltpu.VMEM)),
        input_output_aliases={4 + count: 0} if earlier else {},
        scratch_shapes=[
            pltpu.VMEM((size, 2 * columns), jnp.bfloat16),
            pltpu.VMEM((half, 2 * columns), jnp.float32),
            pltpu.VMEM((size, 2 * columns), jnp.bfloat16),
            pltpu.VMEM((size, 2 * columns), jnp.bfloat16),
            pltpu.VMEM((half, 2 * columns), jnp.float32),
            pltpu.VMEM(high.shape, jnp.bfloat16),
            pltpu.VMEM(low.shape, jnp.bfloat16),
            pltpu.VMEM(rows_t.shape, jnp.bfloat16),
            pltpu.VMEM((count,) + pieces[0].shape, jnp.bfloat16),
            pltpu.VMEM((rows, 2, columns), jnp.float32),
            pltpu.SemaphoreType.DMA((4 + count,)),
        ],
        compiler_params=pltpu.CompilerParams(vmem_limit_bytes=LIMIT),
        cost_estimate=pl.CostEstimate(flops=SOLVE_COST, bytes_accessed=1024, transcendentals=0),
        name="solve",
    )(damping, high, low, rows_t, *pieces, *earlier)


def place_kernel(_, *refs):
    sources, (block, staged, arrived) = refs[:-3], refs[-3:]
    columns = staged.shape[3]
    copies = []
    for number, source in enumerate(sources):
        staged[number, :, 0, :] = source[:, :columns]
        staged[number, :, 1, :] = source[:, columns:]
        offset = (1 - lax.axis_index("core")) * (block.shape[2] // 2) + number * columns
        copy = pltpu.make_async_copy(
            staged.at[number], block.at[:, :, pl.ds(pl.multiple_of(offset, columns), columns)], arrived.at[number]
        )
        copy.start()
        copies.append(copy)
    for copy in copies:
        copy.wait()


def place_call(block, got):
    rows, columns = got[0].shape
    return pl.pallas_call(
        place_kernel,
        out_shape=jax.ShapeDtypeStruct(block.shape, jnp.float32),
        in_specs=[pl.BlockSpec(memory_space=pltpu.HBM)] + [pl.BlockSpec(memory_space=pltpu.VMEM)] * len(got),
        out_specs=pl.BlockSpec(memory_space=pltpu.HBM),
        input_output_aliases={0: 0},
        scratch_shapes=[
            pltpu.VMEM((len(got), rows, 2, columns // 2), jnp.float32),
            pltpu.SemaphoreType.DMA((len(got),)),
        ],
        compiler_params=pltpu.CompilerParams(vmem_limit_bytes=LIMIT),
        name="place",
    )(block, *got)


def plain_gram(place, pieces, shots, rows):
    width = pieces[0].shape[1]
    even = jnp.concatenate(pieces, 0)
    turned = even.reshape(-1, 2, shots, width)
    odd = jnp.stack([-turned[:, 1], turned[:, 0]], 1).reshape(even.shape)
    blocks = []
    for number in range(2):
        blocks.append(lax.dynamic_slice_in_dim(even, place[number] * rows, rows, 1).T)
        blocks.append(-lax.dynamic_slice_in_dim(odd, place[number] * rows, rows, 1).T)
    return even, odd, 0.1 * jnp.sum(jnp.square(even.astype(jnp.float32))) / width, jnp.concatenate(blocks, 0)


def dot_tn(left, right):
    return lax.dot_general(left, right, (((0,), (0,)), ((), ())), preferred_element_type=jnp.float32)


def plain_apply(even, odd, parts):
    out = []
    for side in (even, odd):
        high, low = split(sum(dot_tn(side, part) for part in parts))
        out.append(dot(side, high) + dot(side, low))
    return out[0] + out[1]


def plain_solve(even, odd, damping, rows_t, pieces):
    start = jnp.concatenate(pieces, 0)
    wide = start.astype(jnp.float32)
    image = plain_apply(even, odd, (start,))
    norm_now = jnp.sum(wide * image, axis=0)
    alpha = norm_now / (jnp.sum(image * image, axis=0) + damping * norm_now)
    resid = (1.0 - alpha * damping) * wide - alpha * image
    resid_image = plain_apply(even, odd, split(resid))
    norm_next = jnp.sum(resid * resid_image, axis=0)
    ratio = norm_next / norm_now
    direc = resid + ratio * wide
    direc_image = resid_image + ratio * image
    curv = jnp.sum(direc_image * (direc_image + damping * direc), axis=0)
    weights_high, weights_low = split(alpha * wide + norm_next / curv * direc)
    block = (dot(rows_t, weights_high) + dot(rows_t, weights_low)).reshape(2, 2, -1, start.shape[1])
    return block[0], block[1]


def shards(up_traces, down_traces):
    local_shots, samples, width = up_traces.shape
    nfreq, chips = lax.axis_size("freq"), lax.axis_size("chip")
    core = lax.axis_index("core")
    half = width // 2
    rows = width // (2 * chips)
    size = 2 * local_shots * nfreq * 2 * chips
    matrix = jnp.asarray(spread_table(samples, nfreq, local_shots))

    down_spec = spectra(down_traces, matrix)
    up_spec = spectra(up_traces, after(matrix, down_spec))
    down = after(to_freq(down_spec, nfreq), up_spec)
    own = ring_gather(down, chips)

    up = to_freq(after(up_spec, down), nfreq)
    mine = lax.dynamic_slice_in_dim(up, core * half, half, 1)
    theirs = swap_core(lax.dynamic_slice_in_dim(up, (1 - core) * half, half, 1))
    up = jnp.concatenate([mine, theirs], 0)

    pieces = []
    for piece in own:
        pieces += [piece, swap_core(piece)]
    place = 2 * lax.axis_index("chip") + jnp.stack([core, 1 - core]).astype(jnp.int32)

    small = 2 * chips * 2 * local_shots * nfreq <= 1024 and rows == 128 and half == 2 * CHUNK and local_shots == 16
    if not small:
        operator = plain_gram(place, pieces, local_shots, rows)
        chunk = CHUNK if half % CHUNK == 0 else half
        kept, got = [], []
        for at in range(0, half, chunk):
            stay, send = plain_solve(*operator, ring_gather(up[:, at : at + chunk], chips))
            kept.append(stay)
            got.append(swap_core(send))
        kept, got = jnp.concatenate(kept, 2), jnp.concatenate(got, 2)
        first = core == 0
        block = jnp.concatenate([jnp.where(first, kept, got), jnp.where(first, got, kept)], 2)
        return jnp.transpose(block, (1, 0, 2))[None]

    early = ring_gather(up[:, :CHUNK], chips)
    late = ring_gather(after(up[:, CHUNK:], own[2]), chips)
    place = after(place, late[1])
    operator = gram_call(place, pieces, local_shots, rows)
    early[0] = after(early[0], late[2])
    block, sent_early = solve_call(*operator, early, local_shots, 0, None, width)
    block, sent_late = solve_call(*operator, late, local_shots, CHUNK, block, width)
    return place_call(block, [swap_core(sent_early), swap_core(sent_late)])[None]


def solution(mesh):
    nfreq, nshot = mesh.devices.shape
    fine = Mesh(mesh.devices.reshape(nfreq, nshot // 2, 2), ("freq", "chip", "core"))
    spec = P(("freq", "chip", "core"), None, None)
    out_specs = P("freq", ("chip", "core"), None, None)
    return jax.shard_map(shards, mesh=fine, in_specs=(spec, spec), out_specs=out_specs, check_vma=False)
```

time: 74.6 us -> 69.7 us (0.934)
  waiting for transfers between devices: 26.7 us -> 23.5 us
  local copies, waits for them, and re-layouts: 1.94 us -> 0.08 us
  starting transfers between devices: 21 us -> 22.7 us
  Pallas kernels: 20.2 us -> 18.9 us
    ppermute x6, waiting for transfers between devices: 8.33 us -> 4.39 us  [to_freq(): lax.ppermute(part, 'freq', [(f, f ^ step) for f in range(nfreq)])]
    broadcast_in_dim x1 -> x0, local copies, waits for them, and re-layouts: 1.78 us -> none  [shards(): return jnp.transpose(block, (1, 0, 2))[None]]
    ppermute x9, waiting for transfers between devices: 16 us -> 17.7 us  [ring_gather(): pieces.append(lax.ppermute(pieces[-1], 'chip', pairs))]
    pallas_call x3 -> x4, Pallas kernels: 20.2 us -> 18.9 us  [the longest x2 13.8 us: solve_call(): pl.pallas_call(functools.partial(solve_kernel, shots, first, count), out_...]
    ppermute x9, starting transfers between devices: 11.7 us -> 13 us  [ring_gather(): pieces.append(lax.ppermute(pieces[-1], 'chip', pairs))]
    ppermute x7, waiting for transfers between devices: 2.4 us -> 1.41 us  [swap_core(): return lax.ppermute(array, 'core', [(0, 1), (1, 0)])]
  transfers between devices with their start and end apart: 22 -> 22, of which waited for: 14 -> 12; matrix products, arithmetic and copies ran while one was open for 1% -> 1% of each run, Pallas kernels for 27% -> 16%
where the time goes in v4:
time: 69.7 us; the launch traced here: 69.6 us
  waiting for transfers between devices  23.5 us (34%)
  starting transfers between devices  22.7 us (33%)
  Pallas kernels  18.9 us (27%)
  matrix products  3.95 us (6%)
    ppermute x9, waiting for transfers between devices, ring_gather(): pieces.append(lax.ppermute(pieces[-1], 'chip', pairs))  17.7 us
    pallas_call x2, Pallas kernels, solve_call(): pl.pallas_call(functools.partial(solve_kernel, shots, first, count), out_...  13.8 us
    ppermute x9, starting transfers between devices, ring_gather(): pieces.append(lax.ppermute(pieces[-1], 'chip', pairs))  13 us
    ppermute x6, starting transfers between devices, to_freq(): lax.ppermute(part, 'freq', [(f, f ^ step) for f in range(nfreq)])  8.1 us
    ppermute x6, waiting for transfers between devices, to_freq(): lax.ppermute(part, 'freq', [(f, f ^ step) for f in range(nfreq)])  4.39 us
    pallas_call x1, Pallas kernels, gram_call(): pl.pallas_call(functools.partial(gram_kernel, shots), out_shape=(block, b...  4.26 us
    dot_general x2, matrix products, dot(): return jnp.dot(left, right, preferred_element_type=jnp.float32)  3.95 us
    ppermute x7, starting transfers between devices, swap_core(): return lax.ppermute(array, 'core', [(0, 1), (1, 0)])  1.65 us
  transfers between devices with their start and end apart: 22, of which 12 were waited for; matrix products, arithmetic and copies ran while one was open for 1% of the time, Pallas kernels for 16%

profile of v4, /device:TPU:0, one launch (start us, length us, event | category | flops | bytes accessed | tf_op | source)
XLA Modules:
  0.0 69.6 jit_solution(11599901526688878928)
XLA Ops:
  0.0 0.0 copy-start.1
  0.0 0.0 copy-start
  0.0 3.2 %convolution_convert_fusion.1 = bf16[128,1024]{1,0:T(8,128)(2,1)S(1)} fusion(bf16[128,2048]{1,0:T(8,128)(2,1)} %constant.44.clone, bf16[2048,1024]{1,0:T(8,128)(2,1)} %bitcast.27), kind=kOutput, calls=%fused_computation.1 | convolution fusion | flops 537001984 | bytes 4980736 | tf_op jit(solution)/shard_map/dot_general | solution.py:58
  3.3 3.0 %collective-permute-start = (bf16[32,1024]{1,0:T(8,128)(2,1)S(1)}, bf16[32,1024]{1,0:T(8,128)(2,1)S(1)}, u32[]{:S(2)}, u32[]{:S(2)}) collective-permute-start(bf16[32,1024]{1,0:T(8,128)(2,1)S(1)} %get-tuple-element.44), channel_id=1, source_target_pairs={{0,8},{8,0},{16,24},{24,16},{1,9},{9,1},{17,25},{25,17},{2,10},{10... | collective-permute-start | bytes 196616 | tf_op jit(solution)/shard_map/ppermute | solution.py:76
  6.3 1.5 %collective-permute-start.1 = (bf16[32,1024]{1,0:T(8,128)(2,1)S(1)}, bf16[32,1024]{1,0:T(8,128)(2,1)S(1)}, u32[]{:S(2)}, u32[]{:S(2)}) collective-permute-start(bf16[32,1024]{1,0:T(8,128)(2,1)S(1)} %get-tuple-element.43), channel_id=1, source_target_pairs={{0,16},{8,24},{16,0},{24,8},{1,17},{9,25},{17,1},{25,9},{2,18},{10... | collective-permute-start | bytes 196616 | tf_op jit(solution)/shard_map/ppermute | solution.py:76
  7.8 0.0 collective-permute-start.2
  7.8 0.0 copy-done.1
  7.8 0.0 copy-done
  7.8 0.7 %convolution_convert_fusion = bf16[128,1024]{1,0:T(8,128)(2,1)S(1)} fusion(bf16[128,2048]{1,0:T(8,128)(2,1)S(1)} %copy-done.1, bf16[2048,1024]{1,0:T(8,128)(2,1)S(1)} %bitcast.28), kind=kOutput, calls=%fused_computation | convolution fusion | flops 537001984 | bytes 4980736 | tf_op jit(solution)/shard_map/dot_general | solution.py:58
  8.6 0.1 collective-permute-done
  8.6 1.9 %collective-permute-done.1 = bf16[32,1024]{1,0:T(8,128)(2,1)S(1)} collective-permute-done((bf16[32,1024]{1,0:T(8,128)(2,1)S(1)}, bf16[32,1024]{1,0:T(8,128)(2,1)S(1)}, u32[]{:S(2)}, u32[]{:S(2)}) %collective-permute-start.1) | collective-permute-done | bytes 65568 | tf_op jit(solution)/shard_map/ppermute | solution.py:76
  10.5 2.4 %collective-permute-done.2 = bf16[32,1024]{1,0:T(8,128)(2,1)S(1)} collective-permute-done((bf16[32,1024]{1,0:T(8,128)(2,1)S(1)}, bf16[32,1024]{1,0:T(8,128)(2,1)S(1)}, u32[]{:S(2)}, u32[]{:S(2)}) %collective-permute-start.2) | collective-permute-done | bytes 65568 | tf_op jit(solution)/shard_map/ppermute | solution.py:76
  13.0 1.6 %collective-permute-start.7 = (bf16[128,1024]{1,0:T(8,128)(2,1)S(1)}, bf16[128,1024]{1,0:T(8,128)(2,1)S(1)}, u32[]{:S(2)}, u32[]{:S(2)}) collective-permute-start(bf16[128,1024]{1,0:T(8,128)(2,1)S(1)} %pad_maximum_fusion.refs_0_), channel_id=1, source_target_pairs={{0,2},{2,6},{6,4},{4,0},{1,3},{3,7},{7,5},{5,1},{8,10},{10,14},{14... | collective-permute-start | bytes 786440 | tf_op jit(solution)/shard_map/ppermute | solution.py:40
  14.6 0.6 collective-permute-start.3
  15.2 0.5 collective-permute-start.4
  15.7 2.4 %collective-permute-start.5 = (bf16[32,1024]{1,0:T(8,128)(2,1)S(1)}, bf16[32,1024]{1,0:T(8,128)(2,1)S(1)}, u32[]{:S(2)}, u32[]{:S(2)}) collective-permute-start(bf16[32,1024]{1,0:T(8,128)(2,1)S(1)} %get-tuple-element.38), channel_id=1, source_target_pairs={{0,24},{8,16},{16,8},{24,0},{1,25},{9,17},{17,9},{25,1},{2,26},{10... | collective-permute-start | bytes 196616 | tf_op jit(solution)/shard_map/ppermute | solution.py:76
  18.2 2.1 %collective-permute-done.7.refs_2_ = bf16[128,1024]{1,0:T(8,128)(2,1)S(1)} collective-permute-done((bf16[128,1024]{1,0:T(8,128)(2,1)S(1)}, bf16[128,1024]{1,0:T(8,128)(2,1)S(1)}, u32[]{:S(2)}, u32[]{:S(2)}) %collective-permute-start.7) | collective-permute-done | bytes 262176 | tf_op jit(solution)/shard_map/ppermute | solution.py:40
  20.3 0.8 %collective-permute-start.8 = (bf16[128,1024]{1,0:T(8,128)(2,1)S(1)}, bf16[128,1024]{1,0:T(8,128)(2,1)S(1)}, u32[]{:S(2)}, u32[]{:S(2)}) collective-permute-start(bf16[128,1024]{1,0:T(8,128)(2,1)S(1)} %collective-permute-done.7.refs_2_), channel_id=1, source_target_pairs={{0,2},{2,6},{6,4},{4,0},{1,3},{3,7},{7,5},{5,1},{8,10},{10,14},{14... | collective-permute-start | bytes 786440 | tf_op jit(solution)/shard_map/ppermute | solution.py:40
  21.1 0.0 collective-permute-done.3
  21.1 0.0 collective-permute-done.4
  21.1 0.0 collective-permute-done.5
  21.2 0.1 collective-permute-start.6
  21.2 0.5 collective-permute-start.10
  21.7 6.4 %collective-permute-done.8.refs_4_ = bf16[128,1024]{1,0:T(8,128)(2,1)S(1)} collective-permute-done((bf16[128,1024]{1,0:T(8,128)(2,1)S(1)}, bf16[128,1024]{1,0:T(8,128)(2,1)S(1)}, u32[]{:S(2)}, u32[]{:S(2)}) %collective-permute-start.8) | collective-permute-done | bytes 262176 | tf_op jit(solution)/shard_map/ppermute | solution.py:40
  28.2 0.8 %collective-permute-start.13 = (bf16[128,1024]{1,0:T(8,128)(2,1)S(1)}, bf16[128,1024]{1,0:T(8,128)(2,1)S(1)}, u32[]{:S(2)}, u32[]{:S(2)}) collective-permute-start(bf16[128,1024]{1,0:T(8,128)(2,1)S(1)} %collective-permute-done.8.refs_4_), channel_id=1, source_target_pairs={{0,2},{2,6},{6,4},{4,0},{1,3},{3,7},{7,5},{5,1},{8,10},{10,14},{14... | collective-permute-start | bytes 786440 | tf_op jit(solution)/shard_map/ppermute | solution.py:40
  29.0 0.0 collective-permute-done.6
  29.0 3.4 %collective-permute-start.17 = (bf16[256,256]{1,0:T(8,128)(2,1)S(1)}, bf16[256,256]{1,0:T(8,128)(2,1)S(1)}, u32[]{:S(2)}, u32[]{:S(2)}) collective-permute-start(bf16[256,256]{1,0:T(8,128)(2,1)S(1)} %get-tuple-element.28.refs_3_), channel_id=1, source_target_pairs={{0,2},{2,6},{6,4},{4,0},{1,3},{3,7},{7,5},{5,1},{8,10},{10,14},{14... | collective-permute-start | bytes 393224 | tf_op jit(solution)/shard_map/ppermute | solution.py:40
  32.4 0.1 collective-permute-start.9
  32.5 0.0 collective-permute-start.11
  32.5 0.0 collective-permute-done.10.refs_1_
  32.5 0.5 collective-permute-start.12
  33.0 3.0 %collective-permute-done.13.refs_6_ = bf16[128,1024]{1,0:T(8,128)(2,1)S(1)} collective-permute-done((bf16[128,1024]{1,0:T(8,128)(2,1)S(1)}, bf16[128,1024]{1,0:T(8,128)(2,1)S(1)}, u32[]{:S(2)}, u32[]{:S(2)}) %collective-permute-start.13) | collective-permute-done | bytes 262176 | tf_op jit(solution)/shard_map/ppermute | solution.py:40
  36.0 0.0 collective-permute-start.14
  36.0 1.4 %collective-permute-done.17.refs_4_ = bf16[256,256]{1,0:T(8,128)(2,1)S(1)} collective-permute-done((bf16[256,256]{1,0:T(8,128)(2,1)S(1)}, bf16[256,256]{1,0:T(8,128)(2,1)S(1)}, u32[]{:S(2)}, u32[]{:S(2)}) %collective-permute-start.17) | collective-permute-done | bytes 131104 | tf_op jit(solution)/shard_map/ppermute | solution.py:40
  37.4 0.8 %collective-permute-start.18 = (bf16[256,256]{1,0:T(8,128)(2,1)S(1)}, bf16[256,256]{1,0:T(8,128)(2,1)S(1)}, u32[]{:S(2)}, u32[]{:S(2)}) collective-permute-start(bf16[256,256]{1,0:T(8,128)(2,1)S(1)} %collective-permute-done.17.refs_4_), channel_id=1, source_target_pairs={{0,2},{2,6},{6,4},{4,0},{1,3},{3,7},{7,5},{5,1},{8,10},{10,14},{14... | collective-permute-start | bytes 393224 | tf_op jit(solution)/shard_map/ppermute | solution.py:40
  38.2 0.6 collective-permute-done.9.refs_4_
  38.8 2.8 %collective-permute-start.15 = (bf16[256,256]{1,0:T(8,128)(2,1)S(1)}, bf16[256,256]{1,0:T(8,128)(2,1)S(1)}, u32[]{:S(2)}, u32[]{:S(2)}) collective-permute-start(bf16[256,256]{1,0:T(8,128)(2,1)S(1)} %collective-permute-done.9.refs_4_), channel_id=1, source_target_pairs={{0,2},{2,6},{6,4},{4,0},{1,3},{3,7},{7,5},{5,1},{8,10},{10,14},{14... | collective-permute-start | bytes 393224 | tf_op jit(solution)/shard_map/ppermute | solution.py:40
  41.6 2.6 %collective-permute-done.18.refs_5_ = bf16[256,256]{1,0:T(8,128)(2,1)S(1)} collective-permute-done((bf16[256,256]{1,0:T(8,128)(2,1)S(1)}, bf16[256,256]{1,0:T(8,128)(2,1)S(1)}, u32[]{:S(2)}, u32[]{:S(2)}) %collective-permute-start.18) | collective-permute-done | bytes 131104 | tf_op jit(solution)/shard_map/ppermute | solution.py:40
  44.2 0.8 %collective-permute-start.19 = (bf16[256,256]{1,0:T(8,128)(2,1)S(1)}, bf16[256,256]{1,0:T(8,128)(2,1)S(1)}, u32[]{:S(2)}, u32[]{:S(2)}) collective-permute-start(bf16[256,256]{1,0:T(8,128)(2,1)S(1)} %collective-permute-done.18.refs_5_), channel_id=1, source_target_pairs={{0,2},{2,6},{6,4},{4,0},{1,3},{3,7},{7,5},{5,1},{8,10},{10,14},{14... | collective-permute-start | bytes 393224 | tf_op jit(solution)/shard_map/ppermute | solution.py:40
  45.0 1.5 %collective-permute-done.15.refs_5_ = bf16[256,256]{1,0:T(8,128)(2,1)S(1)} collective-permute-done((bf16[256,256]{1,0:T(8,128)(2,1)S(1)}, bf16[256,256]{1,0:T(8,128)(2,1)S(1)}, u32[]{:S(2)}, u32[]{:S(2)}) %collective-permute-start.15) | collective-permute-done | bytes 131104 | tf_op jit(solution)/shard_map/ppermute | solution.py:40
  46.5 1.9 %collective-permute-start.16 = (bf16[256,256]{1,0:T(8,128)(2,1)S(1)}, bf16[256,256]{1,0:T(8,128)(2,1)S(1)}, u32[]{:S(2)}, u32[]{:S(2)}) collective-permute-start(bf16[256,256]{1,0:T(8,128)(2,1)S(1)} %collective-permute-done.15.refs_5_), channel_id=1, source_target_pairs={{0,2},{2,6},{6,4},{4,0},{1,3},{3,7},{7,5},{5,1},{8,10},{10,14},{14... | collective-permute-start | bytes 393224 | tf_op jit(solution)/shard_map/ppermute | solution.py:40
  48.4 0.1 add_add_fusion.place
  48.5 0.0 collective-permute-done.11.refs_3_
  48.5 0.0 collective-permute-done.12.refs_5_
  48.5 0.0 collective-permute-done.14.refs_7_
  48.5 4.3 %gram.1 = (bf16[512,1024]{1,0:T(8,128)(2,1)S(1)}, bf16[512,1024]{1,0:T(8,128)(2,1)S(1)}, f32[1,1]{1,0:T(1,128)}, bf16[256,1024]{1,0:T(8,128)(2,1)S(1)}) custom-call(s32[2]{0:T(128)S(1)} %add_add_fusion.place, bf16[128,1024]{1,0:T(8,128)(2,1)S(1)} %pad_maximum_fusion.refs_0_, bf16[128,1024]{1,0:T(8,128)(2,1)S(1)} %collective-permute-done.10.refs_1_, ...), custom_call_target="tpu_custom_call" | custom-call | flops 1024 | bytes 1024 | tf_op jit(solution)/shard_map/gram/pallas_call | solution.py:117
  52.7 0.0 collective-permute-done.19.refs_6_
  52.8 6.9 %solve.2 = (f32[128,2,1024]{2,1,0:T(2,128)}, f32[128,512]{1,0:T(8,128)S(1)}) custom-call(f32[1,1]{1,0:T(1,128)} %get-tuple-element.24.damping, bf16[512,1024]{1,0:T(8,128)(2,1)S(1)} %get-tuple-element.25.refs_0_, bf16[512,1024]{1,0:T(8,128)(2,1)S(1)} %get-tuple-element.26.refs_1_, bf16[256,1024]{1,0:T(8,128)(2,1)S(1)} %get-tuple-element.27.refs_2_, ...), custom_call_target="tpu_custom_call" | custom-call | flops 1024 | bytes 1024 | tf_op jit(solution)/shard_map/solve/pallas_call | solution.py:234
  59.6 0.0 collective-permute-done.16.refs_6_
  59.6 6.9 %solve.3 = (f32[128,2,1024]{2,1,0:T(2,128)}, f32[128,512]{1,0:T(8,128)S(1)}) custom-call(f32[1,1]{1,0:T(1,128)} %get-tuple-element.24.damping, bf16[512,1024]{1,0:T(8,128)(2,1)S(1)} %get-tuple-element.25.refs_0_, bf16[512,1024]{1,0:T(8,128)(2,1)S(1)} %get-tuple-element.26.refs_1_, ...), custom_call_target="tpu_custom_call", output_to_operand_aliasing={{0}: (8, {})} | custom-call | flops 1024 | bytes 1024 | tf_op jit(solution)/shard_map/solve/pallas_call | solution.py:234
  66.5 0.1 collective-permute-start.21
  66.6 0.5 collective-permute-start.20
  67.1 1.0 %collective-permute-done.21.refs_1_ = f32[128,512]{1,0:T(8,128)S(1)} collective-permute-done((f32[128,512]{1,0:T(8,128)S(1)}, f32[128,512]{1,0:T(8,128)S(1)}, u32[]{:S(2)}, u32[]{:S(2)}) %collective-permute-start.21) | collective-permute-done | bytes 262176 | tf_op jit(solution)/shard_map/ppermute | solution.py:49
  68.1 0.4 collective-permute-done.20.refs_0_
  68.5 0.9 %place.1 = f32[128,2,1024]{2,1,0:T(2,128)} custom-call(f32[128,2,1024]{2,1,0:T(2,128)} %get-tuple-element.30._, f32[128,512]{1,0:T(8,128)S(1)} %collective-permute-done.20.refs_0_, f32[128,512]{1,0:T(8,128)S(1)} %collective-permute-done.21.refs_1_), custom_call_target="tpu_custom_call", output_to_operand_aliasing={{}: (0, {})} | custom-call | tf_op jit(solution)/shard_map/place/pallas_call | solution.py:281
  (6 shorter events, 0.1 us)
Async XLA Ops:
  0.0 7.8 %copy-start.1 = (bf16[128,2048]{1,0:T(8,128)(2,1)S(1)}, bf16[128,2048]{1,0:T(8,128)(2,1)}, u32[]{:S(2)}) copy-start(bf16[128,2048]{1,0:T(8,128)(2,1)} %constant.44.clone) | copy-start | bytes 1572868
  0.0 7.8 %copy-start = (bf16[16,128,1024]{2,1,0:T(8,128)(2,1)S(1)}, bf16[16,128,1024]{2,1,0:T(8,128)(2,1)}, u32[]{:S(2)}) copy-start(bf16[16,128,1024]{2,1,0:T(8,128)(2,1)} %param.3) | copy-start | bytes 12582916
  3.3 5.4 %collective-permute-start = (bf16[32,1024]{1,0:T(8,128)(2,1)S(1)}, bf16[32,1024]{1,0:T(8,128)(2,1)S(1)}, u32[]{:S(2)}, u32[]{:S(2)}) collective-permute-start(bf16[32,1024]{1,0:T(8,128)(2,1)S(1)} %get-tuple-element.44), channel_id=1, source_target_pairs={{0,8},{8,0},{16,24},{24,16},{1,9},{9,1},{17,25},{25,17},{2,10},{10... | collective-permute-start | bytes 196616 | tf_op jit(solution)/shard_map/ppermute | solution.py:76
  6.3 4.3 %collective-permute-start.1 = (bf16[32,1024]{1,0:T(8,128)(2,1)S(1)}, bf16[32,1024]{1,0:T(8,128)(2,1)S(1)}, u32[]{:S(2)}, u32[]{:S(2)}) collective-permute-start(bf16[32,1024]{1,0:T(8,128)(2,1)S(1)} %get-tuple-element.43), channel_id=1, source_target_pairs={{0,16},{8,24},{16,0},{24,8},{1,17},{9,25},{17,1},{25,9},{2,18},{10... | collective-permute-start | bytes 196616 | tf_op jit(solution)/shard_map/ppermute | solution.py:76
  7.8 5.2 %collective-permute-start.2 = (bf16[32,1024]{1,0:T(8,128)(2,1)S(1)}, bf16[32,1024]{1,0:T(8,128)(2,1)S(1)}, u32[]{:S(2)}, u32[]{:S(2)}) collective-permute-start(bf16[32,1024]{1,0:T(8,128)(2,1)S(1)} %get-tuple-element.42), channel_id=1, source_target_pairs={{0,24},{8,16},{16,8},{24,0},{1,25},{9,17},{17,9},{25,1},{2,26},{10... | collective-permute-start | bytes 196616 | tf_op jit(solution)/shard_map/ppermute | solution.py:76
  13.0 7.3 %collective-permute-start.7 = (bf16[128,1024]{1,0:T(8,128)(2,1)S(1)}, bf16[128,1024]{1,0:T(8,128)(2,1)S(1)}, u32[]{:S(2)}, u32[]{:S(2)}) collective-permute-start(bf16[128,1024]{1,0:T(8,128)(2,1)S(1)} %pad_maximum_fusion.refs_0_), channel_id=1, source_target_pairs={{0,2},{2,6},{6,4},{4,0},{1,3},{3,7},{7,5},{5,1},{8,10},{10,14},{14... | collective-permute-start | bytes 786440 | tf_op jit(solution)/shard_map/ppermute | solution.py:40
  14.6 6.5 %collective-permute-start.3 = (bf16[32,1024]{1,0:T(8,128)(2,1)S(1)}, bf16[32,1024]{1,0:T(8,128)(2,1)S(1)}, u32[]{:S(2)}, u32[]{:S(2)}) collective-permute-start(bf16[32,1024]{1,0:T(8,128)(2,1)S(1)} %get-tuple-element.40), channel_id=1, source_target_pairs={{0,8},{8,0},{16,24},{24,16},{1,9},{9,1},{17,25},{25,17},{2,10},{10... | collective-permute-start | bytes 196616 | tf_op jit(solution)/shard_map/ppermute | solution.py:76
  15.2 5.9 %collective-permute-start.4 = (bf16[32,1024]{1,0:T(8,128)(2,1)S(1)}, bf16[32,1024]{1,0:T(8,128)(2,1)S(1)}, u32[]{:S(2)}, u32[]{:S(2)}) collective-permute-start(bf16[32,1024]{1,0:T(8,128)(2,1)S(1)} %get-tuple-element.39), channel_id=1, source_target_pairs={{0,16},{8,24},{16,0},{24,8},{1,17},{9,25},{17,1},{25,9},{2,18},{10... | collective-permute-start | bytes 196616 | tf_op jit(solution)/shard_map/ppermute | solution.py:76
  15.7 5.4 %collective-permute-start.5 = (bf16[32,1024]{1,0:T(8,128)(2,1)S(1)}, bf16[32,1024]{1,0:T(8,128)(2,1)S(1)}, u32[]{:S(2)}, u32[]{:S(2)}) collective-permute-start(bf16[32,1024]{1,0:T(8,128)(2,1)S(1)} %get-tuple-element.38), channel_id=1, source_target_pairs={{0,24},{8,16},{16,8},{24,0},{1,25},{9,17},{17,9},{25,1},{2,26},{10... | collective-permute-start | bytes 196616 | tf_op jit(solution)/shard_map/ppermute | solution.py:76
  20.3 7.9 %collective-permute-start.8 = (bf16[128,1024]{1,0:T(8,128)(2,1)S(1)}, bf16[128,1024]{1,0:T(8,128)(2,1)S(1)}, u32[]{:S(2)}, u32[]{:S(2)}) collective-permute-start(bf16[128,1024]{1,0:T(8,128)(2,1)S(1)} %collective-permute-done.7.refs_2_), channel_id=1, source_target_pairs={{0,2},{2,6},{6,4},{4,0},{1,3},{3,7},{7,5},{5,1},{8,10},{10,14},{14... | collective-permute-start | bytes 786440 | tf_op jit(solution)/shard_map/ppermute | solution.py:40
  21.2 7.8 %collective-permute-start.6 = (bf16[128,512]{1,0:T(8,128)(2,1)S(1)}, bf16[128,512]{1,0:T(8,128)(2,1)S(1)}, u32[]{:S(2)}, u32[]{:S(2)}) collective-permute-start(bf16[128,512]{1,0:T(8,128)(2,1)S(1)} %get-tuple-element.35), channel_id=1, source_target_pairs={{0,1},{1,0},{2,3},{3,2},{4,5},{5,4},{6,7},{7,6},{8,9},{9,8},{10,11... | collective-permute-start | bytes 393224 | tf_op jit(solution)/shard_map/ppermute | solution.py:49
  21.2 11.3 %collective-permute-start.10 = (bf16[128,1024]{1,0:T(8,128)(2,1)S(1)}, bf16[128,1024]{1,0:T(8,128)(2,1)S(1)}, u32[]{:S(2)}, u32[]{:S(2)}) collective-permute-start(bf16[128,1024]{1,0:T(8,128)(2,1)S(1)} %pad_maximum_fusion.refs_0_), channel_id=1, source_target_pairs={{0,1},{1,0},{2,3},{3,2},{4,5},{5,4},{6,7},{7,6},{8,9},{9,8},{10,11... | collective-permute-start | bytes 786440 | tf_op jit(solution)/shard_map/ppermute | solution.py:49
  28.2 7.8 %collective-permute-start.13 = (bf16[128,1024]{1,0:T(8,128)(2,1)S(1)}, bf16[128,1024]{1,0:T(8,128)(2,1)S(1)}, u32[]{:S(2)}, u32[]{:S(2)}) collective-permute-start(bf16[128,1024]{1,0:T(8,128)(2,1)S(1)} %collective-permute-done.8.refs_4_), channel_id=1, source_target_pairs={{0,2},{2,6},{6,4},{4,0},{1,3},{3,7},{7,5},{5,1},{8,10},{10,14},{14... | collective-permute-start | bytes 786440 | tf_op jit(solution)/shard_map/ppermute | solution.py:40
  29.0 8.4 %collective-permute-start.17 = (bf16[256,256]{1,0:T(8,128)(2,1)S(1)}, bf16[256,256]{1,0:T(8,128)(2,1)S(1)}, u32[]{:S(2)}, u32[]{:S(2)}) collective-permute-start(bf16[256,256]{1,0:T(8,128)(2,1)S(1)} %get-tuple-element.28.refs_3_), channel_id=1, source_target_pairs={{0,2},{2,6},{6,4},{4,0},{1,3},{3,7},{7,5},{5,1},{8,10},{10,14},{14... | collective-permute-start | bytes 393224 | tf_op jit(solution)/shard_map/ppermute | solution.py:40
  32.4 6.4 %collective-permute-start.9 = (bf16[256,256]{1,0:T(8,128)(2,1)S(1)}, bf16[256,256]{1,0:T(8,128)(2,1)S(1)}, u32[]{:S(2)}, u32[]{:S(2)}) collective-permute-start(bf16[256,256]{1,0:T(8,128)(2,1)S(1)} %get-tuple-element.22.refs_3_), channel_id=1, source_target_pairs={{0,2},{2,6},{6,4},{4,0},{1,3},{3,7},{7,5},{5,1},{8,10},{10,14},{14... | collective-permute-start | bytes 393224 | tf_op jit(solution)/shard_map/ppermute | solution.py:40
  32.5 16.0 %collective-permute-start.11 = (bf16[128,1024]{1,0:T(8,128)(2,1)S(1)}, bf16[128,1024]{1,0:T(8,128)(2,1)S(1)}, u32[]{:S(2)}, u32[]{:S(2)}) collective-permute-start(bf16[128,1024]{1,0:T(8,128)(2,1)S(1)} %collective-permute-done.7.refs_2_), channel_id=1, source_target_pairs={{0,1},{1,0},{2,3},{3,2},{4,5},{5,4},{6,7},{7,6},{8,9},{9,8},{10,11... | collective-permute-start | bytes 786440 | tf_op jit(solution)/shard_map/ppermute | solution.py:49
  32.5 16.0 %collective-permute-start.12 = (bf16[128,1024]{1,0:T(8,128)(2,1)S(1)}, bf16[128,1024]{1,0:T(8,128)(2,1)S(1)}, u32[]{:S(2)}, u32[]{:S(2)}) collective-permute-start(bf16[128,1024]{1,0:T(8,128)(2,1)S(1)} %collective-permute-done.8.refs_4_), channel_id=1, source_target_pairs={{0,1},{1,0},{2,3},{3,2},{4,5},{5,4},{6,7},{7,6},{8,9},{9,8},{10,11... | collective-permute-start | bytes 786440 | tf_op jit(solution)/shard_map/ppermute | solution.py:49
  36.0 12.5 %collective-permute-start.14 = (bf16[128,1024]{1,0:T(8,128)(2,1)S(1)}, bf16[128,1024]{1,0:T(8,128)(2,1)S(1)}, u32[]{:S(2)}, u32[]{:S(2)}) collective-permute-start(bf16[128,1024]{1,0:T(8,128)(2,1)S(1)} %collective-permute-done.13.refs_6_), channel_id=1, source_target_pairs={{0,1},{1,0},{2,3},{3,2},{4,5},{5,4},{6,7},{7,6},{8,9},{9,8},{10,11... | collective-permute-start | bytes 786440 | tf_op jit(solution)/shard_map/ppermute | solution.py:49
  37.4 6.8 %collective-permute-start.18 = (bf16[256,256]{1,0:T(8,128)(2,1)S(1)}, bf16[256,256]{1,0:T(8,128)(2,1)S(1)}, u32[]{:S(2)}, u32[]{:S(2)}) collective-permute-start(bf16[256,256]{1,0:T(8,128)(2,1)S(1)} %collective-permute-done.17.refs_4_), channel_id=1, source_target_pairs={{0,2},{2,6},{6,4},{4,0},{1,3},{3,7},{7,5},{5,1},{8,10},{10,14},{14... | collective-permute-start | bytes 393224 | tf_op jit(solution)/shard_map/ppermute | solution.py:40
  38.8 7.6 %collective-permute-start.15 = (bf16[256,256]{1,0:T(8,128)(2,1)S(1)}, bf16[256,256]{1,0:T(8,128)(2,1)S(1)}, u32[]{:S(2)}, u32[]{:S(2)}) collective-permute-start(bf16[256,256]{1,0:T(8,128)(2,1)S(1)} %collective-permute-done.9.refs_4_), channel_id=1, source_target_pairs={{0,2},{2,6},{6,4},{4,0},{1,3},{3,7},{7,5},{5,1},{8,10},{10,14},{14... | collective-permute-start | bytes 393224 | tf_op jit(solution)/shard_map/ppermute | solution.py:40
  44.2 8.5 %collective-permute-start.19 = (bf16[256,256]{1,0:T(8,128)(2,1)S(1)}, bf16[256,256]{1,0:T(8,128)(2,1)S(1)}, u32[]{:S(2)}, u32[]{:S(2)}) collective-permute-start(bf16[256,256]{1,0:T(8,128)(2,1)S(1)} %collective-permute-done.18.refs_5_), channel_id=1, source_target_pairs={{0,2},{2,6},{6,4},{4,0},{1,3},{3,7},{7,5},{5,1},{8,10},{10,14},{14... | collective-permute-start | bytes 393224 | tf_op jit(solution)/shard_map/ppermute | solution.py:40
  46.5 13.2 %collective-permute-start.16 = (bf16[256,256]{1,0:T(8,128)(2,1)S(1)}, bf16[256,256]{1,0:T(8,128)(2,1)S(1)}, u32[]{:S(2)}, u32[]{:S(2)}) collective-permute-start(bf16[256,256]{1,0:T(8,128)(2,1)S(1)} %collective-permute-done.15.refs_5_), channel_id=1, source_target_pairs={{0,2},{2,6},{6,4},{4,0},{1,3},{3,7},{7,5},{5,1},{8,10},{10,14},{14... | collective-permute-start | bytes 393224 | tf_op jit(solution)/shard_map/ppermute | solution.py:40
  66.5 1.6 %collective-permute-start.21 = (f32[128,512]{1,0:T(8,128)S(1)}, f32[128,512]{1,0:T(8,128)S(1)}, u32[]{:S(2)}, u32[]{:S(2)}) collective-permute-start(f32[128,512]{1,0:T(8,128)S(1)} %get-tuple-element.32), channel_id=1, source_target_pairs={{0,1},{1,0},{2,3},{3,2},{4,5},{5,4},{6,7},{7,6},{8,9},{9,8},{10,11... | collective-permute-start | bytes 786440 | tf_op jit(solution)/shard_map/ppermute | solution.py:49
  66.6 1.9 %collective-permute-start.20 = (f32[128,512]{1,0:T(8,128)S(1)}, f32[128,512]{1,0:T(8,128)S(1)}, u32[]{:S(2)}, u32[]{:S(2)}) collective-permute-start(f32[128,512]{1,0:T(8,128)S(1)} %get-tuple-element.31), channel_id=1, source_target_pairs={{0,1},{1,0},{2,3},{3,2},{4,5},{5,4},{6,7},{7,6},{8,9},{9,8},{10,11... | collective-permute-start | bytes 786440 | tf_op jit(solution)/shard_map/ppermute | solution.py:49

commit v5 on v4

--- a/solution.py
+++ b/solution.py
@@ -11,7 +11,7 @@
 
 CHUNK = 256
 LIMIT = 32 * 1024 * 1024
-GRAM_COST = 1024
+GRAM_COST = 20_000_000_000
 SOLVE_COST = 1024
 
 
@@ -155,24 +155,21 @@
 
 
 def solve_kernel(shots, first, count, damping, *refs):
-    sources, refs = refs[: 3 + count], refs[3 + count :]
-    block, sent, start, image, step_high, step_low, step_image, high, low, rows_t, pieces, staged, arrived = refs[-13:]
+    high, low, rows_t, sources = refs[0], refs[1], refs[2], refs[3 : 3 + count]
+    block, sent, start, image, step_high, step_low, step_image, pieces, staged, arrived = refs[-10:]
     half, columns = start.shape[0] // 2, start.shape[1] // 2
-    targets = [high, low, rows_t] + [pieces.at[number] for number in range(count)]
-    copies = [pltpu.make_async_copy(sources[n], target, arrived.at[n]) for n, target in enumerate(targets)]
-    for copy in copies[3:] + copies[:3]:
+    copies = [pltpu.make_async_copy(source, pieces.at[n], arrived.at[n]) for n, source in enumerate(sources)]
+    for copy in copies:
         copy.start()
     tiles = [pl.ds(at, 256) for at in range(0, half, 256)]
     at = 0
     for number in range(count):
-        copies[3 + number].wait()
+        copies[number].wait()
         piece = pieces.at[number]
         for part in range(0, piece.shape[0], 2 * shots):
             real, imag = piece[pl.ds(part, shots), :], piece[pl.ds(part + shots, shots), :]
             fill_turned(start, pl.ds(at, shots), jnp.concatenate([real, imag], 1))
             at += shots
-    copies[0].wait()
-    copies[1].wait()
     damp = damping[...]
     norm_now = jnp.zeros((1, 2 * columns), jnp.float32)
     image_norm = jnp.zeros((1, 2 * columns), jnp.float32)
@@ -211,14 +208,13 @@
         weight_high, weight_low = two_parts(weight)
         fill_turned(step_high, tile, weight_high)
         fill_turned(step_low, tile, weight_low)
-    copies[2].wait()
     rows = rows_t.shape[0] // 2
     value = dot(rows_t[pl.ds(0, rows), :], step_high[...]) + dot(rows_t[pl.ds(0, rows), :], step_low[...])
     staged[:, 0, :] = value[:, :columns]
     staged[:, 1, :] = -value[:, columns:]
     offset = lax.axis_index("core") * (block.shape[2] // 2) + first
     copy = pltpu.make_async_copy(
-        staged, block.at[:, :, pl.ds(pl.multiple_of(offset, columns), columns)], arrived.at[len(targets)]
+        staged, block.at[:, :, pl.ds(pl.multiple_of(offset, columns), columns)], arrived.at[count]
     )
     copy.start()
     value = dot(rows_t[pl.ds(rows, rows), :], step_high[...]) + dot(rows_t[pl.ds(rows, rows), :], step_low[...])
@@ -237,7 +233,8 @@
             jax.ShapeDtypeStruct((rows, 2, width), jnp.float32),
             jax.ShapeDtypeStruct((rows, 2 * columns), jnp.float32),
         ),
-        in_specs=[pl.BlockSpec(memory_space=pltpu.VMEM)] + [pl.BlockSpec(memory_space=pltpu.HBM)] * (3 + count + len(earlier)),
+        in_specs=[pl.BlockSpec(memory_space=pltpu.VMEM)] * 4
+        + [pl.BlockSpec(memory_space=pltpu.HBM)] * (count + len(earlier)),
         out_specs=(pl.BlockSpec(memory_space=pltpu.HBM), pl.BlockSpec(memory_space=pltpu.VMEM)),
         input_output_aliases={4 + count: 0} if earlier else {},
         scratch_shapes=[
@@ -246,12 +243,9 @@
             pltpu.VMEM((size, 2 * columns), jnp.bfloat16),
             pltpu.VMEM((size, 2 * columns), jnp.bfloat16),
             pltpu.VMEM((half, 2 * columns), jnp.float32),
-            pltpu.VMEM(high.shape, jnp.bfloat16),
-            pltpu.VMEM(low.shape, jnp.bfloat16),
-            pltpu.VMEM(rows_t.shape, jnp.bfloat16),
             pltpu.VMEM((count,) + pieces[0].shape, jnp.bfloat16),
             pltpu.VMEM((rows, 2, columns), jnp.float32),
-            pltpu.SemaphoreType.DMA((4 + count,)),
+            pltpu.SemaphoreType.DMA((1 + count,)),
         ],
         compiler_params=pltpu.CompilerParams(vmem_limit_bytes=LIMIT),
         cost_estimate=pl.CostEstimate(flops=SOLVE_COST, bytes_accessed=1024, transcendentals=0),
@@ -373,14 +367,10 @@
         block = jnp.concatenate([jnp.where(first, kept, got), jnp.where(first, got, kept)], 2)
         return jnp.transpose(block, (1, 0, 2))[None]
 
-    early = ring_gather(up[:, :CHUNK], chips)
-    late = ring_gather(after(up[:, CHUNK:], own[2]), chips)
-    place = after(place, late[1])
+    gathered = ring_gather(up, chips)
     operator = gram_call(place, pieces, local_shots, rows)
-    early[0] = after(early[0], late[2])
-    block, sent_early = solve_call(*operator, early, local_shots, 0, None, width)
-    block, sent_late = solve_call(*operator, late, local_shots, CHUNK, block, width)
-    return place_call(block, [swap_core(sent_early), swap_core(sent_late)])[None]
+    block, sent = solve_call(*operator, gathered, local_shots, 0, None, width)
+    return place_call(block, [swap_core(sent)])[None]
 
 
 def solution(mesh):

time: 69.7 us -> 66.2 us (0.950)
  Pallas kernels: 18.9 us -> 15 us
  starting transfers between devices: 22.7 us -> 19.3 us
  matrix products: 3.95 us -> 6.02 us
  waiting for transfers between devices: 23.5 us -> 25.2 us
    pallas_call x2 -> x1, Pallas kernels: 13.8 us -> 9.78 us  [solve_call(): pl.pallas_call(functools.partial(solve_kernel, shots, first, count), out_...]
    ppermute x9 -> x6, starting transfers between devices: 13 us -> 10.5 us  [ring_gather(): pieces.append(lax.ppermute(pieces[-1], 'chip', pairs))]
    dot_general x2, matrix products: 3.95 us -> 6.02 us  [dot(): return jnp.dot(left, right, preferred_element_type=jnp.float32)]
    ppermute x7 -> x6, waiting for transfers between devices: 1.41 us -> 3.24 us  [swap_core(): return lax.ppermute(array, 'core', [(0, 1), (1, 0)])]
    ppermute x7 -> x6, starting transfers between devices: 1.65 us -> 0.66 us  [swap_core(): return lax.ppermute(array, 'core', [(0, 1), (1, 0)])]
    ppermute x9 -> x6, waiting for transfers between devices: 17.7 us -> 17.8 us  [ring_gather(): pieces.append(lax.ppermute(pieces[-1], 'chip', pairs))]
  transfers between devices with their start and end apart: 22 -> 18, of which waited for: 12 -> 12; matrix products, arithmetic and copies ran while one was open for 1% -> 5% of each run, Pallas kernels for 16% -> 6%
where the time goes in v5:
time: 66.2 us; the launch traced here: 66 us
  waiting for transfers between devices  25.2 us (38%)
  starting transfers between devices  19.3 us (29%)
  Pallas kernels  15 us (23%)
  matrix products  6.02 us (9%)
    ppermute x6, waiting for transfers between devices, ring_gather(): pieces.append(lax.ppermute(pieces[-1], 'chip', pairs))  17.8 us
    ppermute x6, starting transfers between devices, ring_gather(): pieces.append(lax.ppermute(pieces[-1], 'chip', pairs))  10.5 us
    pallas_call x1, Pallas kernels, solve_call(): pl.pallas_call(functools.partial(solve_kernel, shots, first, count), out_...  9.78 us
    ppermute x6, starting transfers between devices, to_freq(): lax.ppermute(part, 'freq', [(f, f ^ step) for f in range(nfreq)])  8.16 us
    dot_general x2, matrix products, dot(): return jnp.dot(left, right, preferred_element_type=jnp.float32)  6.02 us
    pallas_call x1, Pallas kernels, gram_call(): pl.pallas_call(functools.partial(gram_kernel, shots), out_shape=(block, b...  4.28 us
    ppermute x6, waiting for transfers between devices, to_freq(): lax.ppermute(part, 'freq', [(f, f ^ step) for f in range(nfreq)])  4.16 us
    ppermute x6, waiting for transfers between devices, swap_core(): return lax.ppermute(array, 'core', [(0, 1), (1, 0)])  3.24 us
  transfers between devices with their start and end apart: 18, of which 12 were waited for; matrix products, arithmetic and copies ran while one was open for 5% of the time, Pallas kernels for 6%

profile of v5, /device:TPU:0, one launch (start us, length us, event | category | flops | bytes accessed | tf_op | source)
XLA Modules:
  0.0 66.0 jit_solution(12495719947852980606)
XLA Ops:
  0.0 0.0 copy-start
  0.0 3.1 %convolution_convert_fusion.1 = bf16[128,1024]{1,0:T(8,128)(2,1)S(1)} fusion(bf16[128,2048]{1,0:T(8,128)(2,1)} %constant.44.clone, bf16[2048,1024]{1,0:T(8,128)(2,1)} %bitcast.27), kind=kOutput, calls=%fused_computation.1 | convolution fusion | flops 537001984 | bytes 4980736 | tf_op jit(solution)/shard_map/dot_general | solution.py:58
  3.2 4.0 %collective-permute-start.2 = (bf16[32,1024]{1,0:T(8,128)(2,1)S(1)}, bf16[32,1024]{1,0:T(8,128)(2,1)S(1)}, u32[]{:S(2)}, u32[]{:S(2)}) collective-permute-start(bf16[32,1024]{1,0:T(8,128)(2,1)S(1)} %get-tuple-element.30), channel_id=1, source_target_pairs={{0,24},{8,16},{16,8},{24,0},{1,25},{9,17},{17,9},{25,1},{2,26},{10... | collective-permute-start | bytes 196616 | tf_op jit(solution)/shard_map/ppermute | solution.py:76
  7.1 0.5 collective-permute-start.1
  7.7 0.1 collective-permute-start
  7.8 0.0 copy-done
  7.8 2.9 %convolution_convert_fusion = bf16[128,1024]{1,0:T(8,128)(2,1)S(1)} fusion(bf16[128,2048]{1,0:T(8,128)(2,1)S(1)} %copy-done, bf16[2048,1024]{1,0:T(8,128)(2,1)} %bitcast.28), kind=kOutput, calls=%fused_computation | convolution fusion | flops 537001984 | bytes 4980736 | tf_op jit(solution)/shard_map/dot_general | solution.py:58
  10.7 0.0 collective-permute-done.2
  10.7 0.7 %collective-permute-done.1 = bf16[32,1024]{1,0:T(8,128)(2,1)S(1)} collective-permute-done((bf16[32,1024]{1,0:T(8,128)(2,1)S(1)}, bf16[32,1024]{1,0:T(8,128)(2,1)S(1)}, u32[]{:S(2)}, u32[]{:S(2)}) %collective-permute-start.1) | collective-permute-done | bytes 65568 | tf_op jit(solution)/shard_map/ppermute | solution.py:76
  11.4 0.5 collective-permute-done
  11.9 1.6 %collective-permute-start.4 = (bf16[128,1024]{1,0:T(8,128)(2,1)S(1)}, bf16[128,1024]{1,0:T(8,128)(2,1)S(1)}, u32[]{:S(2)}, u32[]{:S(2)}) collective-permute-start(bf16[128,1024]{1,0:T(8,128)(2,1)S(1)} %pad_maximum_fusion.refs_0_), channel_id=1, source_target_pairs={{0,2},{2,6},{6,4},{4,0},{1,3},{3,7},{7,5},{5,1},{8,10},{10,14},{14... | collective-permute-start | bytes 786440 | tf_op jit(solution)/shard_map/ppermute | solution.py:40
  13.6 1.7 %collective-permute-start.12 = (bf16[32,1024]{1,0:T(8,128)(2,1)S(1)}, bf16[32,1024]{1,0:T(8,128)(2,1)S(1)}, u32[]{:S(2)}, u32[]{:S(2)}) collective-permute-start(bf16[32,1024]{1,0:T(8,128)(2,1)S(1)} %get-tuple-element.26), channel_id=1, source_target_pairs={{0,24},{8,16},{16,8},{24,0},{1,25},{9,17},{17,9},{25,1},{2,26},{10... | collective-permute-start | bytes 196616 | tf_op jit(solution)/shard_map/ppermute | solution.py:76
  15.3 0.5 collective-permute-start.11
  15.8 1.3 %collective-permute-start.10 = (bf16[32,1024]{1,0:T(8,128)(2,1)S(1)}, bf16[32,1024]{1,0:T(8,128)(2,1)S(1)}, u32[]{:S(2)}, u32[]{:S(2)}) collective-permute-start(bf16[32,1024]{1,0:T(8,128)(2,1)S(1)} %get-tuple-element.28), channel_id=1, source_target_pairs={{0,8},{8,0},{16,24},{24,16},{1,9},{9,1},{17,25},{25,17},{2,10},{10... | collective-permute-start | bytes 196616 | tf_op jit(solution)/shard_map/ppermute | solution.py:76
  17.1 1.8 %collective-permute-done.12 = bf16[32,1024]{1,0:T(8,128)(2,1)S(1)} collective-permute-done((bf16[32,1024]{1,0:T(8,128)(2,1)S(1)}, bf16[32,1024]{1,0:T(8,128)(2,1)S(1)}, u32[]{:S(2)}, u32[]{:S(2)}) %collective-permute-start.12) | collective-permute-done | bytes 65568 | tf_op jit(solution)/shard_map/ppermute | solution.py:76
  18.9 0.7 %collective-permute-done.11 = bf16[32,1024]{1,0:T(8,128)(2,1)S(1)} collective-permute-done((bf16[32,1024]{1,0:T(8,128)(2,1)S(1)}, bf16[32,1024]{1,0:T(8,128)(2,1)S(1)}, u32[]{:S(2)}, u32[]{:S(2)}) %collective-permute-start.11) | collective-permute-done | bytes 65568 | tf_op jit(solution)/shard_map/ppermute | solution.py:76
  19.6 0.5 collective-permute-done.10
  20.1 0.0 collective-permute-done.4.refs_2_
  20.1 2.6 %collective-permute-start.6 = (bf16[128,1024]{1,0:T(8,128)(2,1)S(1)}, bf16[128,1024]{1,0:T(8,128)(2,1)S(1)}, u32[]{:S(2)}, u32[]{:S(2)}) collective-permute-start(bf16[128,1024]{1,0:T(8,128)(2,1)S(1)} %collective-permute-done.4.refs_2_), channel_id=1, source_target_pairs={{0,2},{2,6},{6,4},{4,0},{1,3},{3,7},{7,5},{5,1},{8,10},{10,14},{14... | collective-permute-start | bytes 786440 | tf_op jit(solution)/shard_map/ppermute | solution.py:40
  22.8 0.1 collective-permute-start.13
  22.9 1.3 %collective-permute-done.13 = bf16[128,512]{1,0:T(8,128)(2,1)S(1)} collective-permute-done((bf16[128,512]{1,0:T(8,128)(2,1)S(1)}, bf16[128,512]{1,0:T(8,128)(2,1)S(1)}, u32[]{:S(2)}, u32[]{:S(2)}) %collective-permute-start.13) | collective-permute-done | bytes 131104 | tf_op jit(solution)/shard_map/ppermute | solution.py:49
  24.2 1.1 %collective-permute-start.14 = (bf16[256,512]{1,0:T(8,128)(2,1)S(1)}, bf16[256,512]{1,0:T(8,128)(2,1)S(1)}, u32[]{:S(2)}, u32[]{:S(2)}) collective-permute-start(bf16[256,512]{1,0:T(8,128)(2,1)S(1)} %pad_maximum_fusion.2.refs_3_), channel_id=1, source_target_pairs={{0,2},{2,6},{6,4},{4,0},{1,3},{3,7},{7,5},{5,1},{8,10},{10,14},{14... | collective-permute-start | bytes 786440 | tf_op jit(solution)/shard_map/ppermute | solution.py:40
  25.3 2.4 %collective-permute-done.6.refs_4_ = bf16[128,1024]{1,0:T(8,128)(2,1)S(1)} collective-permute-done((bf16[128,1024]{1,0:T(8,128)(2,1)S(1)}, bf16[128,1024]{1,0:T(8,128)(2,1)S(1)}, u32[]{:S(2)}, u32[]{:S(2)}) %collective-permute-start.6) | collective-permute-done | bytes 262176 | tf_op jit(solution)/shard_map/ppermute | solution.py:40
  27.7 2.5 %collective-permute-start.8 = (bf16[128,1024]{1,0:T(8,128)(2,1)S(1)}, bf16[128,1024]{1,0:T(8,128)(2,1)S(1)}, u32[]{:S(2)}, u32[]{:S(2)}) collective-permute-start(bf16[128,1024]{1,0:T(8,128)(2,1)S(1)} %collective-permute-done.6.refs_4_), channel_id=1, source_target_pairs={{0,2},{2,6},{6,4},{4,0},{1,3},{3,7},{7,5},{5,1},{8,10},{10,14},{14... | collective-permute-start | bytes 786440 | tf_op jit(solution)/shard_map/ppermute | solution.py:40
  30.2 4.2 %collective-permute-done.14.refs_4_ = bf16[256,512]{1,0:T(8,128)(2,1)S(1)} collective-permute-done((bf16[256,512]{1,0:T(8,128)(2,1)S(1)}, bf16[256,512]{1,0:T(8,128)(2,1)S(1)}, u32[]{:S(2)}, u32[]{:S(2)}) %collective-permute-start.14) | collective-permute-done | bytes 262176 | tf_op jit(solution)/shard_map/ppermute | solution.py:40
  34.3 1.5 %collective-permute-start.15 = (bf16[256,512]{1,0:T(8,128)(2,1)S(1)}, bf16[256,512]{1,0:T(8,128)(2,1)S(1)}, u32[]{:S(2)}, u32[]{:S(2)}) collective-permute-start(bf16[256,512]{1,0:T(8,128)(2,1)S(1)} %collective-permute-done.14.refs_4_), channel_id=1, source_target_pairs={{0,2},{2,6},{6,4},{4,0},{1,3},{3,7},{7,5},{5,1},{8,10},{10,14},{14... | collective-permute-start | bytes 786440 | tf_op jit(solution)/shard_map/ppermute | solution.py:40
  35.8 0.0 collective-permute-start.3
  35.8 0.5 collective-permute-start.5
  36.3 0.0 collective-permute-start.7
  36.3 3.6 %collective-permute-done.8.refs_6_ = bf16[128,1024]{1,0:T(8,128)(2,1)S(1)} collective-permute-done((bf16[128,1024]{1,0:T(8,128)(2,1)S(1)}, bf16[128,1024]{1,0:T(8,128)(2,1)S(1)}, u32[]{:S(2)}, u32[]{:S(2)}) %collective-permute-start.8) | collective-permute-done | bytes 262176 | tf_op jit(solution)/shard_map/ppermute | solution.py:40
  39.9 0.0 collective-permute-start.9
  39.9 0.1 add_add_fusion.place
  40.0 4.7 %collective-permute-done.15.refs_5_ = bf16[256,512]{1,0:T(8,128)(2,1)S(1)} collective-permute-done((bf16[256,512]{1,0:T(8,128)(2,1)S(1)}, bf16[256,512]{1,0:T(8,128)(2,1)S(1)}, u32[]{:S(2)}, u32[]{:S(2)}) %collective-permute-start.15) | collective-permute-done | bytes 262176 | tf_op jit(solution)/shard_map/ppermute | solution.py:40
  44.8 1.2 %collective-permute-start.16 = (bf16[256,512]{1,0:T(8,128)(2,1)S(1)}, bf16[256,512]{1,0:T(8,128)(2,1)S(1)}, u32[]{:S(2)}, u32[]{:S(2)}) collective-permute-start(bf16[256,512]{1,0:T(8,128)(2,1)S(1)} %collective-permute-done.15.refs_5_), channel_id=1, source_target_pairs={{0,2},{2,6},{6,4},{4,0},{1,3},{3,7},{7,5},{5,1},{8,10},{10,14},{14... | collective-permute-start | bytes 786440 | tf_op jit(solution)/shard_map/ppermute | solution.py:40
  46.0 0.0 collective-permute-done.3.refs_1_
  46.0 0.0 collective-permute-done.5.refs_3_
  46.0 0.0 collective-permute-done.7.refs_5_
  46.0 0.0 collective-permute-done.9.refs_7_
  46.0 4.3 %gram.1 = (bf16[512,1024]{1,0:T(8,128)(2,1)S(1)}, bf16[512,1024]{1,0:T(8,128)(2,1)S(1)}, f32[1,1]{1,0:T(1,128)}, bf16[256,1024]{1,0:T(8,128)(2,1)S(1)}) custom-call(s32[2]{0:T(128)S(1)} %add_add_fusion.place, bf16[128,1024]{1,0:T(8,128)(2,1)S(1)} %pad_maximum_fusion.refs_0_, bf16[128,1024]{1,0:T(8,128)(2,1)S(1)} %collective-permute-done.3.refs_1_, ...), custom_call_target="tpu_custom_call" | custom-call | flops 20000000000 | bytes 1024 | tf_op jit(solution)/shard_map/gram/pallas_call | solution.py:117
  50.3 2.9 %collective-permute-done.16.refs_6_ = bf16[256,512]{1,0:T(8,128)(2,1)S(1)} collective-permute-done((bf16[256,512]{1,0:T(8,128)(2,1)S(1)}, bf16[256,512]{1,0:T(8,128)(2,1)S(1)}, u32[]{:S(2)}, u32[]{:S(2)}) %collective-permute-start.16) | collective-permute-done | bytes 262176 | tf_op jit(solution)/shard_map/ppermute | solution.py:40
  53.2 9.8 %solve.1 = (f32[128,2,1024]{2,1,0:T(2,128)}, f32[128,1024]{1,0:T(8,128)S(1)}) custom-call(f32[1,1]{1,0:T(1,128)} %get-tuple-element.16.damping, bf16[512,1024]{1,0:T(8,128)(2,1)S(1)} %get-tuple-element.17.refs_0_, bf16[512,1024]{1,0:T(8,128)(2,1)S(1)} %get-tuple-element.18.refs_1_, bf16[256,1024]{1,0:T(8,128)(2,1)S(1)} %get-tuple-element.19.refs_2_, ...), custom_call_target="tpu_custom_call" | custom-call | flops 1024 | bytes 1024 | tf_op jit(solution)/shard_map/solve/pallas_call | solution.py:230
  63.0 0.1 collective-permute-start.17
  63.1 1.9 %collective-permute-done.17.refs_0_ = f32[128,1024]{1,0:T(8,128)S(1)} collective-permute-done((f32[128,1024]{1,0:T(8,128)S(1)}, f32[128,1024]{1,0:T(8,128)S(1)}, u32[]{:S(2)}, u32[]{:S(2)}) %collective-permute-start.17) | collective-permute-done | bytes 524320 | tf_op jit(solution)/shard_map/ppermute | solution.py:49
  65.0 0.9 %place.1 = f32[128,2,1024]{2,1,0:T(2,128)} custom-call(f32[128,2,1024]{2,1,0:T(2,128)} %get-tuple-element.21._, f32[128,1024]{1,0:T(8,128)S(1)} %collective-permute-done.17.refs_0_), custom_call_target="tpu_custom_call", output_to_operand_aliasing={{}: (0, {})} | custom-call | tf_op jit(solution)/shard_map/place/pallas_call | solution.py:275
  (6 shorter events, 0.1 us)
Async XLA Ops:
  0.0 7.8 %copy-start = (bf16[128,2048]{1,0:T(8,128)(2,1)S(1)}, bf16[128,2048]{1,0:T(8,128)(2,1)}, u32[]{:S(2)}) copy-start(bf16[128,2048]{1,0:T(8,128)(2,1)} %constant.44.clone) | copy-start | bytes 1572868
  3.2 7.5 %collective-permute-start.2 = (bf16[32,1024]{1,0:T(8,128)(2,1)S(1)}, bf16[32,1024]{1,0:T(8,128)(2,1)S(1)}, u32[]{:S(2)}, u32[]{:S(2)}) collective-permute-start(bf16[32,1024]{1,0:T(8,128)(2,1)S(1)} %get-tuple-element.30), channel_id=1, source_target_pairs={{0,24},{8,16},{16,8},{24,0},{1,25},{9,17},{17,9},{25,1},{2,26},{10... | collective-permute-start | bytes 196616 | tf_op jit(solution)/shard_map/ppermute | solution.py:76
  7.1 4.3 %collective-permute-start.1 = (bf16[32,1024]{1,0:T(8,128)(2,1)S(1)}, bf16[32,1024]{1,0:T(8,128)(2,1)S(1)}, u32[]{:S(2)}, u32[]{:S(2)}) collective-permute-start(bf16[32,1024]{1,0:T(8,128)(2,1)S(1)} %get-tuple-element.31), channel_id=1, source_target_pairs={{0,16},{8,24},{16,0},{24,8},{1,17},{9,25},{17,1},{25,9},{2,18},{10... | collective-permute-start | bytes 196616 | tf_op jit(solution)/shard_map/ppermute | solution.py:76
  7.7 4.3 %collective-permute-start = (bf16[32,1024]{1,0:T(8,128)(2,1)S(1)}, bf16[32,1024]{1,0:T(8,128)(2,1)S(1)}, u32[]{:S(2)}, u32[]{:S(2)}) collective-permute-start(bf16[32,1024]{1,0:T(8,128)(2,1)S(1)} %get-tuple-element.32), channel_id=1, source_target_pairs={{0,8},{8,0},{16,24},{24,16},{1,9},{9,1},{17,25},{25,17},{2,10},{10... | collective-permute-start | bytes 196616 | tf_op jit(solution)/shard_map/ppermute | solution.py:76
  11.9 8.2 %collective-permute-start.4 = (bf16[128,1024]{1,0:T(8,128)(2,1)S(1)}, bf16[128,1024]{1,0:T(8,128)(2,1)S(1)}, u32[]{:S(2)}, u32[]{:S(2)}) collective-permute-start(bf16[128,1024]{1,0:T(8,128)(2,1)S(1)} %pad_maximum_fusion.refs_0_), channel_id=1, source_target_pairs={{0,2},{2,6},{6,4},{4,0},{1,3},{3,7},{7,5},{5,1},{8,10},{10,14},{14... | collective-permute-start | bytes 786440 | tf_op jit(solution)/shard_map/ppermute | solution.py:40
  13.6 5.3 %collective-permute-start.12 = (bf16[32,1024]{1,0:T(8,128)(2,1)S(1)}, bf16[32,1024]{1,0:T(8,128)(2,1)S(1)}, u32[]{:S(2)}, u32[]{:S(2)}) collective-permute-start(bf16[32,1024]{1,0:T(8,128)(2,1)S(1)} %get-tuple-element.26), channel_id=1, source_target_pairs={{0,24},{8,16},{16,8},{24,0},{1,25},{9,17},{17,9},{25,1},{2,26},{10... | collective-permute-start | bytes 196616 | tf_op jit(solution)/shard_map/ppermute | solution.py:76
  15.3 4.3 %collective-permute-start.11 = (bf16[32,1024]{1,0:T(8,128)(2,1)S(1)}, bf16[32,1024]{1,0:T(8,128)(2,1)S(1)}, u32[]{:S(2)}, u32[]{:S(2)}) collective-permute-start(bf16[32,1024]{1,0:T(8,128)(2,1)S(1)} %get-tuple-element.27), channel_id=1, source_target_pairs={{0,16},{8,24},{16,0},{24,8},{1,17},{9,25},{17,1},{25,9},{2,18},{10... | collective-permute-start | bytes 196616 | tf_op jit(solution)/shard_map/ppermute | solution.py:76
  15.8 4.3 %collective-permute-start.10 = (bf16[32,1024]{1,0:T(8,128)(2,1)S(1)}, bf16[32,1024]{1,0:T(8,128)(2,1)S(1)}, u32[]{:S(2)}, u32[]{:S(2)}) collective-permute-start(bf16[32,1024]{1,0:T(8,128)(2,1)S(1)} %get-tuple-element.28), channel_id=1, source_target_pairs={{0,8},{8,0},{16,24},{24,16},{1,9},{9,1},{17,25},{25,17},{2,10},{10... | collective-permute-start | bytes 196616 | tf_op jit(solution)/shard_map/ppermute | solution.py:76
  20.1 7.6 %collective-permute-start.6 = (bf16[128,1024]{1,0:T(8,128)(2,1)S(1)}, bf16[128,1024]{1,0:T(8,128)(2,1)S(1)}, u32[]{:S(2)}, u32[]{:S(2)}) collective-permute-start(bf16[128,1024]{1,0:T(8,128)(2,1)S(1)} %collective-permute-done.4.refs_2_), channel_id=1, source_target_pairs={{0,2},{2,6},{6,4},{4,0},{1,3},{3,7},{7,5},{5,1},{8,10},{10,14},{14... | collective-permute-start | bytes 786440 | tf_op jit(solution)/shard_map/ppermute | solution.py:40
  22.8 1.4 %collective-permute-start.13 = (bf16[128,512]{1,0:T(8,128)(2,1)S(1)}, bf16[128,512]{1,0:T(8,128)(2,1)S(1)}, u32[]{:S(2)}, u32[]{:S(2)}) collective-permute-start(bf16[128,512]{1,0:T(8,128)(2,1)S(1)} %get-tuple-element.24), channel_id=1, source_target_pairs={{0,1},{1,0},{2,3},{3,2},{4,5},{5,4},{6,7},{7,6},{8,9},{9,8},{10,11... | collective-permute-start | bytes 393224 | tf_op jit(solution)/shard_map/ppermute | solution.py:49
  24.2 10.1 %collective-permute-start.14 = (bf16[256,512]{1,0:T(8,128)(2,1)S(1)}, bf16[256,512]{1,0:T(8,128)(2,1)S(1)}, u32[]{:S(2)}, u32[]{:S(2)}) collective-permute-start(bf16[256,512]{1,0:T(8,128)(2,1)S(1)} %pad_maximum_fusion.2.refs_3_), channel_id=1, source_target_pairs={{0,2},{2,6},{6,4},{4,0},{1,3},{3,7},{7,5},{5,1},{8,10},{10,14},{14... | collective-permute-start | bytes 786440 | tf_op jit(solution)/shard_map/ppermute | solution.py:40
  27.7 12.3 %collective-permute-start.8 = (bf16[128,1024]{1,0:T(8,128)(2,1)S(1)}, bf16[128,1024]{1,0:T(8,128)(2,1)S(1)}, u32[]{:S(2)}, u32[]{:S(2)}) collective-permute-start(bf16[128,1024]{1,0:T(8,128)(2,1)S(1)} %collective-permute-done.6.refs_4_), channel_id=1, source_target_pairs={{0,2},{2,6},{6,4},{4,0},{1,3},{3,7},{7,5},{5,1},{8,10},{10,14},{14... | collective-permute-start | bytes 786440 | tf_op jit(solution)/shard_map/ppermute | solution.py:40
  34.3 10.4 %collective-permute-start.15 = (bf16[256,512]{1,0:T(8,128)(2,1)S(1)}, bf16[256,512]{1,0:T(8,128)(2,1)S(1)}, u32[]{:S(2)}, u32[]{:S(2)}) collective-permute-start(bf16[256,512]{1,0:T(8,128)(2,1)S(1)} %collective-permute-done.14.refs_4_), channel_id=1, source_target_pairs={{0,2},{2,6},{6,4},{4,0},{1,3},{3,7},{7,5},{5,1},{8,10},{10,14},{14... | collective-permute-start | bytes 786440 | tf_op jit(solution)/shard_map/ppermute | solution.py:40
  35.8 10.2 %collective-permute-start.3 = (bf16[128,1024]{1,0:T(8,128)(2,1)S(1)}, bf16[128,1024]{1,0:T(8,128)(2,1)S(1)}, u32[]{:S(2)}, u32[]{:S(2)}) collective-permute-start(bf16[128,1024]{1,0:T(8,128)(2,1)S(1)} %pad_maximum_fusion.refs_0_), channel_id=1, source_target_pairs={{0,1},{1,0},{2,3},{3,2},{4,5},{5,4},{6,7},{7,6},{8,9},{9,8},{10,11... | collective-permute-start | bytes 786440 | tf_op jit(solution)/shard_map/ppermute | solution.py:49
  35.8 10.2 %collective-permute-start.5 = (bf16[128,1024]{1,0:T(8,128)(2,1)S(1)}, bf16[128,1024]{1,0:T(8,128)(2,1)S(1)}, u32[]{:S(2)}, u32[]{:S(2)}) collective-permute-start(bf16[128,1024]{1,0:T(8,128)(2,1)S(1)} %collective-permute-done.4.refs_2_), channel_id=1, source_target_pairs={{0,1},{1,0},{2,3},{3,2},{4,5},{5,4},{6,7},{7,6},{8,9},{9,8},{10,11... | collective-permute-start | bytes 786440 | tf_op jit(solution)/shard_map/ppermute | solution.py:49
  36.3 9.7 %collective-permute-start.7 = (bf16[128,1024]{1,0:T(8,128)(2,1)S(1)}, bf16[128,1024]{1,0:T(8,128)(2,1)S(1)}, u32[]{:S(2)}, u32[]{:S(2)}) collective-permute-start(bf16[128,1024]{1,0:T(8,128)(2,1)S(1)} %collective-permute-done.6.refs_4_), channel_id=1, source_target_pairs={{0,1},{1,0},{2,3},{3,2},{4,5},{5,4},{6,7},{7,6},{8,9},{9,8},{10,11... | collective-permute-start | bytes 786440 | tf_op jit(solution)/shard_map/ppermute | solution.py:49
  39.9 6.1 %collective-permute-start.9 = (bf16[128,1024]{1,0:T(8,128)(2,1)S(1)}, bf16[128,1024]{1,0:T(8,128)(2,1)S(1)}, u32[]{:S(2)}, u32[]{:S(2)}) collective-permute-start(bf16[128,1024]{1,0:T(8,128)(2,1)S(1)} %collective-permute-done.8.refs_6_), channel_id=1, source_target_pairs={{0,1},{1,0},{2,3},{3,2},{4,5},{5,4},{6,7},{7,6},{8,9},{9,8},{10,11... | collective-permute-start | bytes 786440 | tf_op jit(solution)/shard_map/ppermute | solution.py:49
  44.8 8.4 %collective-permute-start.16 = (bf16[256,512]{1,0:T(8,128)(2,1)S(1)}, bf16[256,512]{1,0:T(8,128)(2,1)S(1)}, u32[]{:S(2)}, u32[]{:S(2)}) collective-permute-start(bf16[256,512]{1,0:T(8,128)(2,1)S(1)} %collective-permute-done.15.refs_5_), channel_id=1, source_target_pairs={{0,2},{2,6},{6,4},{4,0},{1,3},{3,7},{7,5},{5,1},{8,10},{10,14},{14... | collective-permute-start | bytes 786440 | tf_op jit(solution)/shard_map/ppermute | solution.py:40
  63.0 2.0 %collective-permute-start.17 = (f32[128,1024]{1,0:T(8,128)S(1)}, f32[128,1024]{1,0:T(8,128)S(1)}, u32[]{:S(2)}, u32[]{:S(2)}) collective-permute-start(f32[128,1024]{1,0:T(8,128)S(1)} %get-tuple-element.22), channel_id=1, source_target_pairs={{0,1},{1,0},{2,3},{3,2},{4,5},{5,4},{6,7},{7,6},{8,9},{9,8},{10,11... | collective-permute-start | bytes 1572872 | tf_op jit(solution)/shard_map/ppermute | solution.py:49

commit v6 on v5

--- a/solution.py
+++ b/solution.py
@@ -11,8 +11,10 @@
 
 CHUNK = 256
 LIMIT = 32 * 1024 * 1024
-GRAM_COST = 20_000_000_000
+GRAM_COST = 1024
 SOLVE_COST = 1024
+KEEP_COST = 1_000_000_000
+STAGE_COST = 1024
 
 
 def make_table(samples, nfreq, first):
@@ -32,12 +34,13 @@
     return [0, 1, 3, 2] if chips == 4 else list(range(chips))
 
 
-def ring_gather(piece, chips):
+def ring_gather(piece, chips, *before_last):
     order = ring_order(chips)
     pairs = [(order[i], order[(i + 1) % chips]) for i in range(chips)]
     pieces = [piece]
-    for _ in range(chips - 1):
-        pieces.append(lax.ppermute(pieces[-1], "chip", pairs))
+    for step in range(1, chips):
+        piece = after(pieces[-1], *before_last) if step == chips - 1 and before_last else pieces[-1]
+        pieces.append(lax.ppermute(piece, "chip", pairs))
     return pieces
 
 
@@ -78,29 +81,24 @@
 
 
 def gram_kernel(shots, place, *refs):
-    sources, (high, low, damping, rows_t), (both, pieces, arrived) = refs[:-7], refs[-7:-3], refs[-3:]
-    count, width = sources[0].shape
-    half = both.shape[0] // 2
-    copies = [pltpu.make_async_copy(source, pieces.at[n], arrived.at[n]) for n, source in enumerate(sources)]
-    for copy in copies:
-        copy.start()
+    pieces, (high, low, damping, rows_t), both = refs[:-5], refs[-5:-1], refs[-1]
+    count, width = pieces[0].shape
     total = jnp.zeros((1, width), jnp.float32)
-    at = 0
-    for number, copy in enumerate(copies):
-        copy.wait()
-        piece = pieces.at[number]
+    for number, piece in enumerate(pieces):
+        at = number // 2 * 2 * count + number % 2 * (count // 2)
         for part in range(0, count, 2 * shots):
             real, imag = piece[pl.ds(part, shots), :], piece[pl.ds(part + shots, shots), :]
             both[pl.ds(at, shots), pl.ds(0, width)] = real
             both[pl.ds(at, shots), pl.ds(width, width)] = -imag
-            both[pl.ds(half + at, shots), pl.ds(0, width)] = imag
-            both[pl.ds(half + at, shots), pl.ds(width, width)] = real
+            both[pl.ds(count + at, shots), pl.ds(0, width)] = imag
+            both[pl.ds(count + at, shots), pl.ds(width, width)] = real
             real, imag = real.astype(jnp.float32), imag.astype(jnp.float32)
             total += jnp.sum(real * real + imag * imag, axis=0, keepdims=True)
             at += shots
     damping[...] = 0.1 * jnp.sum(total, axis=1, keepdims=True) / width
-    for at in range(0, half, 256):
-        gram = dot_nt(both[pl.ds(at, 256), :], both[...])
+    left = jnp.concatenate([both[pl.ds(at, count), :] for at in range(0, both.shape[0], 2 * count)], 0)
+    for at in range(0, left.shape[0], 256):
+        gram = dot_nt(left[at : at + 256], both[...])
         rounded = gram.astype(jnp.bfloat16)
         high[pl.ds(at, 256), :] = rounded
         low[pl.ds(at, 256), :] = (gram - rounded.astype(jnp.float32)).astype(jnp.bfloat16)
@@ -122,25 +120,29 @@
             jax.ShapeDtypeStruct((1, 1), jnp.float32),
             jax.ShapeDtypeStruct((2 * rows, size), jnp.bfloat16),
         ),
-        in_specs=[pl.BlockSpec(memory_space=pltpu.SMEM)] + [pl.BlockSpec(memory_space=pltpu.HBM)] * len(pieces),
+        in_specs=[pl.BlockSpec(memory_space=pltpu.SMEM)] + [pl.BlockSpec(memory_space=pltpu.VMEM)] * len(pieces),
         out_specs=(pl.BlockSpec(memory_space=pltpu.VMEM),) * 4,
-        scratch_shapes=[
-            pltpu.VMEM((size, 2 * width), jnp.bfloat16),
-            pltpu.VMEM((len(pieces), count, width), jnp.bfloat16),
-            pltpu.SemaphoreType.DMA((len(pieces),)),
-        ],
+        scratch_shapes=[pltpu.VMEM((size, 2 * width), jnp.bfloat16)],
         compiler_params=pltpu.CompilerParams(vmem_limit_bytes=LIMIT),
         cost_estimate=pl.CostEstimate(flops=GRAM_COST, bytes_accessed=1024, transcendentals=0),
         name="gram",
     )(place, *pieces)
 
 
-def fill_turned(target, tile, value):
-    half, columns = target.shape[0] // 2, target.shape[1] // 2
-    target[tile, :] = value
-    below = pl.ds(half + tile.start, tile.size)
-    target[below, pl.ds(0, columns)] = value[:, columns:]
-    target[below, pl.ds(columns, columns)] = -value[:, :columns]
+def fill_turned(target, at, below, value):
+    count, columns = value.shape[0], value.shape[1] // 2
+    target[pl.ds(at, count), :] = value
+    target[pl.ds(below, count), pl.ds(0, columns)] = value[:, columns:]
+    target[pl.ds(below, count), pl.ds(columns, columns)] = -value[:, :columns]
+
+
+def fill_piece(shots, source, first, target, number):
+    count, columns = source.shape[0], target.shape[1] // 2
+    at = number * count
+    for part in range(0, count, 2 * shots):
+        real, imag = (source[pl.ds(part + side, shots), pl.ds(first, columns)] for side in (0, shots))
+        fill_turned(target, at, at + count // 2, jnp.concatenate([real, imag], 1))
+        at += shots
 
 
 def per_column(total):
@@ -154,103 +156,216 @@
     return high, (value - high.astype(jnp.float32)).astype(jnp.bfloat16)
 
 
-def solve_kernel(shots, first, count, damping, *refs):
-    high, low, rows_t, sources = refs[0], refs[1], refs[2], refs[3 : 3 + count]
-    block, sent, start, image, step_high, step_low, step_image, pieces, staged, arrived = refs[-10:]
-    half, columns = start.shape[0] // 2, start.shape[1] // 2
-    copies = [pltpu.make_async_copy(source, pieces.at[n], arrived.at[n]) for n, source in enumerate(sources)]
-    for copy in copies:
-        copy.start()
-    tiles = [pl.ds(at, 256) for at in range(0, half, 256)]
-    at = 0
-    for number in range(count):
-        copies[number].wait()
-        piece = pieces.at[number]
-        for part in range(0, piece.shape[0], 2 * shots):
-            real, imag = piece[pl.ds(part, shots), :], piece[pl.ds(part + shots, shots), :]
-            fill_turned(start, pl.ds(at, shots), jnp.concatenate([real, imag], 1))
-            at += shots
+def taking_turns(*lists):
+    for number in range(max(len(steps) for steps in lists)):
+        for steps in lists:
+            if number < len(steps):
+                steps[number]()
+
+
+class Half:
+    def __init__(self, high, low, damping, early, earlier, late, image, step_high, step_low, step_image):
+        self.high, self.low, self.damping = high, low, damping
+        self.early, self.earlier, self.late, self.image = early, earlier, late, image
+        self.step_high, self.step_low, self.step_image = step_high, step_low, step_image
+        self.count, self.columns = late.shape[0] // 2, late.shape[1] // 2
+        self.blocks = range(high.shape[0] // self.count)
+        self.sums = [jnp.zeros((1, 2 * self.columns), jnp.float32) for _ in range(4)]
+
+    def rows(self, block):
+        return pl.ds(block * self.count, self.count)
+
+    def add(self, which, value):
+        self.sums[which] = self.sums[which] + jnp.sum(value, axis=0, keepdims=True)
+
+    def begin(self, block):
+        last = block == self.blocks[-1]
+        ref, at = (self.late, 0) if last else (self.early, 2 * block * self.count)
+        return ref[pl.ds(at, self.count), :].astype(jnp.float32)
+
+    def resid(self, block):
+        return self.keep * self.begin(block) - self.alpha * self.image[self.rows(block), :]
+
+    def store(self, block, value):
+        at = 2 * block * self.count
+        for target, part in zip((self.step_high, self.step_low), two_parts(value)):
+            fill_turned(target, at, at + self.count, part)
+
+    def apply_start(self):
+        columns = pl.ds(self.early.shape[0], 2 * self.count)
+
+        def step(block):
+            rows = self.rows(block)
+            value = self.earlier[rows, :] + (
+                dot(self.high[rows, columns], self.late[...]) + dot(self.low[rows, columns], self.late[...])
+            )
+            self.image[rows, :] = value
+            self.add(0, self.begin(block) * value)
+            self.add(1, value * value)
+
+        return [functools.partial(step, block) for block in self.blocks]
+
+    def take_step(self):
+        def scalars():
+            self.norm_now, image_norm = per_column(self.sums[0]), per_column(self.sums[1])
+            self.alpha = self.norm_now / (image_norm + self.damping * self.norm_now)
+            self.keep = 1.0 - self.alpha * self.damping
+
+        def step(block):
+            self.store(block, self.resid(block))
+
+        return [scalars] + [functools.partial(step, block) for block in self.blocks]
+
+    def apply_step(self):
+        def step(block):
+            rows = self.rows(block)
+            value = dot(self.high[rows, :], self.step_high[...]) + (
+                dot(self.low[rows, :], self.step_high[...]) + dot(self.high[rows, :], self.step_low[...])
+            )
+            self.step_image[rows, :] = value
+            self.add(2, self.resid(block) * value)
+
+        return [functools.partial(step, block) for block in self.blocks]
+
+    def weigh(self):
+        def scalars():
+            self.norm_next = per_column(self.sums[2])
+            self.ratio = self.norm_next / self.norm_now
+
+        def curvature(block):
+            rows = self.rows(block)
+            direc = self.resid(block) + self.ratio * self.begin(block)
+            value = self.step_image[rows, :] + self.ratio * self.image[rows, :]
+            self.add(3, value * (value + self.damping * direc))
+
+        def more_scalars():
+            beta = self.norm_next / per_column(self.sums[3])
+            self.from_start = self.alpha + beta * (self.keep + self.ratio)
+            self.from_image = self.alpha * beta
+
+        def step(block):
+            self.store(block, self.from_start * self.begin(block) - self.from_image * self.image[self.rows(block), :])
+
+        return (
+            [scalars]
+            + [functools.partial(curvature, block) for block in self.blocks]
+            + [more_scalars]
+            + [functools.partial(step, block) for block in self.blocks]
+        )
+
+
+def stage_kernel(shots, high, low, *refs):
+    sources, (early, earlier) = refs[:-2], refs[-2:]
+    columns, known = early.shape[2] // 2, pl.ds(0, early.shape[1])
+    for h in range(2):
+        for number, source in enumerate(sources):
+            fill_piece(shots, source, h * columns, early.at[h], number)
+    for h in range(2):
+        for at in range(0, high.shape[0], 128):
+            rows = pl.ds(at, 128)
+            earlier[h, rows, :] = dot(high[rows, known], early[h]) + dot(low[rows, known], early[h])
+
+
+def stage_call(high, low, pieces, shots):
+    half = high.shape[0]
+    rows, columns = pieces[0].shape
+    return pl.pallas_call(
+        functools.partial(stage_kernel, shots),
+        out_shape=(
+            jax.ShapeDtypeStruct((2, len(pieces) * rows, columns), jnp.bfloat16),
+            jax.ShapeDtypeStruct((2, half, columns), jnp.float32),
+        ),
+        in_specs=[pl.BlockSpec(memory_space=pltpu.VMEM)] * (2 + len(pieces)),
+        out_specs=(pl.BlockSpec(memory_space=pltpu.VMEM),) * 2,
+        compiler_params=pltpu.CompilerParams(vmem_limit_bytes=LIMIT),
+        cost_estimate=pl.CostEstimate(flops=STAGE_COST, bytes_accessed=1024, transcendentals=0),
+        name="stage",
+    )(high, low, *pieces)
+
+
+def solve_kernel(
+    shots, high, low, damping, rows_t, early, earlier, piece, sent, weights_high, weights_low, late, image, step_image
+):
+    columns = late.shape[2] // 2
     damp = damping[...]
-    norm_now = jnp.zeros((1, 2 * columns), jnp.float32)
-    image_norm = jnp.zeros((1, 2 * columns), jnp.float32)
-    for tile in tiles:
-        value = dot(high[tile, :], start[...]) + dot(low[tile, :], start[...])
-        image[tile, :] = value
-        norm_now += jnp.sum(start[tile, :].astype(jnp.float32) * value, axis=0, keepdims=True)
-        image_norm += jnp.sum(value * value, axis=0, keepdims=True)
-    norm_now, image_norm = per_column(norm_now), per_column(image_norm)
-    alpha = norm_now / (image_norm + damp * norm_now)
-    keep = 1.0 - alpha * damp
-    for tile in tiles:
-        resid_high, resid_low = two_parts(keep * start[tile, :].astype(jnp.float32) - alpha * image[tile, :])
-        fill_turned(step_high, tile, resid_high)
-        fill_turned(step_low, tile, resid_low)
-    norm_next = jnp.zeros((1, 2 * columns), jnp.float32)
-    for tile in tiles:
-        value = dot(high[tile, :], step_high[...]) + (
-            dot(low[tile, :], step_high[...]) + dot(high[tile, :], step_low[...])
+    one, two = (
+        Half(
+            high, low, damp, *(ref.at[h] for ref in (early, earlier, late, image, weights_high, weights_low, step_image))
         )
-        step_image[tile, :] = value
-        resid = keep * start[tile, :].astype(jnp.float32) - alpha * image[tile, :]
-        norm_next += jnp.sum(resid * value, axis=0, keepdims=True)
-    norm_next = per_column(norm_next)
-    ratio = norm_next / norm_now
-    curv = jnp.zeros((1, 2 * columns), jnp.float32)
-    for tile in tiles:
-        direc = (keep + ratio) * start[tile, :].astype(jnp.float32) - alpha * image[tile, :]
-        value = step_image[tile, :] + ratio * image[tile, :]
-        curv += jnp.sum(value * (value + damp * direc), axis=0, keepdims=True)
-    beta = norm_next / per_column(curv)
-    from_start = alpha + beta * (keep + ratio)
-    from_image = alpha * beta
-    for tile in tiles:
-        weight = from_start * start[tile, :].astype(jnp.float32) - from_image * image[tile, :]
-        weight_high, weight_low = two_parts(weight)
-        fill_turned(step_high, tile, weight_high)
-        fill_turned(step_low, tile, weight_low)
+        for h in range(2)
+    )
     rows = rows_t.shape[0] // 2
-    value = dot(rows_t[pl.ds(0, rows), :], step_high[...]) + dot(rows_t[pl.ds(0, rows), :], step_low[...])
-    staged[:, 0, :] = value[:, :columns]
-    staged[:, 1, :] = -value[:, columns:]
-    offset = lax.axis_index("core") * (block.shape[2] // 2) + first
-    copy = pltpu.make_async_copy(
-        staged, block.at[:, :, pl.ds(pl.multiple_of(offset, columns), columns)], arrived.at[count]
-    )
-    copy.start()
-    value = dot(rows_t[pl.ds(rows, rows), :], step_high[...]) + dot(rows_t[pl.ds(rows, rows), :], step_low[...])
-    sent[...] = jnp.concatenate([value[:, :columns], -value[:, columns:]], 1)
-    copy.wait()
-
-
-def solve_call(high, low, damping, rows_t, pieces, shots, first, block, width):
+
+    def project(h):
+        def step():
+            left = rows_t[pl.ds(rows, rows), :]
+            value = dot(left, weights_high[h]) + dot(left, weights_low[h])
+            sent[:, pl.ds(h * columns, columns)] = value[:, :columns]
+            sent[:, pl.ds((2 + h) * columns, columns)] = -value[:, columns:]
+
+        return [step]
+
+    fill_piece(shots, piece, 0, late.at[0], 0)
+    fill_piece(shots, piece, columns, late.at[1], 0)
+    taking_turns(one.apply_start())
+    taking_turns(two.apply_start(), one.take_step())
+    taking_turns(one.apply_step(), two.take_step())
+    taking_turns(two.apply_step(), one.weigh())
+    taking_turns(project(0), two.weigh())
+    taking_turns(project(1))
+
+
+def solve_call(high, low, damping, rows_t, early, earlier, piece, shots):
     half, size = high.shape
-    count, columns = len(pieces), pieces[0].shape[1]
+    count, columns = piece.shape[0], piece.shape[1] // 2
     rows = rows_t.shape[0] // 2
-    earlier = [] if block is None else [block]
+    weights = jax.ShapeDtypeStruct((2, size, 2 * columns), jnp.bfloat16)
     return pl.pallas_call(
-        functools.partial(solve_kernel, shots, first, count),
-        out_shape=(
-            jax.ShapeDtypeStruct((rows, 2, width), jnp.float32),
-            jax.ShapeDtypeStruct((rows, 2 * columns), jnp.float32),
-        ),
-        in_specs=[pl.BlockSpec(memory_space=pltpu.VMEM)] * 4
-        + [pl.BlockSpec(memory_space=pltpu.HBM)] * (count + len(earlier)),
-        out_specs=(pl.BlockSpec(memory_space=pltpu.HBM), pl.BlockSpec(memory_space=pltpu.VMEM)),
-        input_output_aliases={4 + count: 0} if earlier else {},
+        functools.partial(solve_kernel, shots),
+        out_shape=(jax.ShapeDtypeStruct((rows, 4 * columns), jnp.float32), weights, weights),
+        in_specs=[pl.BlockSpec(memory_space=pltpu.VMEM)] * 7,
+        out_specs=(pl.BlockSpec(memory_space=pltpu.VMEM),) * 3,
         scratch_shapes=[
-            pltpu.VMEM((size, 2 * columns), jnp.bfloat16),
-            pltpu.VMEM((half, 2 * columns), jnp.float32),
-            pltpu.VMEM((size, 2 * columns), jnp.bfloat16),
-            pltpu.VMEM((size, 2 * columns), jnp.bfloat16),
-            pltpu.VMEM((half, 2 * columns), jnp.float32),
-            pltpu.VMEM((count,) + pieces[0].shape, jnp.bfloat16),
-            pltpu.VMEM((rows, 2, columns), jnp.float32),
-            pltpu.SemaphoreType.DMA((1 + count,)),
+            pltpu.VMEM((2, count, 2 * columns), jnp.bfloat16),
+            pltpu.VMEM((2, half, 2 * columns), jnp.float32),
+            pltpu.VMEM((2, half, 2 * columns), jnp.float32),
         ],
         compiler_params=pltpu.CompilerParams(vmem_limit_bytes=LIMIT),
         cost_estimate=pl.CostEstimate(flops=SOLVE_COST, bytes_accessed=1024, transcendentals=0),
         name="solve",
-    )(damping, high, low, rows_t, *pieces, *earlier)
+    )(high, low, damping, rows_t, early, earlier, piece)
+
+
+def keep_kernel(rows_t, weights_high, weights_low, block, staged, arrived):
+    rows, columns = rows_t.shape[0] // 2, weights_high.shape[2] // 2
+    copies = []
+    for h in range(2):
+        left = rows_t[pl.ds(0, rows), :]
+        value = dot(left, weights_high[h]) + dot(left, weights_low[h])
+        staged[h, :, 0, :] = value[:, :columns]
+        staged[h, :, 1, :] = -value[:, columns:]
+        offset = lax.axis_index("core") * (block.shape[2] // 2) + h * columns
+        copy = pltpu.make_async_copy(
+            staged.at[h], block.at[:, :, pl.ds(pl.multiple_of(offset, columns), columns)], arrived.at[h]
+        )
+        copy.start()
+        copies.append(copy)
+    for copy in copies:
+        copy.wait()
+
+
+def keep_call(rows_t, weights_high, weights_low, width):
+    rows, columns = rows_t.shape[0] // 2, weights_high.shape[2] // 2
+    return pl.pallas_call(
+        keep_kernel,
+        out_shape=jax.ShapeDtypeStruct((rows, 2, width), jnp.float32),
+        in_specs=[pl.BlockSpec(memory_space=pltpu.VMEM)] * 3,
+        out_specs=pl.BlockSpec(memory_space=pltpu.HBM),
+        scratch_shapes=[pltpu.VMEM((2, rows, 2, columns), jnp.float32), pltpu.SemaphoreType.DMA((2,))],
+        compiler_params=pltpu.CompilerParams(vmem_limit_bytes=LIMIT),
+        cost_estimate=pl.CostEstimate(flops=KEEP_COST, bytes_accessed=1024, transcendentals=0),
+        name="keep",
+    )(rows_t, weights_high, weights_low)
 
 
 def place_kernel(_, *refs):
@@ -367,10 +482,12 @@
         block = jnp.concatenate([jnp.where(first, kept, got), jnp.where(first, got, kept)], 2)
         return jnp.transpose(block, (1, 0, 2))[None]
 
-    gathered = ring_gather(up, chips)
     operator = gram_call(place, pieces, local_shots, rows)
-    block, sent = solve_call(*operator, gathered, local_shots, 0, None, width)
-    return place_call(block, [swap_core(sent)])[None]
+    gathered = ring_gather(up, chips, operator[2])
+    early = stage_call(*operator[:2], gathered[:-1], local_shots)
+    sent, *weights = solve_call(*operator, *early, gathered[-1], local_shots)
+    got = swap_core(sent)
+    return place_call(keep_call(operator[3], *weights, width), [got])[None]
 
 
 def solution(mesh):

time: 66.2 us -> 63.5 us (0.959)
  starting transfers between devices: 19.3 us -> 17 us
  matrix products: 6.02 us -> 3.96 us
  waiting for transfers between devices: 25.2 us -> 26.3 us
  Pallas kernels: 15 us -> 15.7 us
    ppermute x6, waiting for transfers between devices: 17.8 us -> 22.5 us  [ring_gather(): pieces.append(lax.ppermute(piece, 'chip', pairs))]
    ppermute x6, waiting for transfers between devices: 3.24 us -> 0.34 us  [swap_core(): return lax.ppermute(array, 'core', [(0, 1), (1, 0)])]
    ppermute x6, starting transfers between devices: 10.5 us -> 8.2 us  [ring_gather(): pieces.append(lax.ppermute(piece, 'chip', pairs))]
    dot_general x2, matrix products: 6.02 us -> 3.96 us  [dot(): return jnp.dot(left, right, preferred_element_type=jnp.float32)]
    pallas_call x1 -> x3, Pallas kernels: 9.78 us -> 11 us  [the longest x1 7.6 us: solve_call(): pl.pallas_call(functools.partial(solve_kernel, shots), out_shape=(jax.Sha...]
    ppermute x6, waiting for transfers between devices: 4.16 us -> 3.38 us  [to_freq(): lax.ppermute(part, 'freq', [(f, f ^ step) for f in range(nfreq)])]
  transfers between devices with their start and end apart: 18 -> 18, of which waited for: 12 -> 10; matrix products, arithmetic and copies ran while one was open for 5% -> 1% of each run, Pallas kernels for 6% -> 11%
where the time goes in v6:
time: 63.5 us; the launch traced here: 63.4 us
  waiting for transfers between devices  26.3 us (41%)
  starting transfers between devices  17 us (27%)
  Pallas kernels  15.7 us (25%)
  matrix products  3.96 us (6%)
    ppermute x6, waiting for transfers between devices, ring_gather(): pieces.append(lax.ppermute(piece, 'chip', pairs))  22.5 us
    ppermute x6, starting transfers between devices, ring_gather(): pieces.append(lax.ppermute(piece, 'chip', pairs))  8.2 us
    ppermute x6, starting transfers between devices, to_freq(): lax.ppermute(part, 'freq', [(f, f ^ step) for f in range(nfreq)])  8.15 us
    pallas_call x1, Pallas kernels, solve_call(): pl.pallas_call(functools.partial(solve_kernel, shots), out_shape=(jax.Sha...  7.6 us
    dot_general x2, matrix products, dot(): return jnp.dot(left, right, preferred_element_type=jnp.float32)  3.96 us
    pallas_call x1, Pallas kernels, gram_call(): pl.pallas_call(functools.partial(gram_kernel, shots), out_shape=(block, b...  3.78 us
    ppermute x6, waiting for transfers between devices, to_freq(): lax.ppermute(part, 'freq', [(f, f ^ step) for f in range(nfreq)])  3.38 us
    pallas_call x1, Pallas kernels, stage_call(): pl.pallas_call(functools.partial(stage_kernel, shots), out_shape=(jax.Sha...  1.84 us
  transfers between devices with their start and end apart: 18, of which 10 were waited for; matrix products, arithmetic and copies ran while one was open for 1% of the time, Pallas kernels for 11%

profile of v6, /device:TPU:0, one launch (start us, length us, event | category | flops | bytes accessed | tf_op | source)
XLA Modules:
  0.0 63.4 jit_solution(5170632285234908700)
XLA Ops:
  0.0 0.0 copy-start.1
  0.0 0.0 copy-start
  0.0 3.2 %convolution_convert_fusion.1 = bf16[128,1024]{1,0:T(8,128)(2,1)S(1)} fusion(bf16[128,2048]{1,0:T(8,128)(2,1)} %constant.44.clone, bf16[2048,1024]{1,0:T(8,128)(2,1)} %bitcast.27), kind=kOutput, calls=%fused_computation.1 | convolution fusion | flops 537001984 | bytes 4980736 | tf_op jit(solution)/shard_map/dot_general | solution.py:61
  3.3 4.0 %collective-permute-start.2 = (bf16[32,1024]{1,0:T(8,128)(2,1)S(1)}, bf16[32,1024]{1,0:T(8,128)(2,1)S(1)}, u32[]{:S(2)}, u32[]{:S(2)}) collective-permute-start(bf16[32,1024]{1,0:T(8,128)(2,1)S(1)} %get-tuple-element.38), channel_id=1, source_target_pairs={{0,24},{8,16},{16,8},{24,0},{1,25},{9,17},{17,9},{25,1},{2,26},{10... | collective-permute-start | bytes 196616 | tf_op jit(solution)/shard_map/ppermute | solution.py:79
  7.2 0.5 collective-permute-start.1
  7.7 0.1 collective-permute-start
  7.9 0.0 copy-done.1
  7.9 0.0 copy-done
  7.9 0.7 %convolution_convert_fusion = bf16[128,1024]{1,0:T(8,128)(2,1)S(1)} fusion(bf16[128,2048]{1,0:T(8,128)(2,1)S(1)} %copy-done.1, bf16[2048,1024]{1,0:T(8,128)(2,1)S(1)} %bitcast.28), kind=kOutput, calls=%fused_computation | convolution fusion | flops 537001984 | bytes 4980736 | tf_op jit(solution)/shard_map/dot_general | solution.py:61
  8.6 0.8 %collective-permute-done.2 = bf16[32,1024]{1,0:T(8,128)(2,1)S(1)} collective-permute-done((bf16[32,1024]{1,0:T(8,128)(2,1)S(1)}, bf16[32,1024]{1,0:T(8,128)(2,1)S(1)}, u32[]{:S(2)}, u32[]{:S(2)}) %collective-permute-start.2) | collective-permute-done | bytes 65568 | tf_op jit(solution)/shard_map/ppermute | solution.py:79
  9.5 2.0 %collective-permute-done.1 = bf16[32,1024]{1,0:T(8,128)(2,1)S(1)} collective-permute-done((bf16[32,1024]{1,0:T(8,128)(2,1)S(1)}, bf16[32,1024]{1,0:T(8,128)(2,1)S(1)}, u32[]{:S(2)}, u32[]{:S(2)}) %collective-permute-start.1) | collective-permute-done | bytes 65568 | tf_op jit(solution)/shard_map/ppermute | solution.py:79
  11.5 0.5 collective-permute-done
  12.0 1.6 %collective-permute-start.4 = (bf16[128,1024]{1,0:T(8,128)(2,1)S(1)}, bf16[128,1024]{1,0:T(8,128)(2,1)S(1)}, u32[]{:S(2)}, u32[]{:S(2)}) collective-permute-start(bf16[128,1024]{1,0:T(8,128)(2,1)S(1)} %pad_maximum_fusion.refs_0_), channel_id=1, source_target_pairs={{0,2},{2,6},{6,4},{4,0},{1,3},{3,7},{7,5},{5,1},{8,10},{10,14},{14... | collective-permute-start | bytes 786440 | tf_op jit(solution)/shard_map/ppermute | solution.py:43
  13.7 1.6 %collective-permute-start.12 = (bf16[32,1024]{1,0:T(8,128)(2,1)S(1)}, bf16[32,1024]{1,0:T(8,128)(2,1)S(1)}, u32[]{:S(2)}, u32[]{:S(2)}) collective-permute-start(bf16[32,1024]{1,0:T(8,128)(2,1)S(1)} %get-tuple-element.34), channel_id=1, source_target_pairs={{0,24},{8,16},{16,8},{24,0},{1,25},{9,17},{17,9},{25,1},{2,26},{10... | collective-permute-start | bytes 196616 | tf_op jit(solution)/shard_map/ppermute | solution.py:79
  15.2 0.5 collective-permute-start.11
  15.7 1.5 %collective-permute-start.10 = (bf16[32,1024]{1,0:T(8,128)(2,1)S(1)}, bf16[32,1024]{1,0:T(8,128)(2,1)S(1)}, u32[]{:S(2)}, u32[]{:S(2)}) collective-permute-start(bf16[32,1024]{1,0:T(8,128)(2,1)S(1)} %get-tuple-element.36), channel_id=1, source_target_pairs={{0,8},{8,0},{16,24},{24,16},{1,9},{9,1},{17,25},{25,17},{2,10},{10... | collective-permute-start | bytes 196616 | tf_op jit(solution)/shard_map/ppermute | solution.py:79
  17.2 2.5 %collective-permute-done.4.refs_2_ = bf16[128,1024]{1,0:T(8,128)(2,1)S(1)} collective-permute-done((bf16[128,1024]{1,0:T(8,128)(2,1)S(1)}, bf16[128,1024]{1,0:T(8,128)(2,1)S(1)}, u32[]{:S(2)}, u32[]{:S(2)}) %collective-permute-start.4) | collective-permute-done | bytes 262176 | tf_op jit(solution)/shard_map/ppermute | solution.py:43
  19.7 0.8 %collective-permute-start.6 = (bf16[128,1024]{1,0:T(8,128)(2,1)S(1)}, bf16[128,1024]{1,0:T(8,128)(2,1)S(1)}, u32[]{:S(2)}, u32[]{:S(2)}) collective-permute-start(bf16[128,1024]{1,0:T(8,128)(2,1)S(1)} %collective-permute-done.4.refs_2_), channel_id=1, source_target_pairs={{0,2},{2,6},{6,4},{4,0},{1,3},{3,7},{7,5},{5,1},{8,10},{10,14},{14... | collective-permute-start | bytes 786440 | tf_op jit(solution)/shard_map/ppermute | solution.py:43
  20.5 0.0 collective-permute-done.12
  20.5 0.0 collective-permute-done.11
  20.5 0.0 collective-permute-done.10
  20.6 0.1 collective-permute-start.13
  20.6 6.3 %collective-permute-done.6.refs_4_ = bf16[128,1024]{1,0:T(8,128)(2,1)S(1)} collective-permute-done((bf16[128,1024]{1,0:T(8,128)(2,1)S(1)}, bf16[128,1024]{1,0:T(8,128)(2,1)S(1)}, u32[]{:S(2)}, u32[]{:S(2)}) %collective-permute-start.6) | collective-permute-done | bytes 262176 | tf_op jit(solution)/shard_map/ppermute | solution.py:43
  27.0 0.8 %collective-permute-start.8 = (bf16[128,1024]{1,0:T(8,128)(2,1)S(1)}, bf16[128,1024]{1,0:T(8,128)(2,1)S(1)}, u32[]{:S(2)}, u32[]{:S(2)}) collective-permute-start(bf16[128,1024]{1,0:T(8,128)(2,1)S(1)} %collective-permute-done.6.refs_4_), channel_id=1, source_target_pairs={{0,2},{2,6},{6,4},{4,0},{1,3},{3,7},{7,5},{5,1},{8,10},{10,14},{14... | collective-permute-start | bytes 786440 | tf_op jit(solution)/shard_map/ppermute | solution.py:43
  27.8 0.0 collective-permute-done.13
  27.8 3.4 %collective-permute-start.14 = (bf16[256,512]{1,0:T(8,128)(2,1)S(1)}, bf16[256,512]{1,0:T(8,128)(2,1)S(1)}, u32[]{:S(2)}, u32[]{:S(2)}) collective-permute-start(bf16[256,512]{1,0:T(8,128)(2,1)S(1)} %pad_maximum_fusion.2.refs_0_), channel_id=1, source_target_pairs={{0,2},{2,6},{6,4},{4,0},{1,3},{3,7},{7,5},{5,1},{8,10},{10,14},{14... | collective-permute-start | bytes 786440 | tf_op jit(solution)/shard_map/ppermute | solution.py:43
  31.2 0.0 collective-permute-start.3
  31.2 0.5 collective-permute-start.5
  31.7 0.0 collective-permute-start.7
  31.7 3.7 %collective-permute-done.8.refs_6_ = bf16[128,1024]{1,0:T(8,128)(2,1)S(1)} collective-permute-done((bf16[128,1024]{1,0:T(8,128)(2,1)S(1)}, bf16[128,1024]{1,0:T(8,128)(2,1)S(1)}, u32[]{:S(2)}, u32[]{:S(2)}) %collective-permute-start.8) | collective-permute-done | bytes 262176 | tf_op jit(solution)/shard_map/ppermute | solution.py:43
  35.4 0.0 collective-permute-start.9
  35.4 2.8 %collective-permute-done.14.refs_1_ = bf16[256,512]{1,0:T(8,128)(2,1)S(1)} collective-permute-done((bf16[256,512]{1,0:T(8,128)(2,1)S(1)}, bf16[256,512]{1,0:T(8,128)(2,1)S(1)}, u32[]{:S(2)}, u32[]{:S(2)}) %collective-permute-start.14) | collective-permute-done | bytes 262176 | tf_op jit(solution)/shard_map/ppermute | solution.py:43
  38.2 0.8 %collective-permute-start.15 = (bf16[256,512]{1,0:T(8,128)(2,1)S(1)}, bf16[256,512]{1,0:T(8,128)(2,1)S(1)}, u32[]{:S(2)}, u32[]{:S(2)}) collective-permute-start(bf16[256,512]{1,0:T(8,128)(2,1)S(1)} %collective-permute-done.14.refs_1_), channel_id=1, source_target_pairs={{0,2},{2,6},{6,4},{4,0},{1,3},{3,7},{7,5},{5,1},{8,10},{10,14},{14... | collective-permute-start | bytes 786440 | tf_op jit(solution)/shard_map/ppermute | solution.py:43
  39.0 0.1 add_add_fusion.place
  39.1 0.0 collective-permute-done.3.refs_1_
  39.1 0.0 collective-permute-done.5.refs_3_
  39.1 0.0 collective-permute-done.7.refs_5_
  39.1 0.0 collective-permute-done.9.refs_7_
  39.1 3.8 %gram.1 = (bf16[512,1024]{1,0:T(8,128)(2,1)S(1)}, bf16[512,1024]{1,0:T(8,128)(2,1)S(1)}, f32[1,1]{1,0:T(1,128)}, bf16[256,1024]{1,0:T(8,128)(2,1)S(1)}) custom-call(s32[2]{0:T(128)S(1)} %add_add_fusion.place, bf16[128,1024]{1,0:T(8,128)(2,1)S(1)} %pad_maximum_fusion.refs_0_, bf16[128,1024]{1,0:T(8,128)(2,1)S(1)} %collective-permute-done.3.refs_1_, ...), custom_call_target="tpu_custom_call" | custom-call | flops 1024 | bytes 1024 | tf_op jit(solution)/shard_map/gram/pallas_call | solution.py:115
  42.9 2.6 %collective-permute-done.15.refs_2_ = bf16[256,512]{1,0:T(8,128)(2,1)S(1)} collective-permute-done((bf16[256,512]{1,0:T(8,128)(2,1)S(1)}, bf16[256,512]{1,0:T(8,128)(2,1)S(1)}, u32[]{:S(2)}, u32[]{:S(2)}) %collective-permute-start.15) | collective-permute-done | bytes 262176 | tf_op jit(solution)/shard_map/ppermute | solution.py:43
  45.5 0.8 %collective-permute-start.16 = (bf16[256,512]{1,0:T(8,128)(2,1)S(1)}, bf16[256,512]{1,0:T(8,128)(2,1)S(1)}, u32[]{:S(2)}, u32[]{:S(2)}) collective-permute-start(bf16[256,512]{1,0:T(8,128)(2,1)S(1)} %collective-permute-done.15.refs_2_), channel_id=1, source_target_pairs={{0,2},{2,6},{6,4},{4,0},{1,3},{3,7},{7,5},{5,1},{8,10},{10,14},{14... | collective-permute-start | bytes 786440 | tf_op jit(solution)/shard_map/ppermute | solution.py:43
  46.3 1.8 %stage.1 = (bf16[2,768,512]{2,1,0:T(8,128)(2,1)S(1)}, f32[2,512,512]{2,1,0:T(8,128)S(1)}) custom-call(bf16[512,1024]{1,0:T(8,128)(2,1)S(1)} %get-tuple-element.21.high, bf16[512,1024]{1,0:T(8,128)(2,1)S(1)} %get-tuple-element.22.low, bf16[256,512]{1,0:T(8,128)(2,1)S(1)} %pad_maximum_fusion.2.refs_0_, bf16[256,512]{1,0:T(8,128)(2,1)S(1)} %collective-permute-done.14.refs_1_, ...), custom_call_target="tpu_custom_call" | custom-call | flops 1024 | bytes 1024 | tf_op jit(solution)/shard_map/stage/pallas_call | solution.py:272
  48.1 4.6 %collective-permute-done.16.piece = bf16[256,512]{1,0:T(8,128)(2,1)S(1)} collective-permute-done((bf16[256,512]{1,0:T(8,128)(2,1)S(1)}, bf16[256,512]{1,0:T(8,128)(2,1)S(1)}, u32[]{:S(2)}, u32[]{:S(2)}) %collective-permute-start.16) | collective-permute-done | bytes 262176 | tf_op jit(solution)/shard_map/ppermute | solution.py:43
  52.8 7.6 %solve.1 = (f32[128,1024]{1,0:T(8,128)S(1)}, bf16[2,1024,512]{2,1,0:T(8,128)(2,1)S(1)}, bf16[2,1024,512]{2,1,0:T(8,128)(2,1)S(1)}) custom-call(bf16[512,1024]{1,0:T(8,128)(2,1)S(1)} %get-tuple-element.21.high, bf16[512,1024]{1,0:T(8,128)(2,1)S(1)} %get-tuple-element.22.low, f32[1,1]{1,0:T(1,128)} %get-tuple-element.23.damping, ...), custom_call_target="tpu_custom_call" | custom-call | flops 1024 | bytes 1024 | tf_op jit(solution)/shard_map/solve/pallas_call | solution.py:323
  60.4 0.1 collective-permute-start.17
  60.4 1.6 %keep.1._ = f32[128,2,1024]{2,1,0:T(2,128)} custom-call(bf16[256,1024]{1,0:T(8,128)(2,1)S(1)} %get-tuple-element.20.rows_t, bf16[2,1024,512]{2,1,0:T(8,128)(2,1)S(1)} %get-tuple-element.28.weights_high, bf16[2,1024,512]{2,1,0:T(8,128)(2,1)S(1)} %get-tuple-element.29.weights_low), custom_call_target="tpu_custom_call" | custom-call | flops 1000000000 | bytes 1024 | tf_op jit(solution)/shard_map/keep/pallas_call | solution.py:359
  62.0 0.3 collective-permute-done.17.refs_0_
  62.3 0.9 %place.1 = f32[128,2,1024]{2,1,0:T(2,128)} custom-call(f32[128,2,1024]{2,1,0:T(2,128)} %keep.1._, f32[128,1024]{1,0:T(8,128)S(1)} %collective-permute-done.17.refs_0_), custom_call_target="tpu_custom_call", output_to_operand_aliasing={{}: (0, {})} | custom-call | tf_op jit(solution)/shard_map/place/pallas_call | solution.py:390
  (6 shorter events, 0.1 us)
Async XLA Ops:
  0.0 7.9 %copy-start.1 = (bf16[128,2048]{1,0:T(8,128)(2,1)S(1)}, bf16[128,2048]{1,0:T(8,128)(2,1)}, u32[]{:S(2)}) copy-start(bf16[128,2048]{1,0:T(8,128)(2,1)} %constant.44.clone) | copy-start | bytes 1572868
  0.0 7.9 %copy-start = (bf16[16,128,1024]{2,1,0:T(8,128)(2,1)S(1)}, bf16[16,128,1024]{2,1,0:T(8,128)(2,1)}, u32[]{:S(2)}) copy-start(bf16[16,128,1024]{2,1,0:T(8,128)(2,1)} %param.3) | copy-start | bytes 12582916
  3.3 6.2 %collective-permute-start.2 = (bf16[32,1024]{1,0:T(8,128)(2,1)S(1)}, bf16[32,1024]{1,0:T(8,128)(2,1)S(1)}, u32[]{:S(2)}, u32[]{:S(2)}) collective-permute-start(bf16[32,1024]{1,0:T(8,128)(2,1)S(1)} %get-tuple-element.38), channel_id=1, source_target_pairs={{0,24},{8,16},{16,8},{24,0},{1,25},{9,17},{17,9},{25,1},{2,26},{10... | collective-permute-start | bytes 196616 | tf_op jit(solution)/shard_map/ppermute | solution.py:79
  7.2 4.3 %collective-permute-start.1 = (bf16[32,1024]{1,0:T(8,128)(2,1)S(1)}, bf16[32,1024]{1,0:T(8,128)(2,1)S(1)}, u32[]{:S(2)}, u32[]{:S(2)}) collective-permute-start(bf16[32,1024]{1,0:T(8,128)(2,1)S(1)} %get-tuple-element.39), channel_id=1, source_target_pairs={{0,16},{8,24},{16,0},{24,8},{1,17},{9,25},{17,1},{25,9},{2,18},{10... | collective-permute-start | bytes 196616 | tf_op jit(solution)/shard_map/ppermute | solution.py:79
  7.7 4.3 %collective-permute-start = (bf16[32,1024]{1,0:T(8,128)(2,1)S(1)}, bf16[32,1024]{1,0:T(8,128)(2,1)S(1)}, u32[]{:S(2)}, u32[]{:S(2)}) collective-permute-start(bf16[32,1024]{1,0:T(8,128)(2,1)S(1)} %get-tuple-element.40), channel_id=1, source_target_pairs={{0,8},{8,0},{16,24},{24,16},{1,9},{9,1},{17,25},{25,17},{2,10},{10... | collective-permute-start | bytes 196616 | tf_op jit(solution)/shard_map/ppermute | solution.py:79
  12.0 7.7 %collective-permute-start.4 = (bf16[128,1024]{1,0:T(8,128)(2,1)S(1)}, bf16[128,1024]{1,0:T(8,128)(2,1)S(1)}, u32[]{:S(2)}, u32[]{:S(2)}) collective-permute-start(bf16[128,1024]{1,0:T(8,128)(2,1)S(1)} %pad_maximum_fusion.refs_0_), channel_id=1, source_target_pairs={{0,2},{2,6},{6,4},{4,0},{1,3},{3,7},{7,5},{5,1},{8,10},{10,14},{14... | collective-permute-start | bytes 786440 | tf_op jit(solution)/shard_map/ppermute | solution.py:43
  13.7 6.8 %collective-permute-start.12 = (bf16[32,1024]{1,0:T(8,128)(2,1)S(1)}, bf16[32,1024]{1,0:T(8,128)(2,1)S(1)}, u32[]{:S(2)}, u32[]{:S(2)}) collective-permute-start(bf16[32,1024]{1,0:T(8,128)(2,1)S(1)} %get-tuple-element.34), channel_id=1, source_target_pairs={{0,24},{8,16},{16,8},{24,0},{1,25},{9,17},{17,9},{25,1},{2,26},{10... | collective-permute-start | bytes 196616 | tf_op jit(solution)/shard_map/ppermute | solution.py:79
  15.2 5.3 %collective-permute-start.11 = (bf16[32,1024]{1,0:T(8,128)(2,1)S(1)}, bf16[32,1024]{1,0:T(8,128)(2,1)S(1)}, u32[]{:S(2)}, u32[]{:S(2)}) collective-permute-start(bf16[32,1024]{1,0:T(8,128)(2,1)S(1)} %get-tuple-element.35), channel_id=1, source_target_pairs={{0,16},{8,24},{16,0},{24,8},{1,17},{9,25},{17,1},{25,9},{2,18},{10... | collective-permute-start | bytes 196616 | tf_op jit(solution)/shard_map/ppermute | solution.py:79
  15.7 4.8 %collective-permute-start.10 = (bf16[32,1024]{1,0:T(8,128)(2,1)S(1)}, bf16[32,1024]{1,0:T(8,128)(2,1)S(1)}, u32[]{:S(2)}, u32[]{:S(2)}) collective-permute-start(bf16[32,1024]{1,0:T(8,128)(2,1)S(1)} %get-tuple-element.36), channel_id=1, source_target_pairs={{0,8},{8,0},{16,24},{24,16},{1,9},{9,1},{17,25},{25,17},{2,10},{10... | collective-permute-start | bytes 196616 | tf_op jit(solution)/shard_map/ppermute | solution.py:79
  19.7 7.3 %collective-permute-start.6 = (bf16[128,1024]{1,0:T(8,128)(2,1)S(1)}, bf16[128,1024]{1,0:T(8,128)(2,1)S(1)}, u32[]{:S(2)}, u32[]{:S(2)}) collective-permute-start(bf16[128,1024]{1,0:T(8,128)(2,1)S(1)} %collective-permute-done.4.refs_2_), channel_id=1, source_target_pairs={{0,2},{2,6},{6,4},{4,0},{1,3},{3,7},{7,5},{5,1},{8,10},{10,14},{14... | collective-permute-start | bytes 786440 | tf_op jit(solution)/shard_map/ppermute | solution.py:43
  20.6 7.2 %collective-permute-start.13 = (bf16[128,512]{1,0:T(8,128)(2,1)S(1)}, bf16[128,512]{1,0:T(8,128)(2,1)S(1)}, u32[]{:S(2)}, u32[]{:S(2)}) collective-permute-start(bf16[128,512]{1,0:T(8,128)(2,1)S(1)} %get-tuple-element.32), channel_id=1, source_target_pairs={{0,1},{1,0},{2,3},{3,2},{4,5},{5,4},{6,7},{7,6},{8,9},{9,8},{10,11... | collective-permute-start | bytes 393224 | tf_op jit(solution)/shard_map/ppermute | solution.py:52
  27.0 8.4 %collective-permute-start.8 = (bf16[128,1024]{1,0:T(8,128)(2,1)S(1)}, bf16[128,1024]{1,0:T(8,128)(2,1)S(1)}, u32[]{:S(2)}, u32[]{:S(2)}) collective-permute-start(bf16[128,1024]{1,0:T(8,128)(2,1)S(1)} %collective-permute-done.6.refs_4_), channel_id=1, source_target_pairs={{0,2},{2,6},{6,4},{4,0},{1,3},{3,7},{7,5},{5,1},{8,10},{10,14},{14... | collective-permute-start | bytes 786440 | tf_op jit(solution)/shard_map/ppermute | solution.py:43
  27.8 10.4 %collective-permute-start.14 = (bf16[256,512]{1,0:T(8,128)(2,1)S(1)}, bf16[256,512]{1,0:T(8,128)(2,1)S(1)}, u32[]{:S(2)}, u32[]{:S(2)}) collective-permute-start(bf16[256,512]{1,0:T(8,128)(2,1)S(1)} %pad_maximum_fusion.2.refs_0_), channel_id=1, source_target_pairs={{0,2},{2,6},{6,4},{4,0},{1,3},{3,7},{7,5},{5,1},{8,10},{10,14},{14... | collective-permute-start | bytes 786440 | tf_op jit(solution)/shard_map/ppermute | solution.py:43
  31.2 7.9 %collective-permute-start.3 = (bf16[128,1024]{1,0:T(8,128)(2,1)S(1)}, bf16[128,1024]{1,0:T(8,128)(2,1)S(1)}, u32[]{:S(2)}, u32[]{:S(2)}) collective-permute-start(bf16[128,1024]{1,0:T(8,128)(2,1)S(1)} %pad_maximum_fusion.refs_0_), channel_id=1, source_target_pairs={{0,1},{1,0},{2,3},{3,2},{4,5},{5,4},{6,7},{7,6},{8,9},{9,8},{10,11... | collective-permute-start | bytes 786440 | tf_op jit(solution)/shard_map/ppermute | solution.py:52
  31.2 7.9 %collective-permute-start.5 = (bf16[128,1024]{1,0:T(8,128)(2,1)S(1)}, bf16[128,1024]{1,0:T(8,128)(2,1)S(1)}, u32[]{:S(2)}, u32[]{:S(2)}) collective-permute-start(bf16[128,1024]{1,0:T(8,128)(2,1)S(1)} %collective-permute-done.4.refs_2_), channel_id=1, source_target_pairs={{0,1},{1,0},{2,3},{3,2},{4,5},{5,4},{6,7},{7,6},{8,9},{9,8},{10,11... | collective-permute-start | bytes 786440 | tf_op jit(solution)/shard_map/ppermute | solution.py:52
  31.7 7.4 %collective-permute-start.7 = (bf16[128,1024]{1,0:T(8,128)(2,1)S(1)}, bf16[128,1024]{1,0:T(8,128)(2,1)S(1)}, u32[]{:S(2)}, u32[]{:S(2)}) collective-permute-start(bf16[128,1024]{1,0:T(8,128)(2,1)S(1)} %collective-permute-done.6.refs_4_), channel_id=1, source_target_pairs={{0,1},{1,0},{2,3},{3,2},{4,5},{5,4},{6,7},{7,6},{8,9},{9,8},{10,11... | collective-permute-start | bytes 786440 | tf_op jit(solution)/shard_map/ppermute | solution.py:52
  35.4 3.7 %collective-permute-start.9 = (bf16[128,1024]{1,0:T(8,128)(2,1)S(1)}, bf16[128,1024]{1,0:T(8,128)(2,1)S(1)}, u32[]{:S(2)}, u32[]{:S(2)}) collective-permute-start(bf16[128,1024]{1,0:T(8,128)(2,1)S(1)} %collective-permute-done.8.refs_6_), channel_id=1, source_target_pairs={{0,1},{1,0},{2,3},{3,2},{4,5},{5,4},{6,7},{7,6},{8,9},{9,8},{10,11... | collective-permute-start | bytes 786440 | tf_op jit(solution)/shard_map/ppermute | solution.py:52
  38.2 7.3 %collective-permute-start.15 = (bf16[256,512]{1,0:T(8,128)(2,1)S(1)}, bf16[256,512]{1,0:T(8,128)(2,1)S(1)}, u32[]{:S(2)}, u32[]{:S(2)}) collective-permute-start(bf16[256,512]{1,0:T(8,128)(2,1)S(1)} %collective-permute-done.14.refs_1_), channel_id=1, source_target_pairs={{0,2},{2,6},{6,4},{4,0},{1,3},{3,7},{7,5},{5,1},{8,10},{10,14},{14... | collective-permute-start | bytes 786440 | tf_op jit(solution)/shard_map/ppermute | solution.py:43
  45.5 7.3 %collective-permute-start.16 = (bf16[256,512]{1,0:T(8,128)(2,1)S(1)}, bf16[256,512]{1,0:T(8,128)(2,1)S(1)}, u32[]{:S(2)}, u32[]{:S(2)}) collective-permute-start(bf16[256,512]{1,0:T(8,128)(2,1)S(1)} %collective-permute-done.15.refs_2_), channel_id=1, source_target_pairs={{0,2},{2,6},{6,4},{4,0},{1,3},{3,7},{7,5},{5,1},{8,10},{10,14},{14... | collective-permute-start | bytes 786440 | tf_op jit(solution)/shard_map/ppermute | solution.py:43
  60.4 2.0 %collective-permute-start.17 = (f32[128,1024]{1,0:T(8,128)S(1)}, f32[128,1024]{1,0:T(8,128)S(1)}, u32[]{:S(2)}, u32[]{:S(2)}) collective-permute-start(f32[128,1024]{1,0:T(8,128)S(1)} %get-tuple-element.30), channel_id=1, source_target_pairs={{0,1},{1,0},{2,3},{3,2},{4,5},{5,4},{6,7},{7,6},{8,9},{9,8},{10,11... | collective-permute-start | bytes 1572872 | tf_op jit(solution)/shard_map/ppermute | solution.py:52

commit v7 on v6

--- a/solution.py
+++ b/solution.py
@@ -11,10 +11,10 @@
 
 CHUNK = 256
 LIMIT = 32 * 1024 * 1024
-GRAM_COST = 1024
+GRAM_COST = 4_000_000_000
 SOLVE_COST = 1024
 KEEP_COST = 1_000_000_000
-STAGE_COST = 1024
+STAGE_COST = 2_000_000_000
 
 
 def make_table(samples, nfreq, first):
@@ -37,10 +37,13 @@
 def ring_gather(piece, chips, *before_last):
     order = ring_order(chips)
     pairs = [(order[i], order[(i + 1) % chips]) for i in range(chips)]
+    if chips == 4:
+        ahead = lax.ppermute(piece, "chip", pairs)
+        back = lax.ppermute(piece, "chip", [(there, here) for here, there in pairs])
+        return [piece, ahead, back, lax.ppermute(after(ahead, *before_last) if before_last else ahead, "chip", pairs)]
     pieces = [piece]
-    for step in range(1, chips):
-        piece = after(pieces[-1], *before_last) if step == chips - 1 and before_last else pieces[-1]
-        pieces.append(lax.ppermute(piece, "chip", pairs))
+    for _ in range(1, chips):
+        pieces.append(lax.ppermute(pieces[-1], "chip", pairs))
     return pieces
 
 
@@ -183,9 +186,6 @@
         ref, at = (self.late, 0) if last else (self.early, 2 * block * self.count)
         return ref[pl.ds(at, self.count), :].astype(jnp.float32)
 
-    def resid(self, block):
-        return self.keep * self.begin(block) - self.alpha * self.image[self.rows(block), :]
-
     def store(self, block, value):
         at = 2 * block * self.count
         for target, part in zip((self.step_high, self.step_low), two_parts(value)):
@@ -212,7 +212,9 @@
             self.keep = 1.0 - self.alpha * self.damping
 
         def step(block):
-            self.store(block, self.resid(block))
+            resid = self.keep * self.begin(block) - self.alpha * self.image[self.rows(block), :]
+            self.step_image[self.rows(block), :] = resid
+            self.store(block, resid)
 
         return [scalars] + [functools.partial(step, block) for block in self.blocks]
 
@@ -222,8 +224,8 @@
             value = dot(self.high[rows, :], self.step_high[...]) + (
                 dot(self.low[rows, :], self.step_high[...]) + dot(self.high[rows, :], self.step_low[...])
             )
+            self.add(2, self.step_image[rows, :] * value)
             self.step_image[rows, :] = value
-            self.add(2, self.resid(block) * value)
 
         return [functools.partial(step, block) for block in self.blocks]
 
@@ -234,8 +236,9 @@
 
         def curvature(block):
             rows = self.rows(block)
-            direc = self.resid(block) + self.ratio * self.begin(block)
-            value = self.step_image[rows, :] + self.ratio * self.image[rows, :]
+            image = self.image[rows, :]
+            direc = (self.keep + self.ratio) * self.begin(block) - self.alpha * image
+            value = self.step_image[rows, :] + self.ratio * image
             self.add(3, value * (value + self.damping * direc))
 
         def more_scalars():
@@ -300,8 +303,8 @@
         def step():
             left = rows_t[pl.ds(rows, rows), :]
             value = dot(left, weights_high[h]) + dot(left, weights_low[h])
-            sent[:, pl.ds(h * columns, columns)] = value[:, :columns]
-            sent[:, pl.ds((2 + h) * columns, columns)] = -value[:, columns:]
+            sent[:, pl.ds(h * columns, columns)] = value[:, :columns].astype(sent.dtype)
+            sent[:, pl.ds((2 + h) * columns, columns)] = (-value[:, columns:]).astype(sent.dtype)
 
         return [step]
 
@@ -322,7 +325,7 @@
     weights = jax.ShapeDtypeStruct((2, size, 2 * columns), jnp.bfloat16)
     return pl.pallas_call(
         functools.partial(solve_kernel, shots),
-        out_shape=(jax.ShapeDtypeStruct((rows, 4 * columns), jnp.float32), weights, weights),
+        out_shape=(jax.ShapeDtypeStruct((rows, 4 * columns), jnp.bfloat16), weights, weights),
         in_specs=[pl.BlockSpec(memory_space=pltpu.VMEM)] * 7,
         out_specs=(pl.BlockSpec(memory_space=pltpu.VMEM),) * 3,
         scratch_shapes=[
@@ -373,8 +376,8 @@
     columns = staged.shape[3]
     copies = []
     for number, source in enumerate(sources):
-        staged[number, :, 0, :] = source[:, :columns]
-        staged[number, :, 1, :] = source[:, columns:]
+        staged[number, :, 0, :] = source[:, :columns].astype(jnp.float32)
+        staged[number, :, 1, :] = source[:, columns:].astype(jnp.float32)
         offset = (1 - lax.axis_index("core")) * (block.shape[2] // 2) + number * columns
         copy = pltpu.make_async_copy(
             staged.at[number], block.at[:, :, pl.ds(pl.multiple_of(offset, columns), columns)], arrived.at[number]
@@ -483,7 +486,7 @@
         return jnp.transpose(block, (1, 0, 2))[None]
 
     operator = gram_call(place, pieces, local_shots, rows)
-    gathered = ring_gather(up, chips, operator[2])
+    gathered = ring_gather(up, chips)
     early = stage_call(*operator[:2], gathered[:-1], local_shots)
     sent, *weights = solve_call(*operator, *early, gathered[-1], local_shots)
     got = swap_core(sent)

time: 63.5 us -> 63.4 us (level)
  the two profiles are of different devices: /device:TPU:0 before, /device:TPU:9 now
where the time goes in v7:
time: 63.4 us; the launch traced here: 63.2 us
  starting transfers between devices  32.3 us (51%)
  Pallas kernels  15.7 us (25%)
  waiting for transfers between devices  10.8 us (17%)
  matrix products  3.95 us (6%)
    ppermute x6, starting transfers between devices, swap_core(): return lax.ppermute(array, 'core', [(0, 1), (1, 0)])  21.3 us
    pallas_call x1, Pallas kernels, solve_call(): pl.pallas_call(functools.partial(solve_kernel, shots), out_shape=(jax.Sha...  7.63 us
    ppermute x6, starting transfers between devices, to_freq(): lax.ppermute(part, 'freq', [(f, f ^ step) for f in range(nfreq)])  5.43 us
    ppermute x6, waiting for transfers between devices, to_freq(): lax.ppermute(part, 'freq', [(f, f ^ step) for f in range(nfreq)])  5.37 us
    dot_general x2, matrix products, dot(): return jnp.dot(left, right, preferred_element_type=jnp.float32)  3.95 us
    pallas_call x1, Pallas kernels, gram_call(): pl.pallas_call(functools.partial(gram_kernel, shots), out_shape=(block, b...  3.79 us
    ppermute x2, starting transfers between devices, ring_gather(): lax.ppermute(after(ahead, *before_last) if before_last else ahead, 'chip'...  3.13 us
    ppermute x2, waiting for transfers between devices, ring_gather(): ahead = lax.ppermute(piece, 'chip', pairs)  2.86 us
  transfers between devices with their start and end apart: 18, of which 10 were waited for; matrix products, arithmetic and copies ran while one was open for 1% of the time, Pallas kernels for 11%

profile of v7, /device:TPU:9, one launch (start us, length us, event | category | flops | bytes accessed | tf_op | source)
XLA Modules:
  0.0 63.2 jit_solution(16886709434091295664)
XLA Ops:
  0.0 0.0 copy-start.1
  0.0 0.0 copy-start
  0.0 3.2 %convolution_convert_fusion.1 = bf16[128,1024]{1,0:T(8,128)(2,1)S(1)} fusion(bf16[128,2048]{1,0:T(8,128)(2,1)} %constant.44.clone, bf16[2048,1024]{1,0:T(8,128)(2,1)} %bitcast.27), kind=kOutput, calls=%fused_computation.1 | convolution fusion | flops 537001984 | bytes 4980736 | tf_op jit(solution)/shard_map/dot_general | solution.py:64
  3.3 2.2 %collective-permute-start.2 = (bf16[32,1024]{1,0:T(8,128)(2,1)S(1)}, bf16[32,1024]{1,0:T(8,128)(2,1)S(1)}, u32[]{:S(2)}, u32[]{:S(2)}) collective-permute-start(bf16[32,1024]{1,0:T(8,128)(2,1)S(1)} %get-tuple-element.36), channel_id=1, source_target_pairs={{0,24},{8,16},{16,8},{24,0},{1,25},{9,17},{17,9},{25,1},{2,26},{10... | collective-permute-start | bytes 196616 | tf_op jit(solution)/shard_map/ppermute | solution.py:82
  5.5 0.2 collective-permute-start.1
  5.7 0.3 collective-permute-start
  6.0 0.0 copy-done.1
  6.0 0.0 copy-done
  6.0 0.7 %convolution_convert_fusion = bf16[128,1024]{1,0:T(8,128)(2,1)S(1)} fusion(bf16[128,2048]{1,0:T(8,128)(2,1)S(1)} %copy-done.1, bf16[2048,1024]{1,0:T(8,128)(2,1)S(1)} %bitcast.28), kind=kOutput, calls=%fused_computation | convolution fusion | flops 537001984 | bytes 4980736 | tf_op jit(solution)/shard_map/dot_general | solution.py:64
  6.7 0.6 collective-permute-done.2
  7.3 1.8 %collective-permute-done.1 = bf16[32,1024]{1,0:T(8,128)(2,1)S(1)} collective-permute-done((bf16[32,1024]{1,0:T(8,128)(2,1)S(1)}, bf16[32,1024]{1,0:T(8,128)(2,1)S(1)}, u32[]{:S(2)}, u32[]{:S(2)}) %collective-permute-start.1) | collective-permute-done | bytes 65568 | tf_op jit(solution)/shard_map/ppermute | solution.py:82
  9.2 0.1 collective-permute-done
  9.3 2.4 %collective-permute-start.4 = (bf16[128,1024]{1,0:T(8,128)(2,1)S(1)}, bf16[128,1024]{1,0:T(8,128)(2,1)S(1)}, u32[]{:S(2)}, u32[]{:S(2)}) collective-permute-start(bf16[128,1024]{1,0:T(8,128)(2,1)S(1)} %pad_maximum_fusion.refs_0_), channel_id=1, source_target_pairs={{0,2},{2,6},{6,4},{4,0},{1,3},{3,7},{7,5},{5,1},{8,10},{10,14},{14... | collective-permute-start | bytes 786440 | tf_op jit(solution)/shard_map/ppermute | solution.py:41
  11.6 1.5 %collective-permute-start.12 = (bf16[32,1024]{1,0:T(8,128)(2,1)S(1)}, bf16[32,1024]{1,0:T(8,128)(2,1)S(1)}, u32[]{:S(2)}, u32[]{:S(2)}) collective-permute-start(bf16[32,1024]{1,0:T(8,128)(2,1)S(1)} %get-tuple-element.32), channel_id=1, source_target_pairs={{0,24},{8,16},{16,8},{24,0},{1,25},{9,17},{17,9},{25,1},{2,26},{10... | collective-permute-start | bytes 196616 | tf_op jit(solution)/shard_map/ppermute | solution.py:82
  13.2 0.7 %collective-permute-start.11 = (bf16[32,1024]{1,0:T(8,128)(2,1)S(1)}, bf16[32,1024]{1,0:T(8,128)(2,1)S(1)}, u32[]{:S(2)}, u32[]{:S(2)}) collective-permute-start(bf16[32,1024]{1,0:T(8,128)(2,1)S(1)} %get-tuple-element.33), channel_id=1, source_target_pairs={{0,16},{8,24},{16,0},{24,8},{1,17},{9,25},{17,1},{25,9},{2,18},{10... | collective-permute-start | bytes 196616 | tf_op jit(solution)/shard_map/ppermute | solution.py:82
  13.8 0.5 collective-permute-start.10
  14.4 0.0 collective-permute-start.6
  14.4 1.4 %collective-permute-done.12 = bf16[32,1024]{1,0:T(8,128)(2,1)S(1)} collective-permute-done((bf16[32,1024]{1,0:T(8,128)(2,1)S(1)}, bf16[32,1024]{1,0:T(8,128)(2,1)S(1)}, u32[]{:S(2)}, u32[]{:S(2)}) %collective-permute-start.12) | collective-permute-done | bytes 65568 | tf_op jit(solution)/shard_map/ppermute | solution.py:82
  15.7 1.0 %collective-permute-done.11 = bf16[32,1024]{1,0:T(8,128)(2,1)S(1)} collective-permute-done((bf16[32,1024]{1,0:T(8,128)(2,1)S(1)}, bf16[32,1024]{1,0:T(8,128)(2,1)S(1)}, u32[]{:S(2)}, u32[]{:S(2)}) %collective-permute-start.11) | collective-permute-done | bytes 65568 | tf_op jit(solution)/shard_map/ppermute | solution.py:82
  16.7 0.5 collective-permute-done.10
  17.3 0.0 collective-permute-done.4.refs_2_
  17.3 1.4 %collective-permute-start.8 = (bf16[128,1024]{1,0:T(8,128)(2,1)S(1)}, bf16[128,1024]{1,0:T(8,128)(2,1)S(1)}, u32[]{:S(2)}, u32[]{:S(2)}) collective-permute-start(bf16[128,1024]{1,0:T(8,128)(2,1)S(1)} %collective-permute-done.4.refs_2_), channel_id=1, source_target_pairs={{0,2},{2,6},{6,4},{4,0},{1,3},{3,7},{7,5},{5,1},{8,10},{10,14},{14... | collective-permute-start | bytes 786440 | tf_op jit(solution)/shard_map/ppermute | solution.py:43
  18.7 9.5 %collective-permute-start.13 = (bf16[128,512]{1,0:T(8,128)(2,1)S(1)}, bf16[128,512]{1,0:T(8,128)(2,1)S(1)}, u32[]{:S(2)}, u32[]{:S(2)}) collective-permute-start(bf16[128,512]{1,0:T(8,128)(2,1)S(1)} %get-tuple-element.30), channel_id=1, source_target_pairs={{0,1},{1,0},{2,3},{3,2},{4,5},{5,4},{6,7},{7,6},{8,9},{9,8},{10,11... | collective-permute-start | bytes 393224 | tf_op jit(solution)/shard_map/ppermute | solution.py:55
  28.2 0.1 collective-permute-start.3
  28.3 0.9 %collective-permute-done.13 = bf16[128,512]{1,0:T(8,128)(2,1)S(1)} collective-permute-done((bf16[128,512]{1,0:T(8,128)(2,1)S(1)}, bf16[128,512]{1,0:T(8,128)(2,1)S(1)}, u32[]{:S(2)}, u32[]{:S(2)}) %collective-permute-start.13) | collective-permute-done | bytes 131104 | tf_op jit(solution)/shard_map/ppermute | solution.py:55
  29.2 0.1 collective-permute-start.14
  29.3 0.4 collective-permute-start.5
  29.7 0.0 collective-permute-done.6.refs_4_
  29.7 0.1 collective-permute-start.7
  29.8 0.0 collective-permute-done.8.refs_6_
  29.8 4.0 %collective-permute-start.9 = (bf16[128,1024]{1,0:T(8,128)(2,1)S(1)}, bf16[128,1024]{1,0:T(8,128)(2,1)S(1)}, u32[]{:S(2)}, u32[]{:S(2)}) collective-permute-start(bf16[128,1024]{1,0:T(8,128)(2,1)S(1)} %collective-permute-done.8.refs_6_), channel_id=1, source_target_pairs={{0,1},{1,0},{2,3},{3,2},{4,5},{5,4},{6,7},{7,6},{8,9},{9,8},{10,11... | collective-permute-start | bytes 786440 | tf_op jit(solution)/shard_map/ppermute | solution.py:55
  33.8 0.1 add_add_fusion.place
  33.9 0.0 collective-permute-done.3.refs_1_
  33.9 0.0 collective-permute-start.15
  33.9 2.9 %collective-permute-done.14.refs_1_ = bf16[256,512]{1,0:T(8,128)(2,1)S(1)} collective-permute-done((bf16[256,512]{1,0:T(8,128)(2,1)S(1)}, bf16[256,512]{1,0:T(8,128)(2,1)S(1)}, u32[]{:S(2)}, u32[]{:S(2)}) %collective-permute-start.14) | collective-permute-done | bytes 262176 | tf_op jit(solution)/shard_map/ppermute | solution.py:41
  36.8 1.7 %collective-permute-start.16 = (bf16[256,512]{1,0:T(8,128)(2,1)S(1)}, bf16[256,512]{1,0:T(8,128)(2,1)S(1)}, u32[]{:S(2)}, u32[]{:S(2)}) collective-permute-start(bf16[256,512]{1,0:T(8,128)(2,1)S(1)} %collective-permute-done.14.refs_1_), channel_id=1, source_target_pairs={{0,2},{2,6},{6,4},{4,0},{1,3},{3,7},{7,5},{5,1},{8,10},{10,14},{14... | collective-permute-start | bytes 786440 | tf_op jit(solution)/shard_map/ppermute | solution.py:43
  38.5 0.0 collective-permute-done.7.refs_5_
  38.5 0.0 collective-permute-done.5.refs_3_
  38.5 0.0 collective-permute-done.9.refs_7_
  38.5 3.8 %gram.1 = (bf16[512,1024]{1,0:T(8,128)(2,1)S(1)}, bf16[512,1024]{1,0:T(8,128)(2,1)S(1)}, f32[1,1]{1,0:T(1,128)}, bf16[256,1024]{1,0:T(8,128)(2,1)S(1)}) custom-call(s32[2]{0:T(128)S(1)} %add_add_fusion.place, bf16[128,1024]{1,0:T(8,128)(2,1)S(1)} %pad_maximum_fusion.refs_0_, bf16[128,1024]{1,0:T(8,128)(2,1)S(1)} %collective-permute-done.3.refs_1_, ...), custom_call_target="tpu_custom_call" | custom-call | flops 4000000000 | bytes 1024 | tf_op jit(solution)/shard_map/gram/pallas_call | solution.py:118
  42.3 1.5 %collective-permute-done.15.refs_2_ = bf16[256,512]{1,0:T(8,128)(2,1)S(1)} collective-permute-done((bf16[256,512]{1,0:T(8,128)(2,1)S(1)}, bf16[256,512]{1,0:T(8,128)(2,1)S(1)}, u32[]{:S(2)}, u32[]{:S(2)}) %collective-permute-start.15) | collective-permute-done | bytes 262176 | tf_op jit(solution)/shard_map/ppermute | solution.py:42
  43.7 1.8 %stage.1 = (bf16[2,768,512]{2,1,0:T(8,128)(2,1)S(1)}, f32[2,512,512]{2,1,0:T(8,128)S(1)}) custom-call(bf16[512,1024]{1,0:T(8,128)(2,1)S(1)} %get-tuple-element.20.high, bf16[512,1024]{1,0:T(8,128)(2,1)S(1)} %get-tuple-element.21.low, bf16[256,512]{1,0:T(8,128)(2,1)S(1)} %pad_maximum_fusion.2.refs_0_, bf16[256,512]{1,0:T(8,128)(2,1)S(1)} %collective-permute-done.14.refs_1_, ...), custom_call_target="tpu_custom_call" | custom-call | flops 2000000000 | bytes 1024 | tf_op jit(solution)/shard_map/stage/pallas_call | solution.py:275
  45.6 0.2 collective-permute-done.16.piece
  45.8 7.6 %solve.1 = (bf16[128,1024]{1,0:T(8,128)(2,1)S(1)}, bf16[2,1024,512]{2,1,0:T(8,128)(2,1)S(1)}, bf16[2,1024,512]{2,1,0:T(8,128)(2,1)S(1)}) custom-call(bf16[512,1024]{1,0:T(8,128)(2,1)S(1)} %get-tuple-element.20.high, bf16[512,1024]{1,0:T(8,128)(2,1)S(1)} %get-tuple-element.21.low, f32[1,1]{1,0:T(1,128)} %get-tuple-element.22.damping, ...), custom_call_target="tpu_custom_call" | custom-call | flops 1024 | bytes 1024 | tf_op jit(solution)/shard_map/solve/pallas_call | solution.py:326
  53.4 7.2 %collective-permute-start.17 = (bf16[128,1024]{1,0:T(8,128)(2,1)S(1)}, bf16[128,1024]{1,0:T(8,128)(2,1)S(1)}, u32[]{:S(2)}, u32[]{:S(2)}) collective-permute-start(bf16[128,1024]{1,0:T(8,128)(2,1)S(1)} %get-tuple-element.28), channel_id=1, source_target_pairs={{0,1},{1,0},{2,3},{3,2},{4,5},{5,4},{6,7},{7,6},{8,9},{9,8},{10,11... | collective-permute-start | bytes 786440 | tf_op jit(solution)/shard_map/ppermute | solution.py:55
  60.6 1.6 %keep.1._ = f32[128,2,1024]{2,1,0:T(2,128)} custom-call(bf16[256,1024]{1,0:T(8,128)(2,1)S(1)} %get-tuple-element.19.rows_t, bf16[2,1024,512]{2,1,0:T(8,128)(2,1)S(1)} %get-tuple-element.26.weights_high, bf16[2,1024,512]{2,1,0:T(8,128)(2,1)S(1)} %get-tuple-element.27.weights_low), custom_call_target="tpu_custom_call" | custom-call | flops 1000000000 | bytes 1024 | tf_op jit(solution)/shard_map/keep/pallas_call | solution.py:362
  62.1 0.0 collective-permute-done.17.refs_0_
  62.1 0.9 %place.1 = f32[128,2,1024]{2,1,0:T(2,128)} custom-call(f32[128,2,1024]{2,1,0:T(2,128)} %keep.1._, bf16[128,1024]{1,0:T(8,128)(2,1)S(1)} %collective-permute-done.17.refs_0_), custom_call_target="tpu_custom_call", output_to_operand_aliasing={{}: (0, {})} | custom-call | tf_op jit(solution)/shard_map/place/pallas_call | solution.py:393
  (6 shorter events, 0.1 us)
Async XLA Ops:
  0.0 6.0 %copy-start.1 = (bf16[128,2048]{1,0:T(8,128)(2,1)S(1)}, bf16[128,2048]{1,0:T(8,128)(2,1)}, u32[]{:S(2)}) copy-start(bf16[128,2048]{1,0:T(8,128)(2,1)} %constant.44.clone) | copy-start | bytes 1572868
  0.0 6.0 %copy-start = (bf16[16,128,1024]{2,1,0:T(8,128)(2,1)S(1)}, bf16[16,128,1024]{2,1,0:T(8,128)(2,1)}, u32[]{:S(2)}) copy-start(bf16[16,128,1024]{2,1,0:T(8,128)(2,1)} %param.3) | copy-start | bytes 12582916
  3.3 4.1 %collective-permute-start.2 = (bf16[32,1024]{1,0:T(8,128)(2,1)S(1)}, bf16[32,1024]{1,0:T(8,128)(2,1)S(1)}, u32[]{:S(2)}, u32[]{:S(2)}) collective-permute-start(bf16[32,1024]{1,0:T(8,128)(2,1)S(1)} %get-tuple-element.36), channel_id=1, source_target_pairs={{0,24},{8,16},{16,8},{24,0},{1,25},{9,17},{17,9},{25,1},{2,26},{10... | collective-permute-start | bytes 196616 | tf_op jit(solution)/shard_map/ppermute | solution.py:82
  5.5 3.7 %collective-permute-start.1 = (bf16[32,1024]{1,0:T(8,128)(2,1)S(1)}, bf16[32,1024]{1,0:T(8,128)(2,1)S(1)}, u32[]{:S(2)}, u32[]{:S(2)}) collective-permute-start(bf16[32,1024]{1,0:T(8,128)(2,1)S(1)} %get-tuple-element.37), channel_id=1, source_target_pairs={{0,16},{8,24},{16,0},{24,8},{1,17},{9,25},{17,1},{25,9},{2,18},{10... | collective-permute-start | bytes 196616 | tf_op jit(solution)/shard_map/ppermute | solution.py:82
  5.7 3.5 %collective-permute-start = (bf16[32,1024]{1,0:T(8,128)(2,1)S(1)}, bf16[32,1024]{1,0:T(8,128)(2,1)S(1)}, u32[]{:S(2)}, u32[]{:S(2)}) collective-permute-start(bf16[32,1024]{1,0:T(8,128)(2,1)S(1)} %get-tuple-element.38), channel_id=1, source_target_pairs={{0,8},{8,0},{16,24},{24,16},{1,9},{9,1},{17,25},{25,17},{2,10},{10... | collective-permute-start | bytes 196616 | tf_op jit(solution)/shard_map/ppermute | solution.py:82
  9.3 8.0 %collective-permute-start.4 = (bf16[128,1024]{1,0:T(8,128)(2,1)S(1)}, bf16[128,1024]{1,0:T(8,128)(2,1)S(1)}, u32[]{:S(2)}, u32[]{:S(2)}) collective-permute-start(bf16[128,1024]{1,0:T(8,128)(2,1)S(1)} %pad_maximum_fusion.refs_0_), channel_id=1, source_target_pairs={{0,2},{2,6},{6,4},{4,0},{1,3},{3,7},{7,5},{5,1},{8,10},{10,14},{14... | collective-permute-start | bytes 786440 | tf_op jit(solution)/shard_map/ppermute | solution.py:41
  11.6 4.1 %collective-permute-start.12 = (bf16[32,1024]{1,0:T(8,128)(2,1)S(1)}, bf16[32,1024]{1,0:T(8,128)(2,1)S(1)}, u32[]{:S(2)}, u32[]{:S(2)}) collective-permute-start(bf16[32,1024]{1,0:T(8,128)(2,1)S(1)} %get-tuple-element.32), channel_id=1, source_target_pairs={{0,24},{8,16},{16,8},{24,0},{1,25},{9,17},{17,9},{25,1},{2,26},{10... | collective-permute-start | bytes 196616 | tf_op jit(solution)/shard_map/ppermute | solution.py:82
  13.2 3.6 %collective-permute-start.11 = (bf16[32,1024]{1,0:T(8,128)(2,1)S(1)}, bf16[32,1024]{1,0:T(8,128)(2,1)S(1)}, u32[]{:S(2)}, u32[]{:S(2)}) collective-permute-start(bf16[32,1024]{1,0:T(8,128)(2,1)S(1)} %get-tuple-element.33), channel_id=1, source_target_pairs={{0,16},{8,24},{16,0},{24,8},{1,17},{9,25},{17,1},{25,9},{2,18},{10... | collective-permute-start | bytes 196616 | tf_op jit(solution)/shard_map/ppermute | solution.py:82
  13.8 3.4 %collective-permute-start.10 = (bf16[32,1024]{1,0:T(8,128)(2,1)S(1)}, bf16[32,1024]{1,0:T(8,128)(2,1)S(1)}, u32[]{:S(2)}, u32[]{:S(2)}) collective-permute-start(bf16[32,1024]{1,0:T(8,128)(2,1)S(1)} %get-tuple-element.34), channel_id=1, source_target_pairs={{0,8},{8,0},{16,24},{24,16},{1,9},{9,1},{17,25},{25,17},{2,10},{10... | collective-permute-start | bytes 196616 | tf_op jit(solution)/shard_map/ppermute | solution.py:82
  14.4 15.3 %collective-permute-start.6 = (bf16[128,1024]{1,0:T(8,128)(2,1)S(1)}, bf16[128,1024]{1,0:T(8,128)(2,1)S(1)}, u32[]{:S(2)}, u32[]{:S(2)}) collective-permute-start(bf16[128,1024]{1,0:T(8,128)(2,1)S(1)} %pad_maximum_fusion.refs_0_), channel_id=1, source_target_pairs={{2,0},{6,2},{4,6},{0,4},{3,1},{7,3},{5,7},{1,5},{10,8},{14,10},{12... | collective-permute-start | bytes 786440 | tf_op jit(solution)/shard_map/ppermute | solution.py:42
  17.3 12.6 %collective-permute-start.8 = (bf16[128,1024]{1,0:T(8,128)(2,1)S(1)}, bf16[128,1024]{1,0:T(8,128)(2,1)S(1)}, u32[]{:S(2)}, u32[]{:S(2)}) collective-permute-start(bf16[128,1024]{1,0:T(8,128)(2,1)S(1)} %collective-permute-done.4.refs_2_), channel_id=1, source_target_pairs={{0,2},{2,6},{6,4},{4,0},{1,3},{3,7},{7,5},{5,1},{8,10},{10,14},{14... | collective-permute-start | bytes 786440 | tf_op jit(solution)/shard_map/ppermute | solution.py:43
  18.7 10.4 %collective-permute-start.13 = (bf16[128,512]{1,0:T(8,128)(2,1)S(1)}, bf16[128,512]{1,0:T(8,128)(2,1)S(1)}, u32[]{:S(2)}, u32[]{:S(2)}) collective-permute-start(bf16[128,512]{1,0:T(8,128)(2,1)S(1)} %get-tuple-element.30), channel_id=1, source_target_pairs={{0,1},{1,0},{2,3},{3,2},{4,5},{5,4},{6,7},{7,6},{8,9},{9,8},{10,11... | collective-permute-start | bytes 393224 | tf_op jit(solution)/shard_map/ppermute | solution.py:55
  28.2 5.7 %collective-permute-start.3 = (bf16[128,1024]{1,0:T(8,128)(2,1)S(1)}, bf16[128,1024]{1,0:T(8,128)(2,1)S(1)}, u32[]{:S(2)}, u32[]{:S(2)}) collective-permute-start(bf16[128,1024]{1,0:T(8,128)(2,1)S(1)} %pad_maximum_fusion.refs_0_), channel_id=1, source_target_pairs={{0,1},{1,0},{2,3},{3,2},{4,5},{5,4},{6,7},{7,6},{8,9},{9,8},{10,11... | collective-permute-start | bytes 786440 | tf_op jit(solution)/shard_map/ppermute | solution.py:55
  29.2 7.6 %collective-permute-start.14 = (bf16[256,512]{1,0:T(8,128)(2,1)S(1)}, bf16[256,512]{1,0:T(8,128)(2,1)S(1)}, u32[]{:S(2)}, u32[]{:S(2)}) collective-permute-start(bf16[256,512]{1,0:T(8,128)(2,1)S(1)} %pad_maximum_fusion.2.refs_0_), channel_id=1, source_target_pairs={{0,2},{2,6},{6,4},{4,0},{1,3},{3,7},{7,5},{5,1},{8,10},{10,14},{14... | collective-permute-start | bytes 786440 | tf_op jit(solution)/shard_map/ppermute | solution.py:41
  29.3 9.2 %collective-permute-start.5 = (bf16[128,1024]{1,0:T(8,128)(2,1)S(1)}, bf16[128,1024]{1,0:T(8,128)(2,1)S(1)}, u32[]{:S(2)}, u32[]{:S(2)}) collective-permute-start(bf16[128,1024]{1,0:T(8,128)(2,1)S(1)} %collective-permute-done.4.refs_2_), channel_id=1, source_target_pairs={{0,1},{1,0},{2,3},{3,2},{4,5},{5,4},{6,7},{7,6},{8,9},{9,8},{10,11... | collective-permute-start | bytes 786440 | tf_op jit(solution)/shard_map/ppermute | solution.py:55
  29.7 8.8 %collective-permute-start.7 = (bf16[128,1024]{1,0:T(8,128)(2,1)S(1)}, bf16[128,1024]{1,0:T(8,128)(2,1)S(1)}, u32[]{:S(2)}, u32[]{:S(2)}) collective-permute-start(bf16[128,1024]{1,0:T(8,128)(2,1)S(1)} %collective-permute-done.6.refs_4_), channel_id=1, source_target_pairs={{0,1},{1,0},{2,3},{3,2},{4,5},{5,4},{6,7},{7,6},{8,9},{9,8},{10,11... | collective-permute-start | bytes 786440 | tf_op jit(solution)/shard_map/ppermute | solution.py:55
  29.8 8.6 %collective-permute-start.9 = (bf16[128,1024]{1,0:T(8,128)(2,1)S(1)}, bf16[128,1024]{1,0:T(8,128)(2,1)S(1)}, u32[]{:S(2)}, u32[]{:S(2)}) collective-permute-start(bf16[128,1024]{1,0:T(8,128)(2,1)S(1)} %collective-permute-done.8.refs_6_), channel_id=1, source_target_pairs={{0,1},{1,0},{2,3},{3,2},{4,5},{5,4},{6,7},{7,6},{8,9},{9,8},{10,11... | collective-permute-start | bytes 786440 | tf_op jit(solution)/shard_map/ppermute | solution.py:55
  33.9 9.8 %collective-permute-start.15 = (bf16[256,512]{1,0:T(8,128)(2,1)S(1)}, bf16[256,512]{1,0:T(8,128)(2,1)S(1)}, u32[]{:S(2)}, u32[]{:S(2)}) collective-permute-start(bf16[256,512]{1,0:T(8,128)(2,1)S(1)} %pad_maximum_fusion.2.refs_0_), channel_id=1, source_target_pairs={{2,0},{6,2},{4,6},{0,4},{3,1},{7,3},{5,7},{1,5},{10,8},{14,10},{12... | collective-permute-start | bytes 786440 | tf_op jit(solution)/shard_map/ppermute | solution.py:42
  36.8 9.0 %collective-permute-start.16 = (bf16[256,512]{1,0:T(8,128)(2,1)S(1)}, bf16[256,512]{1,0:T(8,128)(2,1)S(1)}, u32[]{:S(2)}, u32[]{:S(2)}) collective-permute-start(bf16[256,512]{1,0:T(8,128)(2,1)S(1)} %collective-permute-done.14.refs_1_), channel_id=1, source_target_pairs={{0,2},{2,6},{6,4},{4,0},{1,3},{3,7},{7,5},{5,1},{8,10},{10,14},{14... | collective-permute-start | bytes 786440 | tf_op jit(solution)/shard_map/ppermute | solution.py:43
  53.4 8.7 %collective-permute-start.17 = (bf16[128,1024]{1,0:T(8,128)(2,1)S(1)}, bf16[128,1024]{1,0:T(8,128)(2,1)S(1)}, u32[]{:S(2)}, u32[]{:S(2)}) collective-permute-start(bf16[128,1024]{1,0:T(8,128)(2,1)S(1)} %get-tuple-element.28), channel_id=1, source_target_pairs={{0,1},{1,0},{2,3},{3,2},{4,5},{5,4},{6,7},{7,6},{8,9},{9,8},{10,11... | collective-permute-start | bytes 786440 | tf_op jit(solution)/shard_map/ppermute | solution.py:55

commit v8 on v7

--- a/solution.py
+++ b/solution.py
@@ -14,7 +14,7 @@
 GRAM_COST = 4_000_000_000
 SOLVE_COST = 1024
 KEEP_COST = 1_000_000_000
-STAGE_COST = 2_000_000_000
+STAGE_COST = 20_000_000_000
 
 
 def make_table(samples, nfreq, first):

time: 63.4 us -> 63.4 us (level)
  no operation moved by 1% of the time
where the time goes in v8:
time: 63.4 us; the launch traced here: 63.2 us
  starting transfers between devices  32.3 us (51%)
  Pallas kernels  15.7 us (25%)
  waiting for transfers between devices  10.8 us (17%)
  matrix products  3.95 us (6%)
    ppermute x6, starting transfers between devices, swap_core(): return lax.ppermute(array, 'core', [(0, 1), (1, 0)])  21.3 us
    pallas_call x1, Pallas kernels, solve_call(): pl.pallas_call(functools.partial(solve_kernel, shots), out_shape=(jax.Sha...  7.63 us
    ppermute x6, starting transfers between devices, to_freq(): lax.ppermute(part, 'freq', [(f, f ^ step) for f in range(nfreq)])  5.43 us
    ppermute x6, waiting for transfers between devices, to_freq(): lax.ppermute(part, 'freq', [(f, f ^ step) for f in range(nfreq)])  5.37 us
    dot_general x2, matrix products, dot(): return jnp.dot(left, right, preferred_element_type=jnp.float32)  3.95 us
    pallas_call x1, Pallas kernels, gram_call(): pl.pallas_call(functools.partial(gram_kernel, shots), out_shape=(block, b...  3.79 us
    ppermute x2, starting transfers between devices, ring_gather(): lax.ppermute(after(ahead, *before_last) if before_last else ahead, 'chip'...  3.13 us
    ppermute x2, waiting for transfers between devices, ring_gather(): ahead = lax.ppermute(piece, 'chip', pairs)  2.86 us
  transfers between devices with their start and end apart: 18, of which 10 were waited for; matrix products, arithmetic and copies ran while one was open for 1% of the time, Pallas kernels for 11%

profile of v8, /device:TPU:9, one launch (start us, length us, event | category | flops | bytes accessed | tf_op | source)
XLA Modules:
  0.0 63.2 jit_solution(16886709434091295664)
XLA Ops:
  0.0 0.0 copy-start.1
  0.0 0.0 copy-start
  0.0 3.2 %convolution_convert_fusion.1 = bf16[128,1024]{1,0:T(8,128)(2,1)S(1)} fusion(bf16[128,2048]{1,0:T(8,128)(2,1)} %constant.44.clone, bf16[2048,1024]{1,0:T(8,128)(2,1)} %bitcast.27), kind=kOutput, calls=%fused_computation.1 | convolution fusion | flops 537001984 | bytes 4980736 | tf_op jit(solution)/shard_map/dot_general | solution.py:64
  3.3 2.2 %collective-permute-start.2 = (bf16[32,1024]{1,0:T(8,128)(2,1)S(1)}, bf16[32,1024]{1,0:T(8,128)(2,1)S(1)}, u32[]{:S(2)}, u32[]{:S(2)}) collective-permute-start(bf16[32,1024]{1,0:T(8,128)(2,1)S(1)} %get-tuple-element.36), channel_id=1, source_target_pairs={{0,24},{8,16},{16,8},{24,0},{1,25},{9,17},{17,9},{25,1},{2,26},{10... | collective-permute-start | bytes 196616 | tf_op jit(solution)/shard_map/ppermute | solution.py:82
  5.5 0.2 collective-permute-start.1
  5.7 0.3 collective-permute-start
  6.0 0.0 copy-done.1
  6.0 0.0 copy-done
  6.0 0.7 %convolution_convert_fusion = bf16[128,1024]{1,0:T(8,128)(2,1)S(1)} fusion(bf16[128,2048]{1,0:T(8,128)(2,1)S(1)} %copy-done.1, bf16[2048,1024]{1,0:T(8,128)(2,1)S(1)} %bitcast.28), kind=kOutput, calls=%fused_computation | convolution fusion | flops 537001984 | bytes 4980736 | tf_op jit(solution)/shard_map/dot_general | solution.py:64
  6.7 0.6 collective-permute-done.2
  7.3 1.8 %collective-permute-done.1 = bf16[32,1024]{1,0:T(8,128)(2,1)S(1)} collective-permute-done((bf16[32,1024]{1,0:T(8,128)(2,1)S(1)}, bf16[32,1024]{1,0:T(8,128)(2,1)S(1)}, u32[]{:S(2)}, u32[]{:S(2)}) %collective-permute-start.1) | collective-permute-done | bytes 65568 | tf_op jit(solution)/shard_map/ppermute | solution.py:82
  9.2 0.1 collective-permute-done
  9.3 2.4 %collective-permute-start.4 = (bf16[128,1024]{1,0:T(8,128)(2,1)S(1)}, bf16[128,1024]{1,0:T(8,128)(2,1)S(1)}, u32[]{:S(2)}, u32[]{:S(2)}) collective-permute-start(bf16[128,1024]{1,0:T(8,128)(2,1)S(1)} %pad_maximum_fusion.refs_0_), channel_id=1, source_target_pairs={{0,2},{2,6},{6,4},{4,0},{1,3},{3,7},{7,5},{5,1},{8,10},{10,14},{14... | collective-permute-start | bytes 786440 | tf_op jit(solution)/shard_map/ppermute | solution.py:41
  11.6 1.5 %collective-permute-start.12 = (bf16[32,1024]{1,0:T(8,128)(2,1)S(1)}, bf16[32,1024]{1,0:T(8,128)(2,1)S(1)}, u32[]{:S(2)}, u32[]{:S(2)}) collective-permute-start(bf16[32,1024]{1,0:T(8,128)(2,1)S(1)} %get-tuple-element.32), channel_id=1, source_target_pairs={{0,24},{8,16},{16,8},{24,0},{1,25},{9,17},{17,9},{25,1},{2,26},{10... | collective-permute-start | bytes 196616 | tf_op jit(solution)/shard_map/ppermute | solution.py:82
  13.2 0.7 %collective-permute-start.11 = (bf16[32,1024]{1,0:T(8,128)(2,1)S(1)}, bf16[32,1024]{1,0:T(8,128)(2,1)S(1)}, u32[]{:S(2)}, u32[]{:S(2)}) collective-permute-start(bf16[32,1024]{1,0:T(8,128)(2,1)S(1)} %get-tuple-element.33), channel_id=1, source_target_pairs={{0,16},{8,24},{16,0},{24,8},{1,17},{9,25},{17,1},{25,9},{2,18},{10... | collective-permute-start | bytes 196616 | tf_op jit(solution)/shard_map/ppermute | solution.py:82
  13.8 0.5 collective-permute-start.10
  14.4 0.0 collective-permute-start.6
  14.4 1.4 %collective-permute-done.12 = bf16[32,1024]{1,0:T(8,128)(2,1)S(1)} collective-permute-done((bf16[32,1024]{1,0:T(8,128)(2,1)S(1)}, bf16[32,1024]{1,0:T(8,128)(2,1)S(1)}, u32[]{:S(2)}, u32[]{:S(2)}) %collective-permute-start.12) | collective-permute-done | bytes 65568 | tf_op jit(solution)/shard_map/ppermute | solution.py:82
  15.7 1.0 %collective-permute-done.11 = bf16[32,1024]{1,0:T(8,128)(2,1)S(1)} collective-permute-done((bf16[32,1024]{1,0:T(8,128)(2,1)S(1)}, bf16[32,1024]{1,0:T(8,128)(2,1)S(1)}, u32[]{:S(2)}, u32[]{:S(2)}) %collective-permute-start.11) | collective-permute-done | bytes 65568 | tf_op jit(solution)/shard_map/ppermute | solution.py:82
  16.7 0.5 collective-permute-done.10
  17.3 0.0 collective-permute-done.4.refs_2_
  17.3 1.4 %collective-permute-start.8 = (bf16[128,1024]{1,0:T(8,128)(2,1)S(1)}, bf16[128,1024]{1,0:T(8,128)(2,1)S(1)}, u32[]{:S(2)}, u32[]{:S(2)}) collective-permute-start(bf16[128,1024]{1,0:T(8,128)(2,1)S(1)} %collective-permute-done.4.refs_2_), channel_id=1, source_target_pairs={{0,2},{2,6},{6,4},{4,0},{1,3},{3,7},{7,5},{5,1},{8,10},{10,14},{14... | collective-permute-start | bytes 786440 | tf_op jit(solution)/shard_map/ppermute | solution.py:43
  18.7 9.5 %collective-permute-start.13 = (bf16[128,512]{1,0:T(8,128)(2,1)S(1)}, bf16[128,512]{1,0:T(8,128)(2,1)S(1)}, u32[]{:S(2)}, u32[]{:S(2)}) collective-permute-start(bf16[128,512]{1,0:T(8,128)(2,1)S(1)} %get-tuple-element.30), channel_id=1, source_target_pairs={{0,1},{1,0},{2,3},{3,2},{4,5},{5,4},{6,7},{7,6},{8,9},{9,8},{10,11... | collective-permute-start | bytes 393224 | tf_op jit(solution)/shard_map/ppermute | solution.py:55
  28.2 0.1 collective-permute-start.3
  28.3 0.9 %collective-permute-done.13 = bf16[128,512]{1,0:T(8,128)(2,1)S(1)} collective-permute-done((bf16[128,512]{1,0:T(8,128)(2,1)S(1)}, bf16[128,512]{1,0:T(8,128)(2,1)S(1)}, u32[]{:S(2)}, u32[]{:S(2)}) %collective-permute-start.13) | collective-permute-done | bytes 131104 | tf_op jit(solution)/shard_map/ppermute | solution.py:55
  29.2 0.1 collective-permute-start.14
  29.3 0.4 collective-permute-start.5
  29.7 0.0 collective-permute-done.6.refs_4_
  29.7 0.1 collective-permute-start.7
  29.8 0.0 collective-permute-done.8.refs_6_
  29.8 4.0 %collective-permute-start.9 = (bf16[128,1024]{1,0:T(8,128)(2,1)S(1)}, bf16[128,1024]{1,0:T(8,128)(2,1)S(1)}, u32[]{:S(2)}, u32[]{:S(2)}) collective-permute-start(bf16[128,1024]{1,0:T(8,128)(2,1)S(1)} %collective-permute-done.8.refs_6_), channel_id=1, source_target_pairs={{0,1},{1,0},{2,3},{3,2},{4,5},{5,4},{6,7},{7,6},{8,9},{9,8},{10,11... | collective-permute-start | bytes 786440 | tf_op jit(solution)/shard_map/ppermute | solution.py:55
  33.8 0.1 add_add_fusion.place
  33.9 0.0 collective-permute-done.3.refs_1_
  33.9 0.0 collective-permute-start.15
  33.9 2.9 %collective-permute-done.14.refs_1_ = bf16[256,512]{1,0:T(8,128)(2,1)S(1)} collective-permute-done((bf16[256,512]{1,0:T(8,128)(2,1)S(1)}, bf16[256,512]{1,0:T(8,128)(2,1)S(1)}, u32[]{:S(2)}, u32[]{:S(2)}) %collective-permute-start.14) | collective-permute-done | bytes 262176 | tf_op jit(solution)/shard_map/ppermute | solution.py:41
  36.8 1.7 %collective-permute-start.16 = (bf16[256,512]{1,0:T(8,128)(2,1)S(1)}, bf16[256,512]{1,0:T(8,128)(2,1)S(1)}, u32[]{:S(2)}, u32[]{:S(2)}) collective-permute-start(bf16[256,512]{1,0:T(8,128)(2,1)S(1)} %collective-permute-done.14.refs_1_), channel_id=1, source_target_pairs={{0,2},{2,6},{6,4},{4,0},{1,3},{3,7},{7,5},{5,1},{8,10},{10,14},{14... | collective-permute-start | bytes 786440 | tf_op jit(solution)/shard_map/ppermute | solution.py:43
  38.5 0.0 collective-permute-done.7.refs_5_
  38.5 0.0 collective-permute-done.5.refs_3_
  38.5 0.0 collective-permute-done.9.refs_7_
  38.5 3.8 %gram.1 = (bf16[512,1024]{1,0:T(8,128)(2,1)S(1)}, bf16[512,1024]{1,0:T(8,128)(2,1)S(1)}, f32[1,1]{1,0:T(1,128)}, bf16[256,1024]{1,0:T(8,128)(2,1)S(1)}) custom-call(s32[2]{0:T(128)S(1)} %add_add_fusion.place, bf16[128,1024]{1,0:T(8,128)(2,1)S(1)} %pad_maximum_fusion.refs_0_, bf16[128,1024]{1,0:T(8,128)(2,1)S(1)} %collective-permute-done.3.refs_1_, ...), custom_call_target="tpu_custom_call" | custom-call | flops 4000000000 | bytes 1024 | tf_op jit(solution)/shard_map/gram/pallas_call | solution.py:118
  42.3 1.5 %collective-permute-done.15.refs_2_ = bf16[256,512]{1,0:T(8,128)(2,1)S(1)} collective-permute-done((bf16[256,512]{1,0:T(8,128)(2,1)S(1)}, bf16[256,512]{1,0:T(8,128)(2,1)S(1)}, u32[]{:S(2)}, u32[]{:S(2)}) %collective-permute-start.15) | collective-permute-done | bytes 262176 | tf_op jit(solution)/shard_map/ppermute | solution.py:42
  43.7 1.8 %stage.1 = (bf16[2,768,512]{2,1,0:T(8,128)(2,1)S(1)}, f32[2,512,512]{2,1,0:T(8,128)S(1)}) custom-call(bf16[512,1024]{1,0:T(8,128)(2,1)S(1)} %get-tuple-element.20.high, bf16[512,1024]{1,0:T(8,128)(2,1)S(1)} %get-tuple-element.21.low, bf16[256,512]{1,0:T(8,128)(2,1)S(1)} %pad_maximum_fusion.2.refs_0_, bf16[256,512]{1,0:T(8,128)(2,1)S(1)} %collective-permute-done.14.refs_1_, ...), custom_call_target="tpu_custom_call" | custom-call | flops 20000000000 | bytes 1024 | tf_op jit(solution)/shard_map/stage/pallas_call | solution.py:275
  45.6 0.2 collective-permute-done.16.piece
  45.8 7.6 %solve.1 = (bf16[128,1024]{1,0:T(8,128)(2,1)S(1)}, bf16[2,1024,512]{2,1,0:T(8,128)(2,1)S(1)}, bf16[2,1024,512]{2,1,0:T(8,128)(2,1)S(1)}) custom-call(bf16[512,1024]{1,0:T(8,128)(2,1)S(1)} %get-tuple-element.20.high, bf16[512,1024]{1,0:T(8,128)(2,1)S(1)} %get-tuple-element.21.low, f32[1,1]{1,0:T(1,128)} %get-tuple-element.22.damping, ...), custom_call_target="tpu_custom_call" | custom-call | flops 1024 | bytes 1024 | tf_op jit(solution)/shard_map/solve/pallas_call | solution.py:326
  53.4 7.2 %collective-permute-start.17 = (bf16[128,1024]{1,0:T(8,128)(2,1)S(1)}, bf16[128,1024]{1,0:T(8,128)(2,1)S(1)}, u32[]{:S(2)}, u32[]{:S(2)}) collective-permute-start(bf16[128,1024]{1,0:T(8,128)(2,1)S(1)} %get-tuple-element.28), channel_id=1, source_target_pairs={{0,1},{1,0},{2,3},{3,2},{4,5},{5,4},{6,7},{7,6},{8,9},{9,8},{10,11... | collective-permute-start | bytes 786440 | tf_op jit(solution)/shard_map/ppermute | solution.py:55
  60.6 1.6 %keep.1._ = f32[128,2,1024]{2,1,0:T(2,128)} custom-call(bf16[256,1024]{1,0:T(8,128)(2,1)S(1)} %get-tuple-element.19.rows_t, bf16[2,1024,512]{2,1,0:T(8,128)(2,1)S(1)} %get-tuple-element.26.weights_high, bf16[2,1024,512]{2,1,0:T(8,128)(2,1)S(1)} %get-tuple-element.27.weights_low), custom_call_target="tpu_custom_call" | custom-call | flops 1000000000 | bytes 1024 | tf_op jit(solution)/shard_map/keep/pallas_call | solution.py:362
  62.1 0.0 collective-permute-done.17.refs_0_
  62.1 0.9 %place.1 = f32[128,2,1024]{2,1,0:T(2,128)} custom-call(f32[128,2,1024]{2,1,0:T(2,128)} %keep.1._, bf16[128,1024]{1,0:T(8,128)(2,1)S(1)} %collective-permute-done.17.refs_0_), custom_call_target="tpu_custom_call", output_to_operand_aliasing={{}: (0, {})} | custom-call | tf_op jit(solution)/shard_map/place/pallas_call | solution.py:393
  (6 shorter events, 0.1 us)
Async XLA Ops:
  0.0 6.0 %copy-start.1 = (bf16[128,2048]{1,0:T(8,128)(2,1)S(1)}, bf16[128,2048]{1,0:T(8,128)(2,1)}, u32[]{:S(2)}) copy-start(bf16[128,2048]{1,0:T(8,128)(2,1)} %constant.44.clone) | copy-start | bytes 1572868
  0.0 6.0 %copy-start = (bf16[16,128,1024]{2,1,0:T(8,128)(2,1)S(1)}, bf16[16,128,1024]{2,1,0:T(8,128)(2,1)}, u32[]{:S(2)}) copy-start(bf16[16,128,1024]{2,1,0:T(8,128)(2,1)} %param.3) | copy-start | bytes 12582916
  3.3 4.1 %collective-permute-start.2 = (bf16[32,1024]{1,0:T(8,128)(2,1)S(1)}, bf16[32,1024]{1,0:T(8,128)(2,1)S(1)}, u32[]{:S(2)}, u32[]{:S(2)}) collective-permute-start(bf16[32,1024]{1,0:T(8,128)(2,1)S(1)} %get-tuple-element.36), channel_id=1, source_target_pairs={{0,24},{8,16},{16,8},{24,0},{1,25},{9,17},{17,9},{25,1},{2,26},{10... | collective-permute-start | bytes 196616 | tf_op jit(solution)/shard_map/ppermute | solution.py:82
  5.5 3.7 %collective-permute-start.1 = (bf16[32,1024]{1,0:T(8,128)(2,1)S(1)}, bf16[32,1024]{1,0:T(8,128)(2,1)S(1)}, u32[]{:S(2)}, u32[]{:S(2)}) collective-permute-start(bf16[32,1024]{1,0:T(8,128)(2,1)S(1)} %get-tuple-element.37), channel_id=1, source_target_pairs={{0,16},{8,24},{16,0},{24,8},{1,17},{9,25},{17,1},{25,9},{2,18},{10... | collective-permute-start | bytes 196616 | tf_op jit(solution)/shard_map/ppermute | solution.py:82
  5.7 3.5 %collective-permute-start = (bf16[32,1024]{1,0:T(8,128)(2,1)S(1)}, bf16[32,1024]{1,0:T(8,128)(2,1)S(1)}, u32[]{:S(2)}, u32[]{:S(2)}) collective-permute-start(bf16[32,1024]{1,0:T(8,128)(2,1)S(1)} %get-tuple-element.38), channel_id=1, source_target_pairs={{0,8},{8,0},{16,24},{24,16},{1,9},{9,1},{17,25},{25,17},{2,10},{10... | collective-permute-start | bytes 196616 | tf_op jit(solution)/shard_map/ppermute | solution.py:82
  9.3 8.0 %collective-permute-start.4 = (bf16[128,1024]{1,0:T(8,128)(2,1)S(1)}, bf16[128,1024]{1,0:T(8,128)(2,1)S(1)}, u32[]{:S(2)}, u32[]{:S(2)}) collective-permute-start(bf16[128,1024]{1,0:T(8,128)(2,1)S(1)} %pad_maximum_fusion.refs_0_), channel_id=1, source_target_pairs={{0,2},{2,6},{6,4},{4,0},{1,3},{3,7},{7,5},{5,1},{8,10},{10,14},{14... | collective-permute-start | bytes 786440 | tf_op jit(solution)/shard_map/ppermute | solution.py:41
  11.6 4.1 %collective-permute-start.12 = (bf16[32,1024]{1,0:T(8,128)(2,1)S(1)}, bf16[32,1024]{1,0:T(8,128)(2,1)S(1)}, u32[]{:S(2)}, u32[]{:S(2)}) collective-permute-start(bf16[32,1024]{1,0:T(8,128)(2,1)S(1)} %get-tuple-element.32), channel_id=1, source_target_pairs={{0,24},{8,16},{16,8},{24,0},{1,25},{9,17},{17,9},{25,1},{2,26},{10... | collective-permute-start | bytes 196616 | tf_op jit(solution)/shard_map/ppermute | solution.py:82
  13.2 3.6 %collective-permute-start.11 = (bf16[32,1024]{1,0:T(8,128)(2,1)S(1)}, bf16[32,1024]{1,0:T(8,128)(2,1)S(1)}, u32[]{:S(2)}, u32[]{:S(2)}) collective-permute-start(bf16[32,1024]{1,0:T(8,128)(2,1)S(1)} %get-tuple-element.33), channel_id=1, source_target_pairs={{0,16},{8,24},{16,0},{24,8},{1,17},{9,25},{17,1},{25,9},{2,18},{10... | collective-permute-start | bytes 196616 | tf_op jit(solution)/shard_map/ppermute | solution.py:82
  13.8 3.4 %collective-permute-start.10 = (bf16[32,1024]{1,0:T(8,128)(2,1)S(1)}, bf16[32,1024]{1,0:T(8,128)(2,1)S(1)}, u32[]{:S(2)}, u32[]{:S(2)}) collective-permute-start(bf16[32,1024]{1,0:T(8,128)(2,1)S(1)} %get-tuple-element.34), channel_id=1, source_target_pairs={{0,8},{8,0},{16,24},{24,16},{1,9},{9,1},{17,25},{25,17},{2,10},{10... | collective-permute-start | bytes 196616 | tf_op jit(solution)/shard_map/ppermute | solution.py:82
  14.4 15.3 %collective-permute-start.6 = (bf16[128,1024]{1,0:T(8,128)(2,1)S(1)}, bf16[128,1024]{1,0:T(8,128)(2,1)S(1)}, u32[]{:S(2)}, u32[]{:S(2)}) collective-permute-start(bf16[128,1024]{1,0:T(8,128)(2,1)S(1)} %pad_maximum_fusion.refs_0_), channel_id=1, source_target_pairs={{2,0},{6,2},{4,6},{0,4},{3,1},{7,3},{5,7},{1,5},{10,8},{14,10},{12... | collective-permute-start | bytes 786440 | tf_op jit(solution)/shard_map/ppermute | solution.py:42
  17.3 12.6 %collective-permute-start.8 = (bf16[128,1024]{1,0:T(8,128)(2,1)S(1)}, bf16[128,1024]{1,0:T(8,128)(2,1)S(1)}, u32[]{:S(2)}, u32[]{:S(2)}) collective-permute-start(bf16[128,1024]{1,0:T(8,128)(2,1)S(1)} %collective-permute-done.4.refs_2_), channel_id=1, source_target_pairs={{0,2},{2,6},{6,4},{4,0},{1,3},{3,7},{7,5},{5,1},{8,10},{10,14},{14... | collective-permute-start | bytes 786440 | tf_op jit(solution)/shard_map/ppermute | solution.py:43
  18.7 10.4 %collective-permute-start.13 = (bf16[128,512]{1,0:T(8,128)(2,1)S(1)}, bf16[128,512]{1,0:T(8,128)(2,1)S(1)}, u32[]{:S(2)}, u32[]{:S(2)}) collective-permute-start(bf16[128,512]{1,0:T(8,128)(2,1)S(1)} %get-tuple-element.30), channel_id=1, source_target_pairs={{0,1},{1,0},{2,3},{3,2},{4,5},{5,4},{6,7},{7,6},{8,9},{9,8},{10,11... | collective-permute-start | bytes 393224 | tf_op jit(solution)/shard_map/ppermute | solution.py:55
  28.2 5.7 %collective-permute-start.3 = (bf16[128,1024]{1,0:T(8,128)(2,1)S(1)}, bf16[128,1024]{1,0:T(8,128)(2,1)S(1)}, u32[]{:S(2)}, u32[]{:S(2)}) collective-permute-start(bf16[128,1024]{1,0:T(8,128)(2,1)S(1)} %pad_maximum_fusion.refs_0_), channel_id=1, source_target_pairs={{0,1},{1,0},{2,3},{3,2},{4,5},{5,4},{6,7},{7,6},{8,9},{9,8},{10,11... | collective-permute-start | bytes 786440 | tf_op jit(solution)/shard_map/ppermute | solution.py:55
  29.2 7.6 %collective-permute-start.14 = (bf16[256,512]{1,0:T(8,128)(2,1)S(1)}, bf16[256,512]{1,0:T(8,128)(2,1)S(1)}, u32[]{:S(2)}, u32[]{:S(2)}) collective-permute-start(bf16[256,512]{1,0:T(8,128)(2,1)S(1)} %pad_maximum_fusion.2.refs_0_), channel_id=1, source_target_pairs={{0,2},{2,6},{6,4},{4,0},{1,3},{3,7},{7,5},{5,1},{8,10},{10,14},{14... | collective-permute-start | bytes 786440 | tf_op jit(solution)/shard_map/ppermute | solution.py:41
  29.3 9.2 %collective-permute-start.5 = (bf16[128,1024]{1,0:T(8,128)(2,1)S(1)}, bf16[128,1024]{1,0:T(8,128)(2,1)S(1)}, u32[]{:S(2)}, u32[]{:S(2)}) collective-permute-start(bf16[128,1024]{1,0:T(8,128)(2,1)S(1)} %collective-permute-done.4.refs_2_), channel_id=1, source_target_pairs={{0,1},{1,0},{2,3},{3,2},{4,5},{5,4},{6,7},{7,6},{8,9},{9,8},{10,11... | collective-permute-start | bytes 786440 | tf_op jit(solution)/shard_map/ppermute | solution.py:55
  29.7 8.8 %collective-permute-start.7 = (bf16[128,1024]{1,0:T(8,128)(2,1)S(1)}, bf16[128,1024]{1,0:T(8,128)(2,1)S(1)}, u32[]{:S(2)}, u32[]{:S(2)}) collective-permute-start(bf16[128,1024]{1,0:T(8,128)(2,1)S(1)} %collective-permute-done.6.refs_4_), channel_id=1, source_target_pairs={{0,1},{1,0},{2,3},{3,2},{4,5},{5,4},{6,7},{7,6},{8,9},{9,8},{10,11... | collective-permute-start | bytes 786440 | tf_op jit(solution)/shard_map/ppermute | solution.py:55
  29.8 8.6 %collective-permute-start.9 = (bf16[128,1024]{1,0:T(8,128)(2,1)S(1)}, bf16[128,1024]{1,0:T(8,128)(2,1)S(1)}, u32[]{:S(2)}, u32[]{:S(2)}) collective-permute-start(bf16[128,1024]{1,0:T(8,128)(2,1)S(1)} %collective-permute-done.8.refs_6_), channel_id=1, source_target_pairs={{0,1},{1,0},{2,3},{3,2},{4,5},{5,4},{6,7},{7,6},{8,9},{9,8},{10,11... | collective-permute-start | bytes 786440 | tf_op jit(solution)/shard_map/ppermute | solution.py:55
  33.9 9.8 %collective-permute-start.15 = (bf16[256,512]{1,0:T(8,128)(2,1)S(1)}, bf16[256,512]{1,0:T(8,128)(2,1)S(1)}, u32[]{:S(2)}, u32[]{:S(2)}) collective-permute-start(bf16[256,512]{1,0:T(8,128)(2,1)S(1)} %pad_maximum_fusion.2.refs_0_), channel_id=1, source_target_pairs={{2,0},{6,2},{4,6},{0,4},{3,1},{7,3},{5,7},{1,5},{10,8},{14,10},{12... | collective-permute-start | bytes 786440 | tf_op jit(solution)/shard_map/ppermute | solution.py:42
  36.8 9.0 %collective-permute-start.16 = (bf16[256,512]{1,0:T(8,128)(2,1)S(1)}, bf16[256,512]{1,0:T(8,128)(2,1)S(1)}, u32[]{:S(2)}, u32[]{:S(2)}) collective-permute-start(bf16[256,512]{1,0:T(8,128)(2,1)S(1)} %collective-permute-done.14.refs_1_), channel_id=1, source_target_pairs={{0,2},{2,6},{6,4},{4,0},{1,3},{3,7},{7,5},{5,1},{8,10},{10,14},{14... | collective-permute-start | bytes 786440 | tf_op jit(solution)/shard_map/ppermute | solution.py:43
  53.4 8.7 %collective-permute-start.17 = (bf16[128,1024]{1,0:T(8,128)(2,1)S(1)}, bf16[128,1024]{1,0:T(8,128)(2,1)S(1)}, u32[]{:S(2)}, u32[]{:S(2)}) collective-permute-start(bf16[128,1024]{1,0:T(8,128)(2,1)S(1)} %get-tuple-element.28), channel_id=1, source_target_pairs={{0,1},{1,0},{2,3},{3,2},{4,5},{5,4},{6,7},{7,6},{8,9},{9,8},{10,11... | collective-permute-start | bytes 786440 | tf_op jit(solution)/shard_map/ppermute | solution.py:55
